TPU v7x, 128 devices: a whole 4x4x4 slice. The times are simulated.
128 devices in a mesh: dp: 16 (over x, y), mp: 8 (over z, core).
Axes of the slice: x: 4, y: 4, z: 4, core: 2. Of those that a mesh axis runs over, the one named last changes fastest.
Arguments:
- grad_parts: bfloat16 [16, 3, 4096, 4096], P('dp', None, 'mp')
- moment: float32 [3, 4096, 4096], P(None, ('mp', 'dp'))
- left_roots: bfloat16 [128, 1024, 1024], P(('dp', 'mp'))
- right_roots: bfloat16 [128, 1024, 1024], P(('dp', 'mp'))
- block_owner: int32 [48], replicated, may hold values from 0 to 127, as said below
Outputs:
- update: bfloat16 [128, 1024, 1024], P(('dp', 'mp'))
Inputs may be any that keep to these rules, and one draw needn't show every extreme that they name: `block_owner`: each device owns at most 1 block and some device owns exactly 1; a block's factors sit in its owner's slots in the order of block numbers; slots without a block hold factors that are not used.
All inputs are finite; a program needn't handle non-finite values.
Results may differ from a plain program's by a relative error of at most 0.02.
Values may be sent and summed in bfloat16 or wider, within the bound.
No kernel may reach another device: no remote copies, remote signals or barrier semaphores. Data moves between devices by JAX's collectives and lax.ppermute only.
A program may use at most 128 MiB of HBM per device.

v0:
```python
import jax
import jax.numpy as jnp
from jax import lax
from jax.sharding import PartitionSpec as P

BETA_TWO = 0.999
ADAM_EPS = 1e-08
NORM_EPS = 1e-06


def slot_tables(block_owner, capacity, slot_count):
    block_total = block_owner.shape[0]
    numbers = jnp.arange(block_total, dtype=jnp.int32)
    earlier = (block_owner[:, None] == block_owner[None, :]) & (numbers[None, :] < numbers[:, None])
    ranking = jnp.sum(earlier.astype(jnp.int32), axis=1)
    slot_key = block_owner * capacity + ranking
    queries = jnp.arange(slot_count, dtype=jnp.int32)
    matches = (queries[:, None] == slot_key[None, :]).astype(jnp.int32)
    present = jnp.sum(matches, axis=1)
    block_of = jnp.sum(matches * numbers[None, :], axis=1)
    return (slot_key, block_of, present)


def shards(grad_parts, moment, left_roots, right_roots, block_owner):
    dp_count = lax.axis_size("dp")
    mp_count = lax.axis_size("mp")
    device_count = dp_count * mp_count
    matrix_count = grad_parts.shape[1]
    feature_width = grad_parts.shape[3]
    capacity = left_roots.shape[0]
    block_size = left_roots.shape[1]
    block_rows = feature_width // block_size
    block_total = block_owner.shape[0]
    slot_count = capacity * device_count
    per_block = block_size * mp_count // feature_width
    summed = lax.psum_scatter(
        grad_parts.astype(jnp.float32).astype(jnp.bfloat16), "dp", scatter_dimension=2, tiled=True
    ).astype(jnp.float32)
    gradient = summed[0]
    row_count = gradient.shape[1]
    second = BETA_TWO * moment + (1.0 - BETA_TWO) * gradient * gradient
    adam_dir = gradient / (jnp.sqrt(second) + ADAM_EPS)
    partial_sq = jnp.sum(
        (adam_dir * adam_dir).reshape(matrix_count, row_count, block_rows, block_size), axis=(1, 3)
    )
    slot_key, block_of, present = slot_tables(block_owner, capacity, slot_count)
    mp_index = lax.axis_index("mp")
    device_index = lax.axis_index("dp") * mp_count + mp_index
    my_row = mp_index // per_block
    pieces = gradient.astype(jnp.bfloat16).reshape(matrix_count, row_count, block_rows, block_size)
    pieces = pieces.transpose(0, 2, 1, 3).reshape(matrix_count * block_rows, row_count, block_size)
    target_row = block_of // block_rows % block_rows
    pick_index = block_of // (block_rows * block_rows) * block_rows + block_of % block_rows
    usable = (present > 0) & (target_row == my_row)
    outgoing = jnp.where(
        usable[:, None, None], jnp.take(pieces, pick_index, axis=0), jnp.zeros((), jnp.bfloat16)
    )
    own_slots = device_index * capacity + jnp.arange(capacity, dtype=jnp.int32)
    own_block = jnp.take(block_of, own_slots)
    own_present = jnp.take(present, own_slots) > 0
    own_row = own_block // block_rows % block_rows
    chosen = (jnp.arange(block_rows, dtype=jnp.int32) == my_row).astype(jnp.float32)
    spread = (partial_sq[:, None, :] * chosen[None, :, None]).reshape(block_total)
    totals = lax.psum(spread, ("dp", "mp"))
    lookup = (jnp.arange(block_total, dtype=jnp.int32)[None, :] == own_block[:, None]).astype(
        jnp.float32
    )
    adam_power = jnp.sum(lookup * totals[None, :], axis=1)
    received = lax.all_to_all(
        outgoing.reshape(device_count, capacity, row_count, block_size),
        ("dp", "mp"),
        split_axis=0,
        concat_axis=0,
        tiled=True,
    )
    received = received.reshape(dp_count, mp_count, capacity, row_count, block_size)
    column_set = lax.dynamic_slice_in_dim(received[:, :, 0], own_row[0] * per_block, per_block, 1)
    grad_block = column_set.transpose(1, 0, 2, 3).reshape(block_size, block_size)
    first_step = jnp.dot(left_roots[0], grad_block, preferred_element_type=jnp.float32).astype(
        jnp.bfloat16
    )
    shaped = jnp.dot(first_step, right_roots[0], preferred_element_type=jnp.float32)
    block_power = jnp.sum(shaped * shaped)
    grafted = shaped * (jnp.sqrt(adam_power[0]) * lax.rsqrt(block_power + NORM_EPS))
    results = [jnp.where(own_present[0], grafted, 0.0).astype(jnp.bfloat16)]
    return jnp.stack(results)


def solution(mesh):
    placed = (
        P("dp", None, "mp", None),
        P(None, ("mp", "dp"), None),
        P(("dp", "mp"), None, None),
        P(("dp", "mp"), None, None),
        P(),
    )
    return jax.shard_map(
        shards, mesh=mesh, in_specs=placed, out_specs=P(("dp", "mp"), None, None), check_vma=False
    )
```

profile of v0, /device:TPU:1, one launch (start us, length us, event | category | flops | bytes accessed | tf_op | source)
XLA Modules:
  0.0 317.0 jit_solution(940505643673267427)
XLA Ops:
  6.5 0.0 copy-start
  6.5 0.0 copy-start.2
  6.5 0.0 reduce-scatter.2.cloned.1.call-start
  6.5 0.7 reduce-scatter.2.cloned.1.call-update
  7.3 0.1 copy-done.2
  7.3 0.2 convert_reduce_fusion.1
  7.5 0.1 convert_reduce_fusion
  7.7 100.5 %reduce-scatter.2.cloned.1.call-done = bf16[1,3,32,4096]{3,2,1,0:T(8,128)(2,1)} async-done(((bf16[1,3,512,4096]{3,2,1,0:T(8,128)(2,1)}), bf16[1,3,32,4096]{3,2,1,0:T(8,128)(2,1)}) %reduce-scatter.2.cloned.1.call-update) | async-done | bytes 786448 | tf_op jit(solution)/shard_map/reduce_scatter | solution.py:36
  108.1 1.3 fusion.22
  109.4 0.1 pad_maximum_fusion
  109.5 6.4 %gather_fusion = bf16[128,32,1024]{2,1,0:T(8,128)(2,1)} fusion(bf16[12,32,1024]{2,1,0:T(8,128)(2,1)S(1)} %bitcast.48, s32[1024]{0:T(1024)S(1)} %pad_clamp_fusion), kind=kCustom, calls=%fused_computation | custom fusion | bytes 16777728 | tf_op jit(solution)/shard_map/jit(_take)/gather | solution.py:56
  115.9 7.5 %fusion = bf16[128,1,32,1024]{3,2,1,0:T(8,128)(2,1)} fusion(bf16[128,32,1024]{2,1,0:T(8,128)(2,1)} %gather_fusion, pred[128]{0:T(512)(128)(4,1)S(1)} %get-tuple-element.34, pred[128]{0:T(512)(128)(4,1)S(1)} %get-tuple-element.33), kind=kLoop, calls=%fused_computation.2 | loop fusion | flops 8388608 | bytes 16777472 | tf_op jit(solution)/shard_map/jit(_where)/select_n | solution.py:55
  123.4 0.0 copy-start.1
  123.5 8.1 %all-to-all-start = ((bf16[128,1,32,1024]{3,2,1,0:T(8,128)(2,1)}), bf16[128,1,32,1024]{3,2,1,0:T(8,128)(2,1)}, u32[]{:S(2)}, u32[]{:S(2)}) async-start(bf16[128,1,32,1024]{3,2,1,0:T(8,128)(2,1)} %fusion), calls=%async_computation.1 | async-start | bytes 16777216 | tf_op jit(solution)/shard_map/all_to_all | solution.py:69
  131.6 0.7 dynamic-slice.5
  132.9 0.6 dynamic-slice.4
  134.0 0.0 copy-done.1
  134.0 2.4 fusion.11
  136.4 0.1 reduce_sum.68
  136.5 0.1 reduce_sum.69
  136.6 0.1 broadcast_multiply_fusion
  136.6 0.1 mul.98
  136.7 154.6 %psum.7 = f32[48]{0:T(128)S(1)} all-reduce(f32[48]{0:T(128)S(1)} %mul.98), channel_id=1, replica_groups=mesh['dp'=16,'mp'=8] {'dp','mp'}, use_global_device_ids=true, to_apply=%region_6.7 | all-reduce | flops 48 | bytes 384 | tf_op jit(solution)/shard_map/psum | solution.py:64
  291.4 0.6 fusion.19
  292.6 0.0 all-to-all-done
  292.7 1.8 dynamic-slice_bitcast_fusion
  294.4 1.5 copy.8
  295.9 0.0 copy-done
  295.9 9.4 %multiply_reduce_fusion = (f32[]{:T(128)}, f32[1024,1024]{1,0:T(8,128)}) fusion(bf16[1,1024,1024]{2,1,0:T(8,128)(2,1)S(1)} %copy-done, bf16[1024,1024]{1,0:T(8,128)(2,1)} %bitcast.50, bf16[1,1024,1024]{2,1,0:T(8,128)(2,1)} %param.7), kind=kOutput, calls=%fused_computation.4 | convolution fusion | flops 4298113024 | bytes 10485764 | tf_op jit(solution)/shard_map/dot_general | solution.py:82
  306.0 4.1 %fusion.1 = bf16[1,1024,1024]{2,1,0:T(8,128)(2,1)} fusion(f32[1024,1024]{1,0:T(8,128)} %get-tuple-element.36, f32[]{:T(128)S(6)} %mul.101, pred[]{:T(512)} %bitcast.2), kind=kLoop, calls=%fused_computation.6 | loop fusion | flops 3145728 | bytes 6291461 | tf_op jit(solution)/shard_map/stack | solution.py:86
  (5 shorter events, 0.1 us)
Async XLA Ops:
  6.5 289.4 %copy-start = (bf16[1,1024,1024]{2,1,0:T(8,128)(2,1)S(1)}, bf16[1,1024,1024]{2,1,0:T(8,128)(2,1)}, u32[]{:S(2)}) copy-start(bf16[1,1024,1024]{2,1,0:T(8,128)(2,1)} %param.8) | copy-start | bytes 6291460
  6.5 0.8 copy-start.2
  6.5 101.6 %reduce-scatter.2.cloned.1.call-start = ((), (), s32[]{:S(2)}) async-start(), calls=%async_computation.2 | async-start | bytes 13369344 | tf_op jit(solution)/shard_map/reduce_scatter | solution.py:36
  123.4 10.6 %copy-start.1 = (bf16[1,3,32,4096]{3,2,1,0:T(8,128)(2,1)S(1)}, bf16[1,3,32,4096]{3,2,1,0:T(8,128)(2,1)}, u32[]{:S(2)}) copy-start(bf16[1,3,32,4096]{3,2,1,0:T(8,128)(2,1)} %reduce-scatter.2.cloned.1.call-done) | copy-start | bytes 2359300
  123.5 169.2 %all-to-all-start = ((bf16[128,1,32,1024]{3,2,1,0:T(8,128)(2,1)}), bf16[128,1,32,1024]{3,2,1,0:T(8,128)(2,1)}, u32[]{:S(2)}, u32[]{:S(2)}) async-start(bf16[128,1,32,1024]{3,2,1,0:T(8,128)(2,1)} %fusion), calls=%async_computation.1 | async-start | bytes 16777216 | tf_op jit(solution)/shard_map/all_to_all | solution.py:69
Sparse Core Ops, SparseCore 0:
  10.8 97.2 reduce-scatter.1
where the time goes:
time: 317 us
  blocking collectives  155 us (49%)
  waiting for transfers between devices  101 us (32%)
  between operations  16.1 us (5%)
  other arithmetic  15.2 us (5%)
  local copies, waits for them, and re-layouts  12.4 us (4%)
  matrix products  9.44 us (3%)
  starting transfers between devices  8.1 us (3%)
    psum x1, blocking collectives, shards(): totals = lax.psum(spread, ('dp', 'mp'))  155 us
    reduce_scatter x1, waiting for transfers between devices, shards(): lax.psum_scatter(grad_parts.astype(jnp.float32).astype(jnp.bfloat16), 'dp...  100 us
    dot_general x1, matrix products, shards(): jnp.dot(first_step, right_roots[0], preferred_element_type=jnp.float32)  9.44 us
    all_to_all x1, starting transfers between devices, shards(): lax.all_to_all(outgoing.reshape(device_count, capacity, row_count, block_...  8.1 us
    select_n x1, other arithmetic, shards(): jnp.where(usable[:, None, None], jnp.take(pieces, pick_index, axis=0), jn...  7.55 us
    gather x1, local copies, waits for them, and re-layouts, shards(): jnp.take(pieces, pick_index, axis=0)  6.42 us
  transfers between devices with their start and end apart: 2, of which 1 were waited for; matrix products, arithmetic and copies ran while one was open for 2% of the time, Pallas kernels for 0%

commit v1 on v0

v1 whole, which is shorter than its diff:
```python
import jax
import jax.numpy as jnp
from jax import lax
from jax.sharding import PartitionSpec as P

BETA_TWO = 0.999
ADAM_EPS = 1e-08
NORM_EPS = 1e-06
SIDE = 4
CHUNKS = 2
LANES = 128


def device_number(x, y, z, core):
    return ((x * SIDE + y) * SIDE + z) * 2 + core


def shifted(axis, sign):
    pairs = []
    for x in range(SIDE):
        for y in range(SIDE):
            for z in range(SIDE):
                for core in range(2):
                    place = [x, y]
                    place[axis] = (place[axis] + (sign if core else -sign)) % SIDE
                    pairs.append((device_number(x, y, z, core), device_number(*place, z, core)))
    return pairs


def send(value, axis, sign):
    return lax.ppermute(value, ("dp", "mp"), shifted(axis, sign))


def reduce_axis(piece, position, step, axis):
    wide = lambda value: value.astype(jnp.float32)
    far = send(piece((position + 2) % SIDE), axis, 1)
    near = send(piece((position - step) % SIDE), axis, -1)
    joined = (wide(piece((position + step) % SIDE)) + wide(far)).astype(jnp.bfloat16)
    joined = send(joined, axis, 1)
    return wide(piece(position)) + wide(near) + wide(joined)


def slot_blocks(block_owner, slot_count):
    numbers = jnp.arange(block_owner.shape[0], dtype=jnp.int32)
    queries = jnp.arange(slot_count, dtype=jnp.int32)
    matches = (queries[:, None] == block_owner[None, :]).astype(jnp.int32)
    return jnp.sum(matches * numbers[None, :], axis=1), jnp.sum(matches, axis=1)


def shards(grad_parts, moment, left_roots, right_roots, block_owner):
    dp_count = lax.axis_size("dp")
    mp_count = lax.axis_size("mp")
    dp_index = lax.axis_index("dp")
    mp_index = lax.axis_index("mp")
    matrices = grad_parts.shape[1]
    width = grad_parts.shape[3]
    block = left_roots.shape[1]
    sides = width // block
    x, y = dp_index // SIDE, dp_index % SIDE
    step = 2 * (mp_index % 2) - 1
    rows = moment.shape[1] // CHUNKS
    half = width // 2
    parts = grad_parts[0].reshape(matrices, SIDE, SIDE, CHUNKS, rows, width)

    block_of, present = slot_blocks(block_owner, dp_count * mp_count)
    mine = block_of.reshape(dp_count, mp_count)[:, mp_index]
    source = 2 * (mine // sides % sides)
    column = mine // (sides * sides) * sides + mine % sides
    picks = ((source[:, None] + jnp.arange(2)[None, :]) * (matrices * sides) + column[:, None]).reshape(-1)
    own_present = present[dp_index * mp_count + mp_index] > 0

    received = []
    for chunk in range(CHUNKS):
        sums = []
        for first in (0, 1):
            here = (x, y)[first]
            there = (x, y)[1 - first]
            cut = parts[:, :, :, chunk, :, first * half : (first + 1) * half]

            def piece(j, cut=cut, first=first):
                return lax.dynamic_index_in_dim(cut, j, 1 + first, keepdims=False)

            partial = reduce_axis(piece, here, step, first).astype(jnp.bfloat16)

            def inner(j, partial=partial):
                return lax.dynamic_index_in_dim(partial, j, 1, keepdims=False)

            sums.append(reduce_axis(inner, there, step, 1 - first))
        pieces = []
        for matrix in range(matrices):
            for side in range(sides):
                first, offset = divmod(side * block, half)
                gradient = sums[first][matrix, :, offset : offset + block]
                known = moment[matrix, chunk * rows : (chunk + 1) * rows, side * block : (side + 1) * block]
                second = BETA_TWO * known + (1.0 - BETA_TWO) * gradient * gradient
                direction = gradient / (jnp.sqrt(second) + ADAM_EPS)
                square = direction * direction
                power = sum(square[:, k : k + LANES] for k in range(0, block, LANES))
                pieces.append(jnp.concatenate([gradient, power], axis=1).astype(jnp.bfloat16))
        gathered = lax.all_gather(jnp.stack(pieces), "mp", axis=0, tiled=True)
        outgoing = jnp.take(gathered, picks, axis=0, mode="clip")
        outgoing = outgoing.reshape(dp_count, 2, rows, block + LANES)
        received.append(lax.all_to_all(outgoing, "dp", 0, 0, tiled=True))
    together = jnp.stack(received, axis=2)
    adam_power = jnp.sum(together[..., block:].astype(jnp.float32))
    grad_block = together[..., :block].transpose(1, 0, 2, 3, 4).reshape(block, block)
    first_step = jnp.dot(left_roots[0], grad_block, preferred_element_type=jnp.float32).astype(jnp.bfloat16)
    shaped = jnp.dot(first_step, right_roots[0], preferred_element_type=jnp.float32)
    block_power = jnp.sum(shaped * shaped)
    grafted = shaped * (jnp.sqrt(adam_power) * lax.rsqrt(block_power + NORM_EPS))
    return jnp.where(own_present, grafted, 0.0).astype(jnp.bfloat16)[None]


def solution(mesh):
    placed = (
        P("dp", None, "mp", None),
        P(None, ("mp", "dp"), None),
        P(("dp", "mp"), None, None),
        P(("dp", "mp"), None, None),
        P(),
    )
    return jax.shard_map(
        shards, mesh=mesh, in_specs=placed, out_specs=P(("dp", "mp"), None, None), check_vma=False
    )
```

time: 317 us -> 234 us (0.74)
  blocking collectives: 155 us -> 0 us
  starting transfers between devices: 8.1 us -> 45.2 us
  local copies, waits for them, and re-layouts: 12.4 us -> 36.1 us
  other arithmetic: 15.2 us -> 21.1 us
    psum x1 -> x0, blocking collectives: 155 us -> none  [shards(): totals = lax.psum(spread, ('dp', 'mp'))]
    reduce_scatter x1 -> x0, waiting for transfers between devices: 100 us -> none  [shards(): lax.psum_scatter(grad_parts.astype(jnp.float32).astype(jnp.bfloat16), 'dp...]
    all_gather x0 -> x2, waiting for transfers between devices: none -> 46.9 us  [shards(): gathered = lax.all_gather(jnp.stack(pieces), 'mp', axis=0, tiled=True)]
    ppermute x0 -> x24, waiting for transfers between devices: none -> 42.2 us  [send(): return lax.ppermute(value, ('dp', 'mp'), shifted(axis, sign))]
    ppermute x0 -> x24, starting transfers between devices: none -> 32.1 us  [send(): return lax.ppermute(value, ('dp', 'mp'), shifted(axis, sign))]
    all_to_all x1 -> x2, waiting for transfers between devices: 0.01 us -> 14.7 us  [shards(): received.append(lax.all_to_all(outgoing, 'dp', 0, 0, tiled=True))]
    convert_element_type x1 -> x12, other arithmetic: 0.01 us -> 8.74 us  [the longest x8 4.92 us: reduce_axis(): (wide(piece((position + step) % SIDE)) + wide(far)).astype(jnp.bfloat16)]
    dynamic_slice x0 -> x3, local copies, waits for them, and re-layouts: none -> 7.91 us  [the longest x2 7.32 us: piece(): return lax.dynamic_index_in_dim(cut, j, 1 + first, keepdims=False)]
  transfers between devices with their start and end apart: 2 -> 28, of which waited for: 1 -> 13; matrix products, arithmetic and copies ran while one was open for 2% -> 14% of each run, Pallas kernels for 0% -> 0%
where the time goes in v1:
time: 234 us; the launch traced here: 232 us
  waiting for transfers between devices  104 us (44%)
  starting transfers between devices  45.2 us (19%)
  local copies, waits for them, and re-layouts  36.1 us (15%)
  other arithmetic  21.1 us (9%)
  between operations  16.1 us (7%)
  matrix products  9.55 us (4%)
    all_gather x2, waiting for transfers between devices, shards(): gathered = lax.all_gather(jnp.stack(pieces), 'mp', axis=0, tiled=True)  46.9 us
    ppermute x24, waiting for transfers between devices, send(): return lax.ppermute(value, ('dp', 'mp'), shifted(axis, sign))  42.2 us
    ppermute x24, starting transfers between devices, send(): return lax.ppermute(value, ('dp', 'mp'), shifted(axis, sign))  32.1 us
    all_to_all x2, waiting for transfers between devices, shards(): received.append(lax.all_to_all(outgoing, 'dp', 0, 0, tiled=True))  14.7 us
    all_to_all x2, starting transfers between devices, shards(): received.append(lax.all_to_all(outgoing, 'dp', 0, 0, tiled=True))  13.1 us
    dot_general x1, matrix products, shards(): jnp.dot(first_step, right_roots[0], preferred_element_type=jnp.float32)  9.55 us
    slice x1, local copies, waits for them, and re-layouts, shards(): cut = parts[:, :, :, chunk, :, first * half:(first + 1) * half]  8.61 us
    gather x2, local copies, waits for them, and re-layouts, shards(): outgoing = jnp.take(gathered, picks, axis=0, mode='clip')  7.47 us
  transfers between devices with their start and end apart: 28, of which 13 were waited for; matrix products, arithmetic and copies ran while one was open for 14% of the time, Pallas kernels for 0%

profile of v1, /device:TPU:1, one launch (start us, length us, event | category | flops | bytes accessed | tf_op | source)
XLA Modules:
  0.0 231.8 jit_solution(8553866212509524420)
XLA Ops:
  6.5 8.6 %fusion.210 = (bf16[3,4,4,1,16,2048]{5,4,3,2,1,0:T(8,128)(2,1)}, bf16[3,4,4,1,16,2048]{5,4,3,2,1,0:T(8,128)(2,1)}, bf16[3,4,4,1,16,2048]{5,4,3,2,1,0:T(8,128)(2,1)}, bf16[3,4,4,1,16,2048]{5,4,3,2,1,0:T(8,128)(2,1)}) fusion(bf16[3,4,4,2,16,4096]{5,4,3,2,1,0:T(8,128)(2,1)} %bitcast.276), kind=kLoop, calls=%fused_computation.524 | loop fusion | bytes 25165824 | tf_op jit(solution)/shard_map/slice | solution.py:78
  15.2 5.3 %constant_dynamic-slice_fusion.3 = (bf16[3,1,4,1,16,2048]{5,4,3,2,1,0:T(8,128)(2,1)}, bf16[3,1,4,1,16,2048]{5,4,3,2,1,0:T(8,128)(2,1)}, bf16[3,1,4,1,16,2048]{5,...) fusion(bf16[3,4,4,1,16,2048]{5,4,3,2,1,0:T(8,128)(2,1)} %get-tu, ...), kind=kLoop, calls=%fused_computation.284 | loop fusion | bytes 12582928 | tf_op jit(solution)/shard_map/jit(dynamic_index_in_dim)/dynamic_slice | solution.py:81
  21.4 2.0 collective-permute-start.13
  23.5 2.8 %dynamic-slice_bitcast_fusion.1 = (bf16[3,4,16,2048]{3,2,1,0:T(8,128)(2,1)}, bf16[3,4,16,2048]{3,2,1,0:T(8,128)(2,1)}) fusion(bf16[3,4,4,1,16,2048]{5,4,3,2,1,0:T(8,128)(2,1)} %get-tuple-element.9, s32[]{:T(128)S(6)} %select_n.176, s32[]{:T(128)S(6)} %select_n.180), kind=kLoop, calls=%fused_computation.48 | loop fusion | bytes 3145736 | tf_op jit(solution)/shard_map/jit(dynamic_index_in_dim)/squeeze | solution.py:81
  31.5 2.1 constant_dynamic-slice_fusion.8
  34.9 2.8 %collective-permute-start.6 = (bf16[3,4,16,2048]{3,2,0,1:T(8,128)(2,1)S(1)}, bf16[3,4,16,2048]{3,2,0,1:T(8,128)(2,1)S(1)}, u32[]{:S(2)}, u32[]{:S(2)}) collective-permute-start(bf16[3,4,16,2048]{3,2,0,1:T(8,128)(2,1)S(1)} %bitcast.283), channel_id=1, source_target_pairs={{0,8},{1,25},{2,10},{3,27},{4,12},{5,29},{6,14},{7,31},{8,16},{9,1... | collective-permute-start | bytes 2359304 | tf_op jit(solution)/shard_map/ppermute | solution.py:31
  39.1 2.6 %collective-permute-done.19 = bf16[3,4,16,2048]{3,2,1,0:T(8,128)(2,1)} collective-permute-done((bf16[3,4,16,2048]{3,2,1,0:T(8,128)(2,1)}, bf16[3,4,16,2048]{3,2,1,0:T(8,128)(2,1)}, u32[]{:S(2)}, u32[]{:S(2)}) %collective-permute-start.19) | collective-permute-done | bytes 786464 | tf_op jit(solution)/shard_map/ppermute | solution.py:31
  41.7 3.4 %collective-permute-start.1 = (bf16[3,4,16,2048]{3,2,0,1:T(8,128)(2,1)S(1)}, bf16[3,4,16,2048]{3,2,0,1:T(8,128)(2,1)S(1)}, u32[]{:S(2)}, u32[]{:S(2)}) collective-permute-start(bf16[3,4,16,2048]{3,2,0,1:T(8,128)(2,1)S(1)} %bitcast.284), channel_id=1, source_target_pairs={{0,96},{1,33},{2,98},{3,35},{4,100},{5,37},{6,102},{7,39},{8,104},... | collective-permute-start | bytes 2359304 | tf_op jit(solution)/shard_map/ppermute | solution.py:31
  46.5 11.9 %collective-permute-done.7 = bf16[3,4,16,2048]{3,2,0,1:T(8,128)(2,1)S(1)} collective-permute-done((bf16[3,4,16,2048]{3,2,0,1:T(8,128)(2,1)S(1)}, bf16[3,4,16,2048]{3,2,0,1:T(8,128)(2,1)S(1)}, u32[]{:S(2)}, u32[]{:S(2)}) %collective-permute-start.7) | collective-permute-done | bytes 786464 | tf_op jit(solution)/shard_map/ppermute | solution.py:31
  58.4 1.6 collective-permute-start.20
  60.4 3.6 %collective-permute-start.14 = (bf16[3,4,16,2048]{3,2,0,1:T(8,128)(2,1)S(1)}, bf16[3,4,16,2048]{3,2,0,1:T(8,128)(2,1)S(1)}, u32[]{:S(2)}, u32[]{:S(2)}) collective-permute-start(bf16[3,4,16,2048]{3,2,0,1:T(8,128)(2,1)S(1)} %fusion.10), channel_id=1, source_target_pairs={{0,96},{1,33},{2,98},{3,35},{4,100},{5,37},{6,102},{7,39},{8,104},... | collective-permute-start | bytes 2359304 | tf_op jit(solution)/shard_map/ppermute | solution.py:31
  64.3 7.9 %collective-permute-done.20 = bf16[3,4,16,2048]{3,2,1,0:T(8,128)(2,1)S(1)} collective-permute-done((bf16[3,4,16,2048]{3,2,1,0:T(8,128)(2,1)S(1)}, bf16[3,4,16,2048]{3,2,1,0:T(8,128)(2,1)S(1)}, u32[]{:S(2)}, u32[]{:S(2)}) %collective-permute-start.20) | collective-permute-done | bytes 786464 | tf_op jit(solution)/shard_map/ppermute | solution.py:31
  74.2 2.4 %collective-permute-start.2 = (bf16[3,4,16,2048]{3,2,0,1:T(8,128)(2,1)S(1)}, bf16[3,4,16,2048]{3,2,0,1:T(8,128)(2,1)S(1)}, u32[]{:S(2)}, u32[]{:S(2)}) collective-permute-start(bf16[3,4,16,2048]{3,2,0,1:T(8,128)(2,1)S(1)} %fusion.16), channel_id=1, source_target_pairs={{0,96},{1,33},{2,98},{3,35},{4,100},{5,37},{6,102},{7,39},{8,104},... | collective-permute-start | bytes 2359304 | tf_op jit(solution)/shard_map/ppermute | solution.py:31
  78.8 2.2 collective-permute-start.21
  81.0 3.7 %collective-permute-done.8 = bf16[3,4,16,2048]{3,2,0,1:T(8,128)(2,1)S(1)} collective-permute-done((bf16[3,4,16,2048]{3,2,0,1:T(8,128)(2,1)S(1)}, bf16[3,4,16,2048]{3,2,0,1:T(8,128)(2,1)S(1)}, u32[]{:S(2)}, u32[]{:S(2)}) %collective-permute-start.8) | collective-permute-done | bytes 786464 | tf_op jit(solution)/shard_map/ppermute | solution.py:31
  85.8 2.7 %collective-permute-start.15 = (bf16[3,16,2048]{2,1,0:T(8,128)(2,1)S(1)}, bf16[3,16,2048]{2,1,0:T(8,128)(2,1)S(1)}, u32[]{:S(2)}, u32[]{:S(2)}) collective-permute-start(bf16[3,16,2048]{2,1,0:T(8,128)(2,1)S(1)} %get-tuple-element.53), channel_id=1, source_target_pairs={{0,8},{1,25},{2,10},{3,27},{4,12},{5,29},{6,14},{7,31},{8,16},{9,1... | collective-permute-start | bytes 589832 | tf_op jit(solution)/shard_map/ppermute | solution.py:31
  88.4 2.5 %collective-permute-done.2 = bf16[3,4,16,2048]{3,2,0,1:T(8,128)(2,1)S(1)} collective-permute-done((bf16[3,4,16,2048]{3,2,0,1:T(8,128)(2,1)S(1)}, bf16[3,4,16,2048]{3,2,0,1:T(8,128)(2,1)S(1)}, u32[]{:S(2)}, u32[]{:S(2)}) %collective-permute-start.2) | collective-permute-done | bytes 786464 | tf_op jit(solution)/shard_map/ppermute | solution.py:31
  95.1 3.1 %collective-permute-start.4 = (bf16[3,16,2048]{2,1,0:T(8,128)(2,1)S(1)}, bf16[3,16,2048]{2,1,0:T(8,128)(2,1)S(1)}, u32[]{:S(2)}, u32[]{:S(2)}) collective-permute-start(bf16[3,16,2048]{2,1,0:T(8,128)(2,1)S(1)} %get-tuple-element.58), channel_id=1, source_target_pairs={{0,24},{1,9},{2,26},{3,11},{4,28},{5,13},{6,30},{7,15},{8,0},{9,17... | collective-permute-start | bytes 589832 | tf_op jit(solution)/shard_map/ppermute | solution.py:31
  99.1 3.4 %collective-permute-done.4 = bf16[3,16,2048]{2,1,0:T(8,128)(2,1)S(1)} collective-permute-done((bf16[3,16,2048]{2,1,0:T(8,128)(2,1)S(1)}, bf16[3,16,2048]{2,1,0:T(8,128)(2,1)S(1)}, u32[]{:S(2)}, u32[]{:S(2)}) %collective-permute-start.4) | collective-permute-done | bytes 196640 | tf_op jit(solution)/shard_map/ppermute | solution.py:31
  104.1 4.6 %collective-permute-done.23 = bf16[3,16,2048]{2,1,0:T(8,128)(2,1)S(1)} collective-permute-done((bf16[3,16,2048]{2,1,0:T(8,128)(2,1)S(1)}, bf16[3,16,2048]{2,1,0:T(8,128)(2,1)S(1)}, u32[]{:S(2)}, u32[]{:S(2)}) %collective-permute-start.23) | collective-permute-done | bytes 196640 | tf_op jit(solution)/shard_map/ppermute | solution.py:31
  109.2 1.9 collective-permute-done.17
  112.6 2.5 %collective-permute-done.5 = bf16[3,16,2048]{2,1,0:T(8,128)(2,1)} collective-permute-done((bf16[3,16,2048]{2,1,0:T(8,128)(2,1)}, bf16[3,16,2048]{2,1,0:T(8,128)(2,1)}, u32[]{:S(2)}, u32[]{:S(2)}) %collective-permute-start.5) | collective-permute-done | bytes 196640 | tf_op jit(solution)/shard_map/ppermute | solution.py:31
  121.6 26.1 %all-gather.5.cloned.1.call-done = bf16[96,16,1152]{2,1,0:T(8,128)(2,1)} async-done(((bf16[12,16,1152]{2,1,0:T(8,128)(2,1)}), bf16[96,16,1152]{2,1,0:T(8,128)(2,1)}) %all-gather.5.cloned.1.call-update) | async-done | bytes 3538960 | tf_op jit(solution)/shard_map/all_gather | solution.py:100
  147.7 3.8 %gather_fusion.1 = bf16[32,16,1152]{2,1,0:T(8,128)(2,1)} fusion(bf16[96,16,1152]{2,1,0:T(8,128)(2,1)} %all-gather.5.cloned.1.call-done, s32[1024]{0:T(1024)S(1)} %pad_clamp_fusion), kind=kCustom, calls=%fused_computation.1 | custom fusion | bytes 2359424 | tf_op jit(solution)/shard_map/jit(_take)/gather | solution.py:101
  151.5 6.5 %all-to-all-start.1 = ((bf16[16,2,16,1152]{3,2,1,0:T(8,128)(2,1)}), bf16[16,2,16,1152]{3,2,1,0:T(8,128)(2,1)S(1)}, u32[]{:S(2)}, u32[]{:S(2)}) async-start(bf16[16,2,16,1152]{3,2,1,0:T(8,128)(2,1)} %bitcast.108), calls=%async_computation.1 | async-start | bytes 2359296 | tf_op jit(solution)/shard_map/all_to_all | solution.py:103
  158.0 20.7 %all-gather.3.cloned.1.call-done = bf16[96,16,1152]{2,1,0:T(8,128)(2,1)} async-done(((bf16[12,16,1152]{2,1,0:T(8,128)(2,1)}), bf16[96,16,1152]{2,1,0:T(8,128)(2,1)}) %all-gather.3.cloned.1.call-update) | async-done | bytes 3538960 | tf_op jit(solution)/shard_map/all_gather | solution.py:100
  178.8 3.7 %gather_fusion = bf16[32,16,1152]{2,1,0:T(8,128)(2,1)} fusion(bf16[96,16,1152]{2,1,0:T(8,128)(2,1)} %all-gather.3.cloned.1.call-done, s32[1024]{0:T(1024)S(1)} %pad_clamp_fusion), kind=kCustom, calls=%fused_computation | custom fusion | bytes 2359424 | tf_op jit(solution)/shard_map/jit(_take)/gather | solution.py:101
  182.5 6.6 %all-to-all-start = ((bf16[16,2,16,1152]{3,2,1,0:T(8,128)(2,1)}), bf16[16,2,16,1152]{3,2,1,0:T(8,128)(2,1)}, u32[]{:S(2)}, u32[]{:S(2)}) async-start(bf16[16,2,16,1152]{3,2,1,0:T(8,128)(2,1)} %bitcast.54), calls=%async_computation | async-start | bytes 2359296 | tf_op jit(solution)/shard_map/all_to_all | solution.py:103
  191.6 14.7 %all-to-all-done = bf16[16,2,16,1152]{3,2,1,0:T(8,128)(2,1)} async-done(((bf16[16,2,16,1152]{3,2,1,0:T(8,128)(2,1)}), bf16[16,2,16,1152]{3,2,1,0:T(8,128)(2,1)}, u32[]{:S(2)}, u32[]{:S(2)}) %all-to-all-start) | async-done | bytes 1179680 | tf_op jit(solution)/shard_map/all_to_all | solution.py:103
  207.6 1.5 fusion
  209.9 9.6 %multiply_reduce_fusion = (f32[]{:T(128)}, f32[1024,1024]{1,0:T(8,128)}) fusion(bf16[1,1024,1024]{2,1,0:T(8,128)(2,1)S(1)} %copy-done, bf16[1024,1024]{1,0:T(8,128)(2,1)} %bitcast.281, bf16[1,1024,1024]{2,1,0:T(8,128)(2,1)} %param.7), kind=kOutput, calls=%fused_computation.3 | convolution fusion | flops 4298113024 | bytes 10485764 | tf_op jit(solution)/shard_map/dot_general | solution.py:108
  220.9 4.1 %fusion.1 = bf16[1,1024,1024]{2,1,0:T(8,128)(2,1)} fusion(f32[1024,1024]{1,0:T(8,128)} %get-tuple-element.84, f32[]{:T(128)S(6)} %mul.537, pred[]{:T(512)} %bitcast), kind=kLoop, calls=%fused_computation.7 | loop fusion | flops 3145728 | bytes 6291461 | tf_op jit(solution)/shard_map/broadcast_in_dim | solution.py:111
  (149 shorter events, 34.8 us)
Async XLA Ops:
  6.5 203.4 %copy-start = (bf16[1,1024,1024]{2,1,0:T(8,128)(2,1)S(1)}, bf16[1,1024,1024]{2,1,0:T(8,128)(2,1)}, u32[]{:S(2)}) copy-start(bf16[1,1024,1024]{2,1,0:T(8,128)(2,1)} %param.8) | copy-start | bytes 6291460
  6.5 141.2 %all-gather.5.cloned.1.call-start = ((), (), s32[]{:S(2)}) async-start(), calls=%async_computation.3 | async-start | bytes 3981312 | tf_op jit(solution)/shard_map/all_gather | solution.py:100
  21.4 13.4 %collective-permute-start.13 = (bf16[3,4,16,2048]{3,2,0,1:T(8,128)(2,1)}, bf16[3,4,16,2048]{3,2,0,1:T(8,128)(2,1)}, u32[]{:S(2)}, u32[]{:S(2)}) collective-permute-start(bf16[3,4,16,2048]{3,2,0,1:T(8,128)(2,1)} %bitcast.270), channel_id=1, source_target_pairs={{0,96},{1,33},{2,98},{3,35},{4,100},{5,37},{6,102},{7,39},{8,104},... | collective-permute-start | bytes 2359304 | tf_op jit(solution)/shard_map/ppermute | solution.py:31
  26.3 15.4 %collective-permute-start.19 = (bf16[3,4,16,2048]{3,2,1,0:T(8,128)(2,1)}, bf16[3,4,16,2048]{3,2,1,0:T(8,128)(2,1)}, u32[]{:S(2)}, u32[]{:S(2)}) collective-permute-start(bf16[3,4,16,2048]{3,2,1,0:T(8,128)(2,1)} %get-tuple-element.14), channel_id=1, source_target_pairs={{0,24},{1,9},{2,26},{3,11},{4,28},{5,13},{6,30},{7,15},{8,0},{9,17... | collective-permute-start | bytes 2359304 | tf_op jit(solution)/shard_map/ppermute | solution.py:31
  27.5 36.7 %collective-permute-start.18 = (bf16[3,4,16,2048]{3,2,1,0:T(8,128)(2,1)}, bf16[3,4,16,2048]{3,2,1,0:T(8,128)(2,1)}, u32[]{:S(2)}, u32[]{:S(2)}) collective-permute-start(bf16[3,4,16,2048]{3,2,1,0:T(8,128)(2,1)} %get-tuple-element.13), channel_id=1, source_target_pairs={{0,8},{1,25},{2,10},{3,27},{4,12},{5,29},{6,14},{7,31},{8,16},{9,1... | collective-permute-start | bytes 2359304 | tf_op jit(solution)/shard_map/ppermute | solution.py:31
  30.0 44.1 %collective-permute-start.12 = (bf16[3,4,16,2048]{3,2,0,1:T(8,128)(2,1)}, bf16[3,4,16,2048]{3,2,0,1:T(8,128)(2,1)}, u32[]{:S(2)}, u32[]{:S(2)}) collective-permute-start(bf16[3,4,16,2048]{3,2,0,1:T(8,128)(2,1)} %bitcast.271), channel_id=1, source_target_pairs={{0,32},{1,97},{2,34},{3,99},{4,36},{5,101},{6,38},{7,103},{8,40},{... | collective-permute-start | bytes 2359304 | tf_op jit(solution)/shard_map/ppermute | solution.py:31
  33.7 24.8 %collective-permute-start.7 = (bf16[3,4,16,2048]{3,2,0,1:T(8,128)(2,1)S(1)}, bf16[3,4,16,2048]{3,2,0,1:T(8,128)(2,1)S(1)}, u32[]{:S(2)}, u32[]{:S(2)}) collective-permute-start(bf16[3,4,16,2048]{3,2,0,1:T(8,128)(2,1)S(1)} %bitcast.285), channel_id=1, source_target_pairs={{0,24},{1,9},{2,26},{3,11},{4,28},{5,13},{6,30},{7,15},{8,0},{9,17... | collective-permute-start | bytes 2359304 | tf_op jit(solution)/shard_map/ppermute | solution.py:31
  34.9 43.9 %collective-permute-start.6 = (bf16[3,4,16,2048]{3,2,0,1:T(8,128)(2,1)S(1)}, bf16[3,4,16,2048]{3,2,0,1:T(8,128)(2,1)S(1)}, u32[]{:S(2)}, u32[]{:S(2)}) collective-permute-start(bf16[3,4,16,2048]{3,2,0,1:T(8,128)(2,1)S(1)} %bitcast.283), channel_id=1, source_target_pairs={{0,8},{1,25},{2,10},{3,27},{4,12},{5,29},{6,14},{7,31},{8,16},{9,1... | collective-permute-start | bytes 2359304 | tf_op jit(solution)/shard_map/ppermute | solution.py:31
  41.7 18.6 %collective-permute-start.1 = (bf16[3,4,16,2048]{3,2,0,1:T(8,128)(2,1)S(1)}, bf16[3,4,16,2048]{3,2,0,1:T(8,128)(2,1)S(1)}, u32[]{:S(2)}, u32[]{:S(2)}) collective-permute-start(bf16[3,4,16,2048]{3,2,0,1:T(8,128)(2,1)S(1)} %bitcast.284), channel_id=1, source_target_pairs={{0,96},{1,33},{2,98},{3,35},{4,100},{5,37},{6,102},{7,39},{8,104},... | collective-permute-start | bytes 2359304 | tf_op jit(solution)/shard_map/ppermute | solution.py:31
  46.5 17.4 %copy-start.8 = (bf16[3,1,4,1,16,2048]{5,4,3,2,1,0:T(8,128)(2,1)S(1)}, bf16[3,1,4,1,16,2048]{5,4,3,2,1,0:T(8,128)(2,1)}, u32[]{:S(2)}) copy-start(bf16[3,1,4,1,16,2048]{5,4,3,2,1,0:T(8,128)(2,1)} %get-tuple-element.87) | copy-start | bytes 2359300
  58.4 13.8 %collective-permute-start.20 = (bf16[3,4,16,2048]{3,2,1,0:T(8,128)(2,1)S(1)}, bf16[3,4,16,2048]{3,2,1,0:T(8,128)(2,1)S(1)}, u32[]{:S(2)}, u32[]{:S(2)}) collective-permute-start(bf16[3,4,16,2048]{3,2,1,0:T(8,128)(2,1)S(1)} %fusion.7), channel_id=1, source_target_pairs={{0,24},{1,9},{2,26},{3,11},{4,28},{5,13},{6,30},{7,15},{8,0},{9,17... | collective-permute-start | bytes 2359304 | tf_op jit(solution)/shard_map/ppermute | solution.py:31
  60.4 16.3 %collective-permute-start.14 = (bf16[3,4,16,2048]{3,2,0,1:T(8,128)(2,1)S(1)}, bf16[3,4,16,2048]{3,2,0,1:T(8,128)(2,1)S(1)}, u32[]{:S(2)}, u32[]{:S(2)}) collective-permute-start(bf16[3,4,16,2048]{3,2,0,1:T(8,128)(2,1)S(1)} %fusion.10), channel_id=1, source_target_pairs={{0,96},{1,33},{2,98},{3,35},{4,100},{5,37},{6,102},{7,39},{8,104},... | collective-permute-start | bytes 2359304 | tf_op jit(solution)/shard_map/ppermute | solution.py:31
  64.2 13.0 %copy-start.7 = (bf16[3,1,4,1,16,2048]{5,4,3,2,1,0:T(8,128)(2,1)S(1)}, bf16[3,1,4,1,16,2048]{5,4,3,2,1,0:T(8,128)(2,1)}, u32[]{:S(2)}) copy-start(bf16[3,1,4,1,16,2048]{5,4,3,2,1,0:T(8,128)(2,1)} %get-tuple-element.15) | copy-start | bytes 2359300
  64.3 21.5 %collective-permute-start = (bf16[3,4,16,2048]{3,2,0,1:T(8,128)(2,1)S(1)}, bf16[3,4,16,2048]{3,2,0,1:T(8,128)(2,1)S(1)}, u32[]{:S(2)}, u32[]{:S(2)}) collective-permute-start(bf16[3,4,16,2048]{3,2,0,1:T(8,128)(2,1)S(1)} %bitcast.282), channel_id=1, source_target_pairs={{0,32},{1,97},{2,34},{3,99},{4,36},{5,101},{6,38},{7,103},{8,40},{... | collective-permute-start | bytes 2359304 | tf_op jit(solution)/shard_map/ppermute | solution.py:31
  72.3 12.3 %collective-permute-start.8 = (bf16[3,4,16,2048]{3,2,0,1:T(8,128)(2,1)S(1)}, bf16[3,4,16,2048]{3,2,0,1:T(8,128)(2,1)S(1)}, u32[]{:S(2)}, u32[]{:S(2)}) collective-permute-start(bf16[3,4,16,2048]{3,2,0,1:T(8,128)(2,1)S(1)} %fusion.13), channel_id=1, source_target_pairs={{0,24},{1,9},{2,26},{3,11},{4,28},{5,13},{6,30},{7,15},{8,0},{9,17... | collective-permute-start | bytes 2359304 | tf_op jit(solution)/shard_map/ppermute | solution.py:31
  74.2 16.7 %collective-permute-start.2 = (bf16[3,4,16,2048]{3,2,0,1:T(8,128)(2,1)S(1)}, bf16[3,4,16,2048]{3,2,0,1:T(8,128)(2,1)S(1)}, u32[]{:S(2)}, u32[]{:S(2)}) collective-permute-start(bf16[3,4,16,2048]{3,2,0,1:T(8,128)(2,1)S(1)} %fusion.16), channel_id=1, source_target_pairs={{0,96},{1,33},{2,98},{3,35},{4,100},{5,37},{6,102},{7,39},{8,104},... | collective-permute-start | bytes 2359304 | tf_op jit(solution)/shard_map/ppermute | solution.py:31
  76.6 17.5 %collective-permute-start.22 = (bf16[3,16,2048]{2,1,0:T(8,128)(2,1)S(1)}, bf16[3,16,2048]{2,1,0:T(8,128)(2,1)S(1)}, u32[]{:S(2)}, u32[]{:S(2)}) collective-permute-start(bf16[3,16,2048]{2,1,0:T(8,128)(2,1)S(1)} %get-tuple-element.52), channel_id=1, source_target_pairs={{0,96},{1,33},{2,98},{3,35},{4,100},{5,37},{6,102},{7,39},{8,104},... | collective-permute-start | bytes 589832 | tf_op jit(solution)/shard_map/ppermute | solution.py:31
  78.8 24.9 %collective-permute-start.21 = (bf16[3,16,2048]{2,1,0:T(8,128)(2,1)S(1)}, bf16[3,16,2048]{2,1,0:T(8,128)(2,1)S(1)}, u32[]{:S(2)}, u32[]{:S(2)}) collective-permute-start(bf16[3,16,2048]{2,1,0:T(8,128)(2,1)S(1)} %get-tuple-element.51), channel_id=1, source_target_pairs={{0,32},{1,97},{2,34},{3,99},{4,36},{5,101},{6,38},{7,103},{8,40},{... | collective-permute-start | bytes 589832 | tf_op jit(solution)/shard_map/ppermute | solution.py:31
  84.6 10.5 %collective-permute-start.16 = (bf16[3,16,2048]{2,1,0:T(8,128)(2,1)S(1)}, bf16[3,16,2048]{2,1,0:T(8,128)(2,1)S(1)}, u32[]{:S(2)}, u32[]{:S(2)}) collective-permute-start(bf16[3,16,2048]{2,1,0:T(8,128)(2,1)S(1)} %get-tuple-element.54), channel_id=1, source_target_pairs={{0,24},{1,9},{2,26},{3,11},{4,28},{5,13},{6,30},{7,15},{8,0},{9,17... | collective-permute-start | bytes 589832 | tf_op jit(solution)/shard_map/ppermute | solution.py:31
  85.8 23.2 %collective-permute-start.15 = (bf16[3,16,2048]{2,1,0:T(8,128)(2,1)S(1)}, bf16[3,16,2048]{2,1,0:T(8,128)(2,1)S(1)}, u32[]{:S(2)}, u32[]{:S(2)}) collective-permute-start(bf16[3,16,2048]{2,1,0:T(8,128)(2,1)S(1)} %get-tuple-element.53), channel_id=1, source_target_pairs={{0,8},{1,25},{2,10},{3,27},{4,12},{5,29},{6,14},{7,31},{8,16},{9,1... | collective-permute-start | bytes 589832 | tf_op jit(solution)/shard_map/ppermute | solution.py:31
  90.9 7.3 %collective-permute-start.10 = (bf16[3,16,2048]{2,1,0:T(8,128)(2,1)S(1)}, bf16[3,16,2048]{2,1,0:T(8,128)(2,1)S(1)}, u32[]{:S(2)}, u32[]{:S(2)}) collective-permute-start(bf16[3,16,2048]{2,1,0:T(8,128)(2,1)S(1)} %get-tuple-element.56), channel_id=1, source_target_pairs={{0,96},{1,33},{2,98},{3,35},{4,100},{5,37},{6,102},{7,39},{8,104},... | collective-permute-start | bytes 589832 | tf_op jit(solution)/shard_map/ppermute | solution.py:31
  94.1 14.6 %copy-start.10 = (f32[3,32,4096]{2,1,0:T(8,128)S(1)}, f32[3,32,4096]{2,1,0:T(8,128)}, u32[]{:S(2)}) copy-start(f32[3,32,4096]{2,1,0:T(8,128)} %param.6) | copy-start | bytes 4718596
  94.1 23.5 %collective-permute-start.9 = (bf16[3,16,2048]{2,1,0:T(8,128)(2,1)}, bf16[3,16,2048]{2,1,0:T(8,128)(2,1)S(1)}, u32[]{:S(2)}, u32[]{:S(2)}) collective-permute-start(bf16[3,16,2048]{2,1,0:T(8,128)(2,1)} %get-tuple-element.55), channel_id=1, source_target_pairs={{0,32},{1,97},{2,34},{3,99},{4,36},{5,101},{6,38},{7,103},{8,40},{... | collective-permute-start | bytes 589832 | tf_op jit(solution)/shard_map/ppermute | solution.py:31
  95.1 7.4 %collective-permute-start.4 = (bf16[3,16,2048]{2,1,0:T(8,128)(2,1)S(1)}, bf16[3,16,2048]{2,1,0:T(8,128)(2,1)S(1)}, u32[]{:S(2)}, u32[]{:S(2)}) collective-permute-start(bf16[3,16,2048]{2,1,0:T(8,128)(2,1)S(1)} %get-tuple-element.58), channel_id=1, source_target_pairs={{0,24},{1,9},{2,26},{3,11},{4,28},{5,13},{6,30},{7,15},{8,0},{9,17... | collective-permute-start | bytes 589832 | tf_op jit(solution)/shard_map/ppermute | solution.py:31
  98.3 14.3 %collective-permute-start.3 = (bf16[3,16,2048]{2,1,0:T(8,128)(2,1)}, bf16[3,16,2048]{2,1,0:T(8,128)(2,1)}, u32[]{:S(2)}, u32[]{:S(2)}) collective-permute-start(bf16[3,16,2048]{2,1,0:T(8,128)(2,1)} %get-tuple-element.57), channel_id=1, source_target_pairs={{0,8},{1,25},{2,10},{3,27},{4,12},{5,29},{6,14},{7,31},{8,16},{9,1... | collective-permute-start | bytes 589832 | tf_op jit(solution)/shard_map/ppermute | solution.py:31
  102.5 6.1 %collective-permute-start.23 = (bf16[3,16,2048]{2,1,0:T(8,128)(2,1)S(1)}, bf16[3,16,2048]{2,1,0:T(8,128)(2,1)S(1)}, u32[]{:S(2)}, u32[]{:S(2)}) collective-permute-start(bf16[3,16,2048]{2,1,0:T(8,128)(2,1)S(1)} %fusion.23), channel_id=1, source_target_pairs={{0,96},{1,33},{2,98},{3,35},{4,100},{5,37},{6,102},{7,39},{8,104},... | collective-permute-start | bytes 589832 | tf_op jit(solution)/shard_map/ppermute | solution.py:31
  103.7 7.4 %collective-permute-start.17 = (bf16[3,16,2048]{2,1,0:T(8,128)(2,1)S(1)}, bf16[3,16,2048]{2,1,0:T(8,128)(2,1)S(1)}, u32[]{:S(2)}, u32[]{:S(2)}) collective-permute-start(bf16[3,16,2048]{2,1,0:T(8,128)(2,1)S(1)} %fusion.25), channel_id=1, source_target_pairs={{0,24},{1,9},{2,26},{3,11},{4,28},{5,13},{6,30},{7,15},{8,0},{9,17... | collective-permute-start | bytes 589832 | tf_op jit(solution)/shard_map/ppermute | solution.py:31
  108.7 9.0 %collective-permute-start.11 = (bf16[3,16,2048]{2,1,0:T(8,128)(2,1)}, bf16[3,16,2048]{2,1,0:T(8,128)(2,1)}, u32[]{:S(2)}, u32[]{:S(2)}) collective-permute-start(bf16[3,16,2048]{2,1,0:T(8,128)(2,1)} %fusion.27), channel_id=1, source_target_pairs={{0,96},{1,33},{2,98},{3,35},{4,100},{5,37},{6,102},{7,39},{8,104},... | collective-permute-start | bytes 589832 | tf_op jit(solution)/shard_map/ppermute | solution.py:31
  109.0 6.1 %collective-permute-start.5 = (bf16[3,16,2048]{2,1,0:T(8,128)(2,1)}, bf16[3,16,2048]{2,1,0:T(8,128)(2,1)}, u32[]{:S(2)}, u32[]{:S(2)}) collective-permute-start(bf16[3,16,2048]{2,1,0:T(8,128)(2,1)} %fusion.29), channel_id=1, source_target_pairs={{0,24},{1,9},{2,26},{3,11},{4,28},{5,13},{6,30},{7,15},{8,0},{9,17... | collective-permute-start | bytes 589832 | tf_op jit(solution)/shard_map/ppermute | solution.py:31
  112.6 66.2 %all-gather.3.cloned.1.call-start = ((), (), s32[]{:S(2)}) async-start(), calls=%async_computation.2 | async-start | bytes 3981312 | tf_op jit(solution)/shard_map/all_gather | solution.py:100
  151.5 31.0 %all-to-all-start.1 = ((bf16[16,2,16,1152]{3,2,1,0:T(8,128)(2,1)}), bf16[16,2,16,1152]{3,2,1,0:T(8,128)(2,1)S(1)}, u32[]{:S(2)}, u32[]{:S(2)}) async-start(bf16[16,2,16,1152]{3,2,1,0:T(8,128)(2,1)} %bitcast.108), calls=%async_computation.1 | async-start | bytes 2359296 | tf_op jit(solution)/shard_map/all_to_all | solution.py:103
  182.5 23.8 %all-to-all-start = ((bf16[16,2,16,1152]{3,2,1,0:T(8,128)(2,1)}), bf16[16,2,16,1152]{3,2,1,0:T(8,128)(2,1)}, u32[]{:S(2)}, u32[]{:S(2)}) async-start(bf16[16,2,16,1152]{3,2,1,0:T(8,128)(2,1)} %bitcast.54), calls=%async_computation | async-start | bytes 2359296 | tf_op jit(solution)/shard_map/all_to_all | solution.py:103
  (10 other events, 48.4 us)
Sparse Core Ops, SparseCore 0:
  112.7 34.9 all-gather.4
  149.4 29.3 all-gather.2

commit v2 on v1

v2 whole, which is shorter than its diff:
```python
import functools

import jax
import jax.numpy as jnp
from jax import lax
from jax.experimental import pallas as pl
from jax.experimental.pallas import tpu as pltpu
from jax.sharding import PartitionSpec as P

BETA_TWO = 0.999
ADAM_EPS = 1e-08
NORM_EPS = 1e-06
SIDE = 4
CHUNKS = 2
LANES = 128
VMEM_LIMIT = 48 * 1024 * 1024
F32 = jnp.float32
BF16 = jnp.bfloat16


def device_number(x, y, z, core):
    return ((x * SIDE + y) * SIDE + z) * 2 + core


def routes(move):
    pairs = []
    for x in range(SIDE):
        for y in range(SIDE):
            for z in range(SIDE):
                for core in range(2):
                    dx, dy, dz, swap = move(core)
                    target = device_number((x + dx) % SIDE, (y + dy) % SIDE, (z + dz) % SIDE, core ^ swap)
                    pairs.append((device_number(x, y, z, core), target))
    return pairs


def send(value, move):
    return lax.ppermute(value, ("dp", "mp"), routes(move))


def in_plane(phase, sign):
    return lambda core: (sign, 0, 0, 0) if core == phase else (0, sign, 0, 0)


def wide(value):
    return value.astype(F32)


def call(kernel, out_shape, grid, in_specs, out_specs, scratch=(), cost=1 << 20):
    return pl.pallas_call(
        kernel,
        out_shape=out_shape,
        grid_spec=pltpu.PrefetchScalarGridSpec(
            num_scalar_prefetch=1, grid=grid, in_specs=in_specs, out_specs=out_specs, scratch_shapes=list(scratch)
        ),
        compiler_params=pltpu.CompilerParams(vmem_limit_bytes=VMEM_LIMIT),
        cost_estimate=pl.CostEstimate(flops=cost, bytes_accessed=4 * cost, transcendentals=0),
    )


def row_block(ids, j, q):
    j, q = lax.rem(j + 2 * SIDE, SIDE), lax.rem(q + 2 * SIDE, SIDE)
    return jnp.where(ids[2] == 0, j * SIDE + q, q * SIDE + j)


def grads_spec(m, rows, half, chunk, offset, column, ahead=0):
    def index(t, ids):
        q = t if not ahead else lax.rem(ids[1] + ahead + t, SIDE)
        return 0, row_block(ids, ids[0] + offset, q), chunk, 0, column

    return pl.BlockSpec((m, 1, 1, rows, half), index)


def extract(ids, parts, chunk):
    m, _, _, rows, width = parts.shape
    half = width // 2

    def kernel(ids, a, b, c, d, up, down):
        up[0, :, 0] = a[:, 0, 0]
        up[1, :, 0] = b[:, 0, 0]
        down[0, :, 0] = c[:, 0, 0]
        down[1, :, 0] = d[:, 0, 0]

    spec = functools.partial(grads_spec, m, rows, half, chunk)
    out = jax.ShapeDtypeStruct((2, m, SIDE, rows, half), BF16)
    out_spec = pl.BlockSpec((2, m, 1, rows, half), lambda t, ids: (0, 0, t, 0, 0))
    return call(
        kernel,
        [out, out],
        (SIDE,),
        [spec(2, 1), spec(1, 0), spec(-2, 0), spec(-1, 1)],
        [out_spec, out_spec],
    )(ids, parts, parts, parts, parts)


def relay(ids, parts, from_up, from_down, chunk):
    m, _, _, rows, width = parts.shape
    half = width // 2

    def kernel(ids, a, b, below, above, up, down):
        up[:, 0] = (wide(a[:, 0, 0]) + wide(below[0, :, 0])).astype(BF16)
        down[:, 0] = (wide(b[:, 0, 0]) + wide(above[0, :, 0])).astype(BF16)

    spec = functools.partial(grads_spec, m, rows, half, chunk)
    out = jax.ShapeDtypeStruct((m, SIDE, rows, half), BF16)
    out_spec = pl.BlockSpec((m, 1, rows, half), lambda t, ids: (0, t, 0, 0))
    got = pl.BlockSpec((1, m, 1, rows, half), lambda t, ids: (0, 0, t, 0, 0))
    return call(kernel, [out, out], (SIDE,), [spec(1, 1), spec(-1, 0), got, got], [out_spec, out_spec])(
        ids, parts, parts, from_down, from_up
    )


def first_sum(ids, parts, from_up, from_down, late_up, late_down, chunk):
    m, _, _, rows, width = parts.shape
    half = width // 2

    def kernel(ids, own, below, above, late_above, late_below, total, up, down):
        t = pl.program_id(0)
        left = (wide(own[:, 0, 0, :, :half]) + wide(below[0, :, 0]) + wide(late_above[:, 0])).astype(BF16)
        right = (wide(own[:, 0, 0, :, half:]) + wide(above[0, :, 0]) + wide(late_below[:, 0])).astype(BF16)
        total[:, 0, :, :half] = left
        total[:, 0, :, half:] = right

        @pl.when(t == 0)
        def _():
            up[1] = left

        @pl.when(t == 1)
        def _():
            up[0] = right
            down[0] = left

        @pl.when(t == 2)
        def _():
            down[1] = right

    def at(t, ids):
        return lax.rem(ids[1] + 1 + t, SIDE)

    got = pl.BlockSpec((1, m, 1, rows, half), lambda t, ids: (1, 0, at(t, ids), 0, 0))
    late = pl.BlockSpec((m, 1, rows, half), lambda t, ids: (0, at(t, ids), 0, 0))
    whole = pl.BlockSpec((2, m, rows, half), lambda t, ids: (0, 0, 0, 0))
    return call(
        kernel,
        [jax.ShapeDtypeStruct((m, SIDE, rows, width), BF16)] + [jax.ShapeDtypeStruct((2, m, rows, half), BF16)] * 2,
        (SIDE,),
        [grads_spec(m, rows, width, chunk, 0, 0, ahead=1), got, got, late, late],
        [pl.BlockSpec((m, 1, rows, width), lambda t, ids: (0, at(t, ids), 0, 0)), whole, whole],
    )(ids, parts, from_down, from_up, late_up, late_down)


def second_relay(ids, total, from_up, from_down):
    m, _, rows, width = total.shape
    half = width // 2

    def kernel(ids, a, b, below, above, up, down):
        up[...] = (wide(a[:, 0]) + wide(below[0])).astype(BF16)
        down[...] = (wide(b[:, 0]) + wide(above[0])).astype(BF16)

    def spec(offset, column):
        return pl.BlockSpec(
            (m, 1, rows, half), lambda t, ids: (0, lax.rem(ids[1] + offset + SIDE, SIDE), 0, column)
        )

    out = jax.ShapeDtypeStruct((m, rows, half), BF16)
    out_spec = pl.BlockSpec((m, rows, half), lambda t, ids: (0, 0, 0))
    got = pl.BlockSpec((1, m, rows, half), lambda t, ids: (0, 0, 0, 0))
    return call(kernel, [out, out], (1,), [spec(1, 1), spec(-1, 0), got, got], [out_spec, out_spec])(
        ids, total, total, from_down, from_up
    )


def second_sum(ids, total, from_up, from_down, late_up, late_down, moment, chunk, block):
    m, _, rows, width = total.shape
    half = width // 2
    sides = width // block

    def kernel(ids, own, below, above, late_above, late_below, known, out):
        for side in range(sides):
            at = side * block
            here = slice(at % half, at % half + block)
            raw, late = (below, late_above) if at < half else (above, late_below)
            power = jnp.zeros((rows, LANES), F32)
            for k in range(at, at + block, LANES):
                piece = slice(k % half, k % half + LANES)
                gradient = wide(own[0, 0, :, k : k + LANES]) + wide(raw[0, 0, :, piece]) + wide(late[0, :, piece])
                second = BETA_TWO * known[0, 0, :, k : k + LANES] + (1.0 - BETA_TWO) * gradient * gradient
                direction = gradient / (jnp.sqrt(second) + ADAM_EPS)
                power = power + direction * direction
                out[side, :, k - at : k - at + LANES] = gradient.astype(BF16)
            out[side, :, block:] = power.astype(BF16)

    half_spec = pl.BlockSpec((1, rows, half), lambda t, ids: (t, 0, 0))
    got = pl.BlockSpec((1, 1, rows, half), lambda t, ids: (1, t, 0, 0))
    return call(
        kernel,
        jax.ShapeDtypeStruct((m * sides, rows, block + LANES), BF16),
        (m,),
        [
            pl.BlockSpec((1, 1, rows, width), lambda t, ids: (t, ids[1], 0, 0)),
            got,
            got,
            half_spec,
            half_spec,
            pl.BlockSpec((1, 1, rows, width), lambda t, ids: (t, chunk, 0, 0)),
        ],
        pl.BlockSpec((sides, rows, block + LANES), lambda t, ids: (t, 0, 0)),
    )(ids, total, from_down, from_up, late_up, late_down, moment)


def choose(picks, held):
    slots = picks.shape[0] // 2
    _, rows, columns = held[0].shape

    def kernel(picks, *refs):
        sources, out, sem = refs[: len(held)], refs[len(held)], refs[-1]

        @pl.loop(0, slots)
        def _(slot):
            for number, source in enumerate(sources):

                @pl.when(picks[2 * slot] == number)
                def _(source=source):
                    pltpu.make_async_copy(source.at[picks[2 * slot + 1]], out.at[slot], sem).start()

        pltpu.make_async_copy(out, out, sem).wait()

    anywhere = pl.BlockSpec(memory_space=pl.ANY)
    return call(
        kernel,
        jax.ShapeDtypeStruct((slots, rows, columns), BF16),
        (1,),
        [anywhere] * len(held),
        anywhere,
        [pltpu.SemaphoreType.DMA],
    )(picks, *held)


def finish(ids, received, swapped, left_root, right_root, block):
    dp_count, _, rows, _ = received[0].shape
    tile = 256

    def kernel(ids, *refs):
        count = len(received)
        same, other = refs[:count], refs[count : 2 * count]
        left, right, out, grads, shaped = refs[2 * count :]
        core = ids[0]
        power = jnp.zeros((rows, LANES), F32)
        for chunk in range(count):
            for group in range(dp_count):
                for ref, place in ((same[chunk], core), (other[chunk], 1 - core)):
                    at = pl.multiple_of((place * dp_count + group) * (count * rows) + chunk * rows, rows)
                    value = ref[group, 0]
                    grads[pl.ds(at, rows), :] = value[:, :block]
                    power = power + wide(value[:, block:])

        def step(i, total):
            at = pl.ds(pl.multiple_of(i * tile, tile), tile)
            first = jnp.dot(left[0, at, :], grads[...], preferred_element_type=F32).astype(BF16)
            value = jnp.dot(first, right[0], preferred_element_type=F32)
            shaped[at, :] = value
            return total + jnp.sum((value * value).reshape(tile // 8, 8, block), axis=0)

        total = lax.fori_loop(0, block // tile, step, jnp.zeros((8, block), F32))
        scale = jnp.sqrt(jnp.sum(power, keepdims=True)) * lax.rsqrt(jnp.sum(total, keepdims=True) + NORM_EPS)
        owned = ids[1] > 0

        @pl.when(owned)
        def _():
            out[0] = (shaped[...] * scale).astype(BF16)

        @pl.when(jnp.logical_not(owned))
        def _():
            out[0] = jnp.zeros((block, block), BF16)

    def whole(shape):
        return pl.BlockSpec(shape, lambda t, ids: (0,) * len(shape))

    return call(
        kernel,
        jax.ShapeDtypeStruct((1, block, block), BF16),
        (1,),
        [pl.BlockSpec((dp_count, 1) + v.shape[2:], lambda t, ids: (0, 0, 0, 0)) for v in received]
        + [whole(v.shape) for v in swapped]
        + [whole((1, block, block))] * 2,
        whole((1, block, block)),
        [pltpu.VMEM((block, block), BF16), pltpu.VMEM((block, block), F32)],
        cost=1 << 22,
    )(ids, *received, *swapped, left_root, right_root)


def slot_blocks(block_owner, slot_count):
    numbers = jnp.arange(block_owner.shape[0], dtype=jnp.int32)
    queries = jnp.arange(slot_count, dtype=jnp.int32)
    matches = (queries[:, None] == block_owner[None, :]).astype(jnp.int32)
    return jnp.sum(matches * numbers[None, :], axis=1), jnp.sum(matches, axis=1)


def shards(grad_parts, moment, left_roots, right_roots, block_owner):
    dp_count = lax.axis_size("dp")
    mp_count = lax.axis_size("mp")
    dp_index = lax.axis_index("dp")
    mp_index = lax.axis_index("mp")
    matrices = grad_parts.shape[1]
    width = grad_parts.shape[3]
    block = left_roots.shape[1]
    sides = width // block
    rows = moment.shape[1] // CHUNKS
    x, y = dp_index // SIDE, dp_index % SIDE
    z, core = mp_index // 2, mp_index % 2
    ids = jnp.stack([jnp.where(core == 0, x, y), jnp.where(core == 0, y, x), core]).astype(jnp.int32)
    parts = grad_parts.reshape(matrices, dp_count, CHUNKS, rows, width)
    known = moment.reshape(matrices, CHUNKS, rows, width)

    block_of, present = slot_blocks(block_owner, dp_count * mp_count)
    of_plane = lax.dynamic_slice_in_dim(block_of.reshape(dp_count, SIDE, 2), z, 1, 1)[:, 0]
    of_plane = jnp.where(core == 0, of_plane, of_plane[:, ::-1]).reshape(-1)
    offset = (of_plane // sides - z) % SIDE
    column = of_plane // (sides * sides) * sides + of_plane % sides
    picks = jnp.stack([offset, column], axis=1).reshape(-1).astype(jnp.int32)
    own = jnp.stack([core, present[dp_index * mp_count + mp_index]]).astype(jnp.int32)

    received, swapped = [], []
    for chunk in range(CHUNKS):
        up, down = extract(ids, parts, chunk)
        from_down, from_up = send(up, in_plane(0, 1)), send(down, in_plane(0, -1))
        up, down = relay(ids, parts, from_up, from_down, chunk)
        late_down, late_up = send(up, in_plane(0, 1)), send(down, in_plane(0, -1))
        total, up, down = first_sum(ids, parts, from_up, from_down, late_up, late_down, chunk)
        from_down, from_up = send(up, in_plane(1, 1)), send(down, in_plane(1, -1))
        up, down = second_relay(ids, total, from_up, from_down)
        late_down, late_up = send(up, in_plane(1, 1)), send(down, in_plane(1, -1))
        pieces = second_sum(ids, total, from_up, from_down, late_up, late_down, known, chunk, block)
        held = [pieces] + [send(pieces, lambda core, k=k: (0, 0, -k, 0)) for k in (1, 2, 3)]
        outgoing = choose(picks, held).reshape(dp_count, 2, rows, block + LANES)
        arrived = lax.all_to_all(outgoing, "dp", 0, 0, tiled=True)
        received.append(arrived)
        swapped.append(send(arrived[:, 1:], lambda core: (0, 0, 0, 1)))
    return finish(own, received, swapped, left_roots, right_roots, block)


def solution(mesh):
    placed = (
        P("dp", None, "mp", None),
        P(None, ("mp", "dp"), None),
        P(("dp", "mp"), None, None),
        P(("dp", "mp"), None, None),
        P(),
    )
    return jax.shard_map(
        shards, mesh=mesh, in_specs=placed, out_specs=P(("dp", "mp"), None, None), check_vma=False
    )
```

time: 234 us -> 210 us (0.90)
  Pallas kernels: 0 us -> 44.8 us
  local copies, waits for them, and re-layouts: 36.1 us -> 10.4 us
  other arithmetic: 21.1 us -> 1.42 us
  between operations: 16.1 us -> 0.26 us
  matrix products: 9.55 us -> 0 us
  waiting for transfers between devices: 104 us -> 112 us
  starting transfers between devices: 45.2 us -> 40.2 us
    ppermute x24, waiting for transfers between devices: 42.2 us -> 97.1 us  [send(): return lax.ppermute(value, ('dp', 'mp'), routes(move))]
    all_gather x2 -> x0, waiting for transfers between devices: 46.9 us -> none  [shards(): gathered = lax.all_gather(jnp.stack(pieces), 'mp', axis=0, tiled=True)]
    pallas_call x0 -> x13, Pallas kernels: none -> 44.8 us  [the longest x1 9.32 us: finish(): call(kernel, jax.ShapeDtypeStruct((1, block, block), BF16), (1,), [pl.Blo...]
    dot_general x1 -> x0, matrix products: 9.55 us -> none  [shards(): jnp.dot(first_step, right_roots[0], preferred_element_type=jnp.float32)]
    convert_element_type x12 -> x0, other arithmetic: 8.74 us -> none  [the longest x8 4.92 us: reduce_axis(): (wide(piece((position + step) % SIDE)) + wide(far)).astype(jnp.bfloat16)]
    gather x2 -> x0, local copies, waits for them, and re-layouts: 7.47 us -> none  [shards(): outgoing = jnp.take(gathered, picks, axis=0, mode='clip')]
    slice x5 -> x2, local copies, waits for them, and re-layouts: 8.71 us -> 1.73 us  [shards(): swapped.append(send(arrived[:, 1:], lambda core: (0, 0, 0, 1)))]
    dynamic_slice x3, local copies, waits for them, and re-layouts: 7.91 us -> 1.44 us  [the longest x2 0.85 us: shards(): lax.dynamic_slice_in_dim(block_of.reshape(dp_count, SIDE, 2), z, 1, 1)[:, 0]]
  transfers between devices with their start and end apart: 28 -> 26, of which waited for: 13 -> 14; matrix products, arithmetic and copies ran while one was open for 14% -> 3% of each run, Pallas kernels for 0% -> 15%
where the time goes in v2:
time: 210 us; the launch traced here: 209 us
  waiting for transfers between devices  112 us (53%)
  Pallas kernels  44.8 us (21%)
  starting transfers between devices  40.2 us (19%)
  local copies, waits for them, and re-layouts  10.4 us (5%)
    ppermute x24, waiting for transfers between devices, send(): return lax.ppermute(value, ('dp', 'mp'), routes(move))  97.1 us
    ppermute x24, starting transfers between devices, send(): return lax.ppermute(value, ('dp', 'mp'), routes(move))  31.6 us
    all_to_all x2, waiting for transfers between devices, shards(): arrived = lax.all_to_all(outgoing, 'dp', 0, 0, tiled=True)  15.2 us
    pallas_call x1, Pallas kernels, finish(): call(kernel, jax.ShapeDtypeStruct((1, block, block), BF16), (1,), [pl.Blo...  9.32 us
    all_to_all x2, starting transfers between devices, shards(): arrived = lax.all_to_all(outgoing, 'dp', 0, 0, tiled=True)  8.62 us
    pallas_call x2, Pallas kernels, relay(): call(kernel, [out, out], (SIDE,), [spec(1, 1), spec(-1, 0), got, got], [o...  8.02 us
    pallas_call x2, Pallas kernels, first_sum(): call(kernel, [jax.ShapeDtypeStruct((m, SIDE, rows, width), BF16)] + [jax....  7.45 us
    pallas_call x2, Pallas kernels, extract(): call(kernel, [out, out], (SIDE,), [spec(2, 1), spec(1, 0), spec(-2, 0), s...  7.21 us
  transfers between devices with their start and end apart: 26, of which 14 were waited for; matrix products, arithmetic and copies ran while one was open for 3% of the time, Pallas kernels for 15%

profile of v2, /device:TPU:1, one launch (start us, length us, event | category | flops | bytes accessed | tf_op | source)
XLA Modules:
  0.0 209.4 jit_solution(10526302822566814468)
XLA Ops:
  0.1 3.6 %shard_map.55 = (bf16[2,3,4,16,2048]{4,3,2,1,0:T(8,128)(2,1)S(1)}, bf16[2,3,4,16,2048]{4,3,2,1,0:T(8,128)(2,1)S(1)}) custom-call(s32[3]{0:T(128)S(1)} %pad_add_fusion.2.ids, bf16[3,16,2,16,4096]{4,3,2,1,0:T(8,128)(2,1)} %bitcast.13, bf16[3,16,2,16,4096]{4,3,2,1,0:T(8,128)(2,1)} %bitcast.14, bf16[3,16,2,16,4096]{4,3,2,1,0:T(8,128)(2,1)} %bitcast.15, ...), custom_call_target="tpu_custom_call" | custom-call | flops 1048576 | bytes 4194304 | tf_op jit(solution)/shard_map/pallas_call | solution.py:87
  3.7 2.2 %collective-permute-start = (bf16[2,3,4,16,2048]{4,3,2,1,0:T(8,128)(2,1)S(1)}, bf16[2,3,4,16,2048]{4,3,2,1,0:T(8,128)(2,1)S(1)}, u32[]{:S(2)}, u32[]{:S(2)}) collective-permute-start(bf16[2,3,4,16,2048]{4,3,2,1,0:T(8,128)(2,1)S(1)} %get-tuple-element.23), channel_id=1, source_target_pairs={{0,32},{1,9},{2,34},{3,11},{4,36},{5,13},{6,38},{7,15},{8,40},{9,1... | collective-permute-start | bytes 4718600 | tf_op jit(solution)/shard_map/ppermute | solution.py:38
  7.4 3.6 %shard_map.61 = (bf16[2,3,4,16,2048]{4,3,2,1,0:T(8,128)(2,1)S(1)}, bf16[2,3,4,16,2048]{4,3,2,1,0:T(8,128)(2,1)S(1)}) custom-call(s32[3]{0:T(128)S(1)} %pad_add_fusion.2.ids, bf16[3,16,2,16,4096]{4,3,2,1,0:T(8,128)(2,1)} %bitcast.17, bf16[3,16,2,16,4096]{4,3,2,1,0:T(8,128)(2,1)} %bitcast.18, bf16[3,16,2,16,4096]{4,3,2,1,0:T(8,128)(2,1)} %bitcast.19, ...), custom_call_target="tpu_custom_call" | custom-call | flops 1048576 | bytes 4194304 | tf_op jit(solution)/shard_map/pallas_call | solution.py:87
  11.1 2.7 %collective-permute-start.12 = (bf16[2,3,4,16,2048]{4,3,2,1,0:T(8,128)(2,1)S(1)}, bf16[2,3,4,16,2048]{4,3,2,1,0:T(8,128)(2,1)S(1)}, u32[]{:S(2)}, u32[]{:S(2)}) collective-permute-start(bf16[2,3,4,16,2048]{4,3,2,1,0:T(8,128)(2,1)S(1)} %get-tuple-element.33), channel_id=1, source_target_pairs={{0,96},{1,25},{2,98},{3,27},{4,100},{5,29},{6,102},{7,31},{8,104},... | collective-permute-start | bytes 4718600 | tf_op jit(solution)/shard_map/ppermute | solution.py:38
  13.8 11.7 %collective-permute-done.below = bf16[2,3,4,16,2048]{4,3,2,1,0:T(8,128)(2,1)S(1)} collective-permute-done((bf16[2,3,4,16,2048]{4,3,2,1,0:T(8,128)(2,1)S(1)}, bf16[2,3,4,16,2048]{4,3,2,1,0:T(8,128)(2,1)S(1)}, u32[]{:S(2)}, u32[]{:S(2)}) %collective-permute-start) | collective-permute-done | bytes 1572896 | tf_op jit(solution)/shard_map/ppermute | solution.py:38
  25.4 3.2 %shard_map.56 = (bf16[3,4,16,2048]{3,2,1,0:T(8,128)(2,1)S(1)}, bf16[3,4,16,2048]{3,2,1,0:T(8,128)(2,1)S(1)}) custom-call(s32[3]{0:T(128)S(1)} %pad_add_fusion.2.ids, bf16[3,16,2,16,4096]{4,3,2,1,0:T(8,128)(2,1)} %bitcast.21, bf16[3,16,2,16,4096]{4,3,2,1,0:T(8,128)(2,1)} %bitcast.22, bf16[2,3,4,16,2048]{4,3,2,1,0:T(8,128)(2,1)S(1)} %collective-permute-done.below, ...), custom_call_target="tpu_custom_call" | custom-call | flops 1048576 | bytes 4194304 | tf_op jit(solution)/shard_map/pallas_call | solution.py:108
  28.7 2.8 %collective-permute-start.2 = (bf16[3,4,16,2048]{3,2,1,0:T(8,128)(2,1)S(1)}, bf16[3,4,16,2048]{3,2,1,0:T(8,128)(2,1)S(1)}, u32[]{:S(2)}, u32[]{:S(2)}) collective-permute-start(bf16[3,4,16,2048]{3,2,1,0:T(8,128)(2,1)S(1)} %get-tuple-element.25), channel_id=1, source_target_pairs={{0,96},{1,25},{2,98},{3,27},{4,100},{5,29},{6,102},{7,31},{8,104},... | collective-permute-start | bytes 2359304 | tf_op jit(solution)/shard_map/ppermute | solution.py:38
  31.5 19.3 %collective-permute-done.2.late_above = bf16[3,4,16,2048]{3,2,1,0:T(8,128)(2,1)S(1)} collective-permute-done((bf16[3,4,16,2048]{3,2,1,0:T(8,128)(2,1)S(1)}, bf16[3,4,16,2048]{3,2,1,0:T(8,128)(2,1)S(1)}, u32[]{:S(2)}, u32[]{:S(2)}) %collective-permute-start.2) | collective-permute-done | bytes 786464 | tf_op jit(solution)/shard_map/ppermute | solution.py:38
  50.7 3.6 %shard_map.57 = (bf16[3,4,16,4096]{3,2,1,0:T(8,128)(2,1)S(1)}, bf16[2,3,16,2048]{3,2,1,0:T(8,128)(2,1)S(1)}, bf16[2,3,16,2048]{3,2,1,0:T(8,128)(2,1)S(1)}) custom-call(s32[3]{0:T(128)S(1)} %pad_add_fusion.2.ids, bf16[3,16,2,16,4096]{4,3,2,1,0:T(8,128)(2,1)} %bitcast.23, bf16[2,3,4,16,2048]{4,3,2,1,0:T(8,128)(2,1)S(1)} %collective-permute-done.below, ...), custom_call_target="tpu_custom_call" | custom-call | flops 1048576 | bytes 4194304 | tf_op jit(solution)/shard_map/pallas_call | solution.py:143
  57.1 4.8 %shard_map.62 = (bf16[3,4,16,2048]{3,2,1,0:T(8,128)(2,1)}, bf16[3,4,16,2048]{3,2,1,0:T(8,128)(2,1)}) custom-call(s32[3]{0:T(128)S(1)} %pad_add_fusion.2.ids, bf16[3,16,2,16,4096]{4,3,2,1,0:T(8,128)(2,1)} %bitcast.24, bf16[3,16,2,16,4096]{4,3,2,1,0:T(8,128)(2,1)} %bitcast.25, bf16[2,3,4,16,2048]{4,3,2,1,0:T(8,128)(2,1)S(1)} %collective-permute-done.11.below, ...), custom_call_target="tpu_custom_call" | custom-call | flops 1048576 | bytes 4194304 | tf_op jit(solution)/shard_map/pallas_call | solution.py:108
  61.9 2.8 %collective-permute-start.13 = (bf16[3,4,16,2048]{3,2,1,0:T(8,128)(2,1)}, bf16[3,4,16,2048]{3,2,1,0:T(8,128)(2,1)}, u32[]{:S(2)}, u32[]{:S(2)}) collective-permute-start(bf16[3,4,16,2048]{3,2,1,0:T(8,128)(2,1)} %get-tuple-element.34), channel_id=1, source_target_pairs={{0,96},{1,25},{2,98},{3,27},{4,100},{5,29},{6,102},{7,31},{8,104},... | collective-permute-start | bytes 2359304 | tf_op jit(solution)/shard_map/ppermute | solution.py:38
  69.9 3.5 %collective-permute-done.6.late_above = bf16[3,16,2048]{2,1,0:T(8,128)(2,1)} collective-permute-done((bf16[3,16,2048]{2,1,0:T(8,128)(2,1)}, bf16[3,16,2048]{2,1,0:T(8,128)(2,1)}, u32[]{:S(2)}, u32[]{:S(2)}) %collective-permute-start.6) | collective-permute-done | bytes 196640 | tf_op jit(solution)/shard_map/ppermute | solution.py:38
  73.4 2.2 %collective-permute-done.7.late_below = bf16[3,16,2048]{2,1,0:T(8,128)(2,1)} collective-permute-done((bf16[3,16,2048]{2,1,0:T(8,128)(2,1)}, bf16[3,16,2048]{2,1,0:T(8,128)(2,1)}, u32[]{:S(2)}, u32[]{:S(2)}) %collective-permute-start.7) | collective-permute-done | bytes 196640 | tf_op jit(solution)/shard_map/ppermute | solution.py:38
  76.6 3.4 %shard_map.59.refs_0_ = bf16[12,16,1152]{2,1,0:T(8,128)(2,1)} custom-call(s32[3]{0:T(128)S(1)} %pad_add_fusion.2.ids, bf16[3,4,16,4096]{3,2,1,0:T(8,128)(2,1)S(1)} %get-tuple-element.27.a.b.own, bf16[2,3,16,2048]{3,2,1,0:T(8,128)(2,1)S(1)} %collective-permute-done.4.below, bf16[2,3,16,2048]{3,2,1,0:T(8,128)(2,1)S(1)} %copy-done.9, ...), custom_call_target="tpu_custom_call" | custom-call | flops 1048576 | bytes 4194304 | tf_op jit(solution)/shard_map/pallas_call | solution.py:195
  80.0 3.7 %collective-permute-start.8 = (bf16[12,16,1152]{2,1,0:T(8,128)(2,1)}, bf16[12,16,1152]{2,1,0:T(8,128)(2,1)S(1)}, u32[]{:S(2)}, u32[]{:S(2)}) collective-permute-start(bf16[12,16,1152]{2,1,0:T(8,128)(2,1)} %shard_map.59.refs_0_), channel_id=1, source_target_pairs={{0,6},{1,7},{2,0},{3,1},{4,2},{5,3},{6,4},{7,5},{8,14},{9,15},{10,... | collective-permute-start | bytes 1327112 | tf_op jit(solution)/shard_map/ppermute | solution.py:38
  84.8 8.4 %collective-permute-done.8.refs_1_ = bf16[12,16,1152]{2,1,0:T(8,128)(2,1)S(1)} collective-permute-done((bf16[12,16,1152]{2,1,0:T(8,128)(2,1)}, bf16[12,16,1152]{2,1,0:T(8,128)(2,1)S(1)}, u32[]{:S(2)}, u32[]{:S(2)}) %collective-permute-start.8) | collective-permute-done | bytes 442400 | tf_op jit(solution)/shard_map/ppermute | solution.py:38
  93.2 13.1 %collective-permute-done.10.refs_3_ = bf16[12,16,1152]{2,1,0:T(8,128)(2,1)S(1)} collective-permute-done((bf16[12,16,1152]{2,1,0:T(8,128)(2,1)}, bf16[12,16,1152]{2,1,0:T(8,128)(2,1)S(1)}, u32[]{:S(2)}, u32[]{:S(2)}) %collective-permute-start.10) | collective-permute-done | bytes 442400 | tf_op jit(solution)/shard_map/ppermute | solution.py:38
  106.3 2.8 %shard_map.60 = bf16[32,16,1152]{2,1,0:T(8,128)(2,1)S(1)} custom-call(s32[64]{0:T(128)S(1)} %reshape.204.picks, bf16[12,16,1152]{2,1,0:T(8,128)(2,1)} %shard_map.59.refs_0_, bf16[12,16,1152]{2,1,0:T(8,128)(2,1)S(1)} %collective-permute-done.8.refs_1_, bf16[12,16,1152]{2,1,0:T(8,128)(2,1)S(1)} %collective-permute-done.9.refs_2_, ...), custom_call_target="tpu_custom_call" | custom-call | flops 1048576 | bytes 4194304 | tf_op jit(solution)/shard_map/pallas_call | solution.py:229
  110.2 4.3 %all-to-all-start = ((bf16[16,2,16,1152]{3,2,1,0:T(8,128)(2,1)}), bf16[16,2,16,1152]{3,2,1,0:T(8,128)(2,1)S(1)}, u32[]{:S(2)}, u32[]{:S(2)}) async-start(bf16[16,2,16,1152]{3,2,1,0:T(8,128)(2,1)} %bitcast.11), calls=%async_computation | async-start | bytes 2359296 | tf_op jit(solution)/shard_map/all_to_all | solution.py:336
  116.0 3.9 %shard_map.63 = (bf16[3,4,16,4096]{3,2,1,0:T(8,128)(2,1)S(1)}, bf16[2,3,16,2048]{3,2,1,0:T(8,128)(2,1)S(1)}, bf16[2,3,16,2048]{3,2,1,0:T(8,128)(2,1)S(1)}) custom-call(s32[3]{0:T(128)S(1)} %pad_add_fusion.2.ids, bf16[3,16,2,16,4096]{4,3,2,1,0:T(8,128)(2,1)} %bitcast.26, bf16[2,3,4,16,2048]{4,3,2,1,0:T(8,128)(2,1)S(1)} %copy-done.2, ...), custom_call_target="tpu_custom_call" | custom-call | flops 1048576 | bytes 4194304 | tf_op jit(solution)/shard_map/pallas_call | solution.py:143
  122.6 12.8 %collective-permute-done.15.below = bf16[2,3,16,2048]{3,2,1,0:T(8,128)(2,1)S(1)} collective-permute-done((bf16[2,3,16,2048]{3,2,1,0:T(8,128)(2,1)S(1)}, bf16[2,3,16,2048]{3,2,1,0:T(8,128)(2,1)S(1)}, u32[]{:S(2)}, u32[]{:S(2)}) %collective-permute-start.15) | collective-permute-done | bytes 393248 | tf_op jit(solution)/shard_map/ppermute | solution.py:38
  137.6 3.3 %collective-permute-done.17.late_above = bf16[3,16,2048]{2,1,0:T(8,128)(2,1)S(1)} collective-permute-done((bf16[3,16,2048]{2,1,0:T(8,128)(2,1)S(1)}, bf16[3,16,2048]{2,1,0:T(8,128)(2,1)S(1)}, u32[]{:S(2)}, u32[]{:S(2)}) %collective-permute-start.17) | collective-permute-done | bytes 196640 | tf_op jit(solution)/shard_map/ppermute | solution.py:38
  143.8 1.7 collective-permute-start.20
  146.2 5.6 %collective-permute-done.19.refs_1_ = bf16[12,16,1152]{2,1,0:T(8,128)(2,1)S(1)} collective-permute-done((bf16[12,16,1152]{2,1,0:T(8,128)(2,1)S(1)}, bf16[12,16,1152]{2,1,0:T(8,128)(2,1)S(1)}, u32[]{:S(2)}, u32[]{:S(2)}) %collective-permute-start.19) | collective-permute-done | bytes 442400 | tf_op jit(solution)/shard_map/ppermute | solution.py:38
  151.8 1.5 collective-permute-done.20.refs_2_
  153.4 13.3 %collective-permute-done.21.refs_3_ = bf16[12,16,1152]{2,1,0:T(8,128)(2,1)S(1)} collective-permute-done((bf16[12,16,1152]{2,1,0:T(8,128)(2,1)S(1)}, bf16[12,16,1152]{2,1,0:T(8,128)(2,1)S(1)}, u32[]{:S(2)}, u32[]{:S(2)}) %collective-permute-start.21) | collective-permute-done | bytes 442400 | tf_op jit(solution)/shard_map/ppermute | solution.py:38
  166.7 3.3 %shard_map.66 = bf16[32,16,1152]{2,1,0:T(8,128)(2,1)S(1)} custom-call(s32[64]{0:T(128)S(1)} %reshape.204.picks, bf16[12,16,1152]{2,1,0:T(8,128)(2,1)S(1)} %shard_map.65.refs_0_, bf16[12,16,1152]{2,1,0:T(8,128)(2,1)S(1)} %collective-permute-done.19.refs_1_, bf16[12,16,1152]{2,1,0:T(8,128)(2,1)S(1)} %collective-permute-done.20.refs_2_, ...), custom_call_target="tpu_custom_call" | custom-call | flops 1048576 | bytes 4194304 | tf_op jit(solution)/shard_map/pallas_call | solution.py:229
  171.1 4.3 %all-to-all-start.1 = ((bf16[16,2,16,1152]{3,2,1,0:T(8,128)(2,1)}), bf16[16,2,16,1152]{3,2,1,0:T(8,128)(2,1)S(1)}, u32[]{:S(2)}, u32[]{:S(2)}) async-start(bf16[16,2,16,1152]{3,2,1,0:T(8,128)(2,1)} %bitcast.12), calls=%async_computation.1 | async-start | bytes 2359296 | tf_op jit(solution)/shard_map/all_to_all | solution.py:336
  177.0 15.2 %all-to-all-done.1.refs_1_ = bf16[16,2,16,1152]{3,2,1,0:T(8,128)(2,1)S(1)} async-done(((bf16[16,2,16,1152]{3,2,1,0:T(8,128)(2,1)}), bf16[16,2,16,1152]{3,2,1,0:T(8,128)(2,1)S(1)}, u32[]{:S(2)}, u32[]{:S(2)}) %all-to-all-start.1) | async-done | bytes 1179680 | tf_op jit(solution)/shard_map/all_to_all | solution.py:336
  193.1 3.4 %collective-permute-start.23 = (bf16[16,1,16,1152]{3,2,1,0:T(8,128)(2,1)}, bf16[16,1,16,1152]{3,2,1,0:T(8,128)(2,1)}, u32[]{:S(2)}, u32[]{:S(2)}) collective-permute-start(bf16[16,1,16,1152]{3,2,1,0:T(8,128)(2,1)} %slice.9), channel_id=1, source_target_pairs={{0,1},{1,0},{2,3},{3,2},{4,5},{5,4},{6,7},{7,6},{8,9},{9,8},{10,11... | collective-permute-start | bytes 1769480 | tf_op jit(solution)/shard_map/ppermute | solution.py:38
  198.5 1.6 copy-done.7
  200.0 9.3 %shard_map.67 = bf16[1,1024,1024]{2,1,0:T(8,128)(2,1)} custom-call(s32[2]{0:T(128)S(1)} %pad_add_fusion.1.ids, bf16[16,2,16,1152]{3,2,1,0:T(8,128)(2,1)S(1)} %all-to-all-done.refs_0_, bf16[16,2,16,1152]{3,2,1,0:T(8,128)(2,1)S(1)} %all-to-all-done.1.refs_1_, bf16[16,1,16,1152]{3,2,1,0:T(8,128)(2,1)S(1)} %collective-permute-done.22.refs_2_, ...), custom_call_target="tpu_custom_call" | custom-call | flops 4194304 | bytes 16777216 | tf_op jit(solution)/shard_map/pallas_call | solution.py:279
  (74 shorter events, 28.1 us)
Async XLA Ops:
  3.7 21.7 %collective-permute-start = (bf16[2,3,4,16,2048]{4,3,2,1,0:T(8,128)(2,1)S(1)}, bf16[2,3,4,16,2048]{4,3,2,1,0:T(8,128)(2,1)S(1)}, u32[]{:S(2)}, u32[]{:S(2)}) collective-permute-start(bf16[2,3,4,16,2048]{4,3,2,1,0:T(8,128)(2,1)S(1)} %get-tuple-element.23), channel_id=1, source_target_pairs={{0,32},{1,9},{2,34},{3,11},{4,36},{5,13},{6,38},{7,15},{8,40},{9,1... | collective-permute-start | bytes 4718600 | tf_op jit(solution)/shard_map/ppermute | solution.py:38
  5.9 19.6 %collective-permute-start.1 = (bf16[2,3,4,16,2048]{4,3,2,1,0:T(8,128)(2,1)S(1)}, bf16[2,3,4,16,2048]{4,3,2,1,0:T(8,128)(2,1)S(1)}, u32[]{:S(2)}, u32[]{:S(2)}) collective-permute-start(bf16[2,3,4,16,2048]{4,3,2,1,0:T(8,128)(2,1)S(1)} %get-tuple-element.24), channel_id=1, source_target_pairs={{0,96},{1,25},{2,98},{3,27},{4,100},{5,29},{6,102},{7,31},{8,104},... | collective-permute-start | bytes 4718600 | tf_op jit(solution)/shard_map/ppermute | solution.py:38
  11.0 46.0 %collective-permute-start.11 = (bf16[2,3,4,16,2048]{4,3,2,1,0:T(8,128)(2,1)S(1)}, bf16[2,3,4,16,2048]{4,3,2,1,0:T(8,128)(2,1)S(1)}, u32[]{:S(2)}, u32[]{:S(2)}) collective-permute-start(bf16[2,3,4,16,2048]{4,3,2,1,0:T(8,128)(2,1)S(1)} %get-tuple-element.32), channel_id=1, source_target_pairs={{0,32},{1,9},{2,34},{3,11},{4,36},{5,13},{6,38},{7,15},{8,40},{9,1... | collective-permute-start | bytes 4718600 | tf_op jit(solution)/shard_map/ppermute | solution.py:38
  11.1 46.0 %collective-permute-start.12 = (bf16[2,3,4,16,2048]{4,3,2,1,0:T(8,128)(2,1)S(1)}, bf16[2,3,4,16,2048]{4,3,2,1,0:T(8,128)(2,1)S(1)}, u32[]{:S(2)}, u32[]{:S(2)}) collective-permute-start(bf16[2,3,4,16,2048]{4,3,2,1,0:T(8,128)(2,1)S(1)} %get-tuple-element.33), channel_id=1, source_target_pairs={{0,96},{1,25},{2,98},{3,27},{4,100},{5,29},{6,102},{7,31},{8,104},... | collective-permute-start | bytes 4718600 | tf_op jit(solution)/shard_map/ppermute | solution.py:38
  25.4 3.2 %copy-start.4 = (bf16[2,3,4,16,2048]{4,3,2,1,0:T(8,128)(2,1)}, bf16[2,3,4,16,2048]{4,3,2,1,0:T(8,128)(2,1)S(1)}, u32[]{:S(2)}) copy-start(bf16[2,3,4,16,2048]{4,3,2,1,0:T(8,128)(2,1)S(1)} %collective-permute-done.1.above) | copy-start | bytes 4718596
  28.7 22.1 %collective-permute-start.2 = (bf16[3,4,16,2048]{3,2,1,0:T(8,128)(2,1)S(1)}, bf16[3,4,16,2048]{3,2,1,0:T(8,128)(2,1)S(1)}, u32[]{:S(2)}, u32[]{:S(2)}) collective-permute-start(bf16[3,4,16,2048]{3,2,1,0:T(8,128)(2,1)S(1)} %get-tuple-element.25), channel_id=1, source_target_pairs={{0,96},{1,25},{2,98},{3,27},{4,100},{5,29},{6,102},{7,31},{8,104},... | collective-permute-start | bytes 2359304 | tf_op jit(solution)/shard_map/ppermute | solution.py:38
  31.5 19.3 %collective-permute-start.3 = (bf16[3,4,16,2048]{3,2,1,0:T(8,128)(2,1)S(1)}, bf16[3,4,16,2048]{3,2,1,0:T(8,128)(2,1)S(1)}, u32[]{:S(2)}, u32[]{:S(2)}) collective-permute-start(bf16[3,4,16,2048]{3,2,1,0:T(8,128)(2,1)S(1)} %get-tuple-element.26), channel_id=1, source_target_pairs={{0,32},{1,9},{2,34},{3,11},{4,36},{5,13},{6,38},{7,15},{8,40},{9,1... | collective-permute-start | bytes 2359304 | tf_op jit(solution)/shard_map/ppermute | solution.py:38
  54.3 10.4 %collective-permute-start.4 = (bf16[2,3,16,2048]{3,2,1,0:T(8,128)(2,1)S(1)}, bf16[2,3,16,2048]{3,2,1,0:T(8,128)(2,1)S(1)}, u32[]{:S(2)}, u32[]{:S(2)}) collective-permute-start(bf16[2,3,16,2048]{3,2,1,0:T(8,128)(2,1)S(1)} %get-tuple-element.28), channel_id=1, source_target_pairs={{0,8},{1,33},{2,10},{3,35},{4,12},{5,37},{6,14},{7,39},{8,16},{9,4... | collective-permute-start | bytes 1179656 | tf_op jit(solution)/shard_map/ppermute | solution.py:38
  55.6 9.1 %collective-permute-start.5 = (bf16[2,3,16,2048]{3,2,1,0:T(8,128)(2,1)S(1)}, bf16[2,3,16,2048]{3,2,1,0:T(8,128)(2,1)S(1)}, u32[]{:S(2)}, u32[]{:S(2)}) collective-permute-start(bf16[2,3,16,2048]{3,2,1,0:T(8,128)(2,1)S(1)} %get-tuple-element.29), channel_id=1, source_target_pairs={{0,24},{1,97},{2,26},{3,99},{4,28},{5,101},{6,30},{7,103},{8,0},{9... | collective-permute-start | bytes 1179656 | tf_op jit(solution)/shard_map/ppermute | solution.py:38
  57.1 4.8 %copy-start.1 = (bf16[2,3,4,16,2048]{4,3,2,1,0:T(8,128)(2,1)}, bf16[2,3,4,16,2048]{4,3,2,1,0:T(8,128)(2,1)S(1)}, u32[]{:S(2)}) copy-start(bf16[2,3,4,16,2048]{4,3,2,1,0:T(8,128)(2,1)S(1)} %collective-permute-done.11.below) | copy-start | bytes 4718596
  57.1 4.8 %copy-start.3 = (bf16[2,3,4,16,2048]{4,3,2,1,0:T(8,128)(2,1)}, bf16[2,3,4,16,2048]{4,3,2,1,0:T(8,128)(2,1)S(1)}, u32[]{:S(2)}) copy-start(bf16[2,3,4,16,2048]{4,3,2,1,0:T(8,128)(2,1)S(1)} %collective-permute-done.12.above) | copy-start | bytes 4718596
  61.9 52.7 %collective-permute-start.13 = (bf16[3,4,16,2048]{3,2,1,0:T(8,128)(2,1)}, bf16[3,4,16,2048]{3,2,1,0:T(8,128)(2,1)}, u32[]{:S(2)}, u32[]{:S(2)}) collective-permute-start(bf16[3,4,16,2048]{3,2,1,0:T(8,128)(2,1)} %get-tuple-element.34), channel_id=1, source_target_pairs={{0,96},{1,25},{2,98},{3,27},{4,100},{5,29},{6,102},{7,31},{8,104},... | collective-permute-start | bytes 2359304 | tf_op jit(solution)/shard_map/ppermute | solution.py:38
  64.7 49.9 %collective-permute-start.14 = (bf16[3,4,16,2048]{3,2,1,0:T(8,128)(2,1)}, bf16[3,4,16,2048]{3,2,1,0:T(8,128)(2,1)}, u32[]{:S(2)}, u32[]{:S(2)}) collective-permute-start(bf16[3,4,16,2048]{3,2,1,0:T(8,128)(2,1)} %get-tuple-element.35), channel_id=1, source_target_pairs={{0,32},{1,9},{2,34},{3,11},{4,36},{5,13},{6,38},{7,15},{8,40},{9,1... | collective-permute-start | bytes 2359304 | tf_op jit(solution)/shard_map/ppermute | solution.py:38
  64.7 2.8 %copy-start.10 = (s32[48]{0:T(128)S(1)}, s32[48]{0:T(128)}, u32[]{:S(2)}) copy-start(s32[48]{0:T(128)} %param.9) | copy-start | bytes 580
  64.7 10.9 %copy-start = (f32[3,32,4096]{2,1,0:T(8,128)S(1)}, f32[3,32,4096]{2,1,0:T(8,128)}, u32[]{:S(2)}) copy-start(f32[3,32,4096]{2,1,0:T(8,128)} %param.6) | copy-start | bytes 4718596
  66.1 7.3 %collective-permute-start.6 = (bf16[3,16,2048]{2,1,0:T(8,128)(2,1)}, bf16[3,16,2048]{2,1,0:T(8,128)(2,1)}, u32[]{:S(2)}, u32[]{:S(2)}) collective-permute-start(bf16[3,16,2048]{2,1,0:T(8,128)(2,1)} %get-tuple-element.30), channel_id=1, source_target_pairs={{0,24},{1,97},{2,26},{3,99},{4,28},{5,101},{6,30},{7,103},{8,0},{9... | collective-permute-start | bytes 589832 | tf_op jit(solution)/shard_map/ppermute | solution.py:38
  67.4 8.2 %collective-permute-start.7 = (bf16[3,16,2048]{2,1,0:T(8,128)(2,1)}, bf16[3,16,2048]{2,1,0:T(8,128)(2,1)}, u32[]{:S(2)}, u32[]{:S(2)}) collective-permute-start(bf16[3,16,2048]{2,1,0:T(8,128)(2,1)} %get-tuple-element.31), channel_id=1, source_target_pairs={{0,8},{1,33},{2,10},{3,35},{4,12},{5,37},{6,14},{7,39},{8,16},{9,4... | collective-permute-start | bytes 589832 | tf_op jit(solution)/shard_map/ppermute | solution.py:38
  80.0 13.2 %collective-permute-start.8 = (bf16[12,16,1152]{2,1,0:T(8,128)(2,1)}, bf16[12,16,1152]{2,1,0:T(8,128)(2,1)S(1)}, u32[]{:S(2)}, u32[]{:S(2)}) collective-permute-start(bf16[12,16,1152]{2,1,0:T(8,128)(2,1)} %shard_map.59.refs_0_), channel_id=1, source_target_pairs={{0,6},{1,7},{2,0},{3,1},{4,2},{5,3},{6,4},{7,5},{8,14},{9,15},{10,... | collective-permute-start | bytes 1327112 | tf_op jit(solution)/shard_map/ppermute | solution.py:38
  83.7 9.5 %collective-permute-start.9 = (bf16[12,16,1152]{2,1,0:T(8,128)(2,1)}, bf16[12,16,1152]{2,1,0:T(8,128)(2,1)S(1)}, u32[]{:S(2)}, u32[]{:S(2)}) collective-permute-start(bf16[12,16,1152]{2,1,0:T(8,128)(2,1)} %shard_map.59.refs_0_), channel_id=1, source_target_pairs={{0,4},{1,5},{2,6},{3,7},{4,0},{5,1},{6,2},{7,3},{8,12},{9,13},{10,... | collective-permute-start | bytes 1327112 | tf_op jit(solution)/shard_map/ppermute | solution.py:38
  83.7 22.6 %collective-permute-start.10 = (bf16[12,16,1152]{2,1,0:T(8,128)(2,1)}, bf16[12,16,1152]{2,1,0:T(8,128)(2,1)S(1)}, u32[]{:S(2)}, u32[]{:S(2)}) collective-permute-start(bf16[12,16,1152]{2,1,0:T(8,128)(2,1)} %shard_map.59.refs_0_), channel_id=1, source_target_pairs={{0,2},{1,3},{2,4},{3,5},{4,6},{5,7},{6,0},{7,1},{8,10},{9,11},{10,... | collective-permute-start | bytes 1327112 | tf_op jit(solution)/shard_map/ppermute | solution.py:38
  110.2 60.8 %all-to-all-start = ((bf16[16,2,16,1152]{3,2,1,0:T(8,128)(2,1)}), bf16[16,2,16,1152]{3,2,1,0:T(8,128)(2,1)S(1)}, u32[]{:S(2)}, u32[]{:S(2)}) async-start(bf16[16,2,16,1152]{3,2,1,0:T(8,128)(2,1)} %bitcast.11), calls=%async_computation | async-start | bytes 2359296 | tf_op jit(solution)/shard_map/all_to_all | solution.py:336
  119.9 15.6 %collective-permute-start.15 = (bf16[2,3,16,2048]{3,2,1,0:T(8,128)(2,1)S(1)}, bf16[2,3,16,2048]{3,2,1,0:T(8,128)(2,1)S(1)}, u32[]{:S(2)}, u32[]{:S(2)}) collective-permute-start(bf16[2,3,16,2048]{3,2,1,0:T(8,128)(2,1)S(1)} %get-tuple-element.37), channel_id=1, source_target_pairs={{0,8},{1,33},{2,10},{3,35},{4,12},{5,37},{6,14},{7,39},{8,16},{9,4... | collective-permute-start | bytes 1179656 | tf_op jit(solution)/shard_map/ppermute | solution.py:38
  121.3 14.1 %collective-permute-start.16 = (bf16[2,3,16,2048]{3,2,1,0:T(8,128)(2,1)S(1)}, bf16[2,3,16,2048]{3,2,1,0:T(8,128)(2,1)S(1)}, u32[]{:S(2)}, u32[]{:S(2)}) collective-permute-start(bf16[2,3,16,2048]{3,2,1,0:T(8,128)(2,1)S(1)} %get-tuple-element.38), channel_id=1, source_target_pairs={{0,24},{1,97},{2,26},{3,99},{4,28},{5,101},{6,30},{7,103},{8,0},{9... | collective-permute-start | bytes 1179656 | tf_op jit(solution)/shard_map/ppermute | solution.py:38
  136.1 4.9 %collective-permute-start.17 = (bf16[3,16,2048]{2,1,0:T(8,128)(2,1)S(1)}, bf16[3,16,2048]{2,1,0:T(8,128)(2,1)S(1)}, u32[]{:S(2)}, u32[]{:S(2)}) collective-permute-start(bf16[3,16,2048]{2,1,0:T(8,128)(2,1)S(1)} %get-tuple-element.39), channel_id=1, source_target_pairs={{0,24},{1,97},{2,26},{3,99},{4,28},{5,101},{6,30},{7,103},{8,0},{9... | collective-permute-start | bytes 589832 | tf_op jit(solution)/shard_map/ppermute | solution.py:38
  136.7 5.7 %collective-permute-start.18 = (bf16[3,16,2048]{2,1,0:T(8,128)(2,1)S(1)}, bf16[3,16,2048]{2,1,0:T(8,128)(2,1)S(1)}, u32[]{:S(2)}, u32[]{:S(2)}) collective-permute-start(bf16[3,16,2048]{2,1,0:T(8,128)(2,1)S(1)} %get-tuple-element.40), channel_id=1, source_target_pairs={{0,8},{1,33},{2,10},{3,35},{4,12},{5,37},{6,14},{7,39},{8,16},{9,4... | collective-permute-start | bytes 589832 | tf_op jit(solution)/shard_map/ppermute | solution.py:38
  143.7 8.2 %collective-permute-start.19 = (bf16[12,16,1152]{2,1,0:T(8,128)(2,1)S(1)}, bf16[12,16,1152]{2,1,0:T(8,128)(2,1)S(1)}, u32[]{:S(2)}, u32[]{:S(2)}) collective-permute-start(bf16[12,16,1152]{2,1,0:T(8,128)(2,1)S(1)} %shard_map.65.refs_0_), channel_id=1, source_target_pairs={{0,6},{1,7},{2,0},{3,1},{4,2},{5,3},{6,4},{7,5},{8,14},{9,15},{10,... | collective-permute-start | bytes 1327112 | tf_op jit(solution)/shard_map/ppermute | solution.py:38
  143.8 9.6 %collective-permute-start.20 = (bf16[12,16,1152]{2,1,0:T(8,128)(2,1)S(1)}, bf16[12,16,1152]{2,1,0:T(8,128)(2,1)S(1)}, u32[]{:S(2)}, u32[]{:S(2)}) collective-permute-start(bf16[12,16,1152]{2,1,0:T(8,128)(2,1)S(1)} %shard_map.65.refs_0_), channel_id=1, source_target_pairs={{0,4},{1,5},{2,6},{3,7},{4,0},{5,1},{6,2},{7,3},{8,12},{9,13},{10,... | collective-permute-start | bytes 1327112 | tf_op jit(solution)/shard_map/ppermute | solution.py:38
  145.4 21.3 %collective-permute-start.21 = (bf16[12,16,1152]{2,1,0:T(8,128)(2,1)S(1)}, bf16[12,16,1152]{2,1,0:T(8,128)(2,1)S(1)}, u32[]{:S(2)}, u32[]{:S(2)}) collective-permute-start(bf16[12,16,1152]{2,1,0:T(8,128)(2,1)S(1)} %shard_map.65.refs_0_), channel_id=1, source_target_pairs={{0,2},{1,3},{2,4},{3,5},{4,6},{5,7},{6,0},{7,1},{8,10},{9,11},{10,... | collective-permute-start | bytes 1327112 | tf_op jit(solution)/shard_map/ppermute | solution.py:38
  171.1 21.2 %all-to-all-start.1 = ((bf16[16,2,16,1152]{3,2,1,0:T(8,128)(2,1)}), bf16[16,2,16,1152]{3,2,1,0:T(8,128)(2,1)S(1)}, u32[]{:S(2)}, u32[]{:S(2)}) async-start(bf16[16,2,16,1152]{3,2,1,0:T(8,128)(2,1)} %bitcast.12), calls=%async_computation.1 | async-start | bytes 2359296 | tf_op jit(solution)/shard_map/all_to_all | solution.py:336
  175.4 21.1 %copy-start.11 = (s32[128]{0:T(128)S(1)}, s32[128]{0:T(128)}, u32[]{:S(2)}) copy-start(s32[128]{0:T(128)} %get-tuple-element.42) | copy-start | bytes 1540
  176.2 21.5 %collective-permute-start.22 = (bf16[16,1,16,1152]{3,2,1,0:T(8,128)(2,1)}, bf16[16,1,16,1152]{3,2,1,0:T(8,128)(2,1)S(1)}, u32[]{:S(2)}, u32[]{:S(2)}) collective-permute-start(bf16[16,1,16,1152]{3,2,1,0:T(8,128)(2,1)} %slice.8), channel_id=1, source_target_pairs={{0,1},{1,0},{2,3},{3,2},{4,5},{5,4},{6,7},{7,6},{8,9},{9,8},{10,11... | collective-permute-start | bytes 1769480 | tf_op jit(solution)/shard_map/ppermute | solution.py:38
  193.1 5.3 %collective-permute-start.23 = (bf16[16,1,16,1152]{3,2,1,0:T(8,128)(2,1)}, bf16[16,1,16,1152]{3,2,1,0:T(8,128)(2,1)}, u32[]{:S(2)}, u32[]{:S(2)}) collective-permute-start(bf16[16,1,16,1152]{3,2,1,0:T(8,128)(2,1)} %slice.9), channel_id=1, source_target_pairs={{0,1},{1,0},{2,3},{3,2},{4,5},{5,4},{6,7},{7,6},{8,9},{9,8},{10,11... | collective-permute-start | bytes 1769480 | tf_op jit(solution)/shard_map/ppermute | solution.py:38
  (6 other events, 7.5 us)

commit v3 on v2

v3 whole, which is shorter than its diff:
```python
import functools

import jax
import jax.numpy as jnp
from jax import lax
from jax.experimental import pallas as pl
from jax.experimental.pallas import tpu as pltpu
from jax.sharding import PartitionSpec as P

BETA_TWO = 0.999
ADAM_EPS = 1e-08
NORM_EPS = 1e-06
SIDE = 4
CHUNKS = 2
LANES = 128
VMEM_LIMIT = 48 * 1024 * 1024
F32 = jnp.float32
BF16 = jnp.bfloat16


def device_number(x, y, z, core):
    return ((x * SIDE + y) * SIDE + z) * 2 + core


def routes(move):
    pairs = []
    for x in range(SIDE):
        for y in range(SIDE):
            for z in range(SIDE):
                for core in range(2):
                    dx, dy, dz, swap = move(core)
                    target = device_number((x + dx) % SIDE, (y + dy) % SIDE, (z + dz) % SIDE, core ^ swap)
                    pairs.append((device_number(x, y, z, core), target))
    return pairs


def send(value, move):
    return lax.ppermute(value, ("dp", "mp"), routes(move))


def in_plane(phase, sign):
    return lambda core: (sign, 0, 0, 0) if core == phase else (0, sign, 0, 0)


def wide(value):
    return value.astype(F32)


def call(kernel, out_shape, grid, in_specs, out_specs, scratch=(), cost=1, after=()):
    inputs = len(in_specs)
    in_specs = list(in_specs) + [pl.BlockSpec(memory_space=pl.ANY)] * len(after)

    def body(ids, *refs):
        kernel(ids, *refs[:inputs], *refs[len(in_specs) :])

    made = pl.pallas_call(
        body,
        out_shape=out_shape,
        grid_spec=pltpu.PrefetchScalarGridSpec(
            num_scalar_prefetch=1, grid=grid, in_specs=in_specs, out_specs=out_specs, scratch_shapes=list(scratch)
        ),
        compiler_params=pltpu.CompilerParams(vmem_limit_bytes=VMEM_LIMIT),
        cost_estimate=pl.CostEstimate(flops=cost, bytes_accessed=4 * cost, transcendentals=0),
    )
    return lambda *operands: made(*operands, *after)


def row_block(ids, j, q):
    j, q = lax.rem(j + 2 * SIDE, SIDE), lax.rem(q + 2 * SIDE, SIDE)
    return jnp.where(ids[2] == 0, j * SIDE + q, q * SIDE + j)


def grads_spec(m, rows, half, chunk, offset, column, ahead=0):
    def index(t, ids):
        q = t if not ahead else lax.rem(ids[1] + ahead + t, SIDE)
        return 0, row_block(ids, ids[0] + offset, q), chunk, 0, column

    return pl.BlockSpec((m, 1, 1, rows, half), index)


def extract(ids, parts, chunk, pieces, after):
    m, _, _, rows, width = parts.shape
    half = width // 2
    count = len(pieces) // 2

    def kernel(ids, *refs):
        sources, (up, down) = refs[: 2 * count], refs[2 * count :]
        for k in range(count):
            up[k, :, 0] = sources[k][:, 0, 0]
            down[k, :, 0] = sources[count + k][:, 0, 0]

    out = jax.ShapeDtypeStruct((count, m, SIDE, rows, half), BF16)
    out_spec = pl.BlockSpec((count, m, 1, rows, half), lambda t, ids: (0, 0, t, 0, 0))
    return call(
        kernel,
        [out, out],
        (SIDE,),
        [grads_spec(m, rows, half, chunk, *piece) for piece in pieces],
        [out_spec, out_spec],
        after=after,
    )(ids, *([parts] * len(pieces)))


def relay(ids, parts, from_up, from_down, chunk, after):
    m, _, _, rows, width = parts.shape
    half = width // 2

    def kernel(ids, a, b, below, above, up, down):
        up[:, 0] = (wide(a[:, 0, 0]) + wide(below[0, :, 0])).astype(BF16)
        down[:, 0] = (wide(b[:, 0, 0]) + wide(above[0, :, 0])).astype(BF16)

    spec = functools.partial(grads_spec, m, rows, half, chunk)
    out = jax.ShapeDtypeStruct((m, SIDE, rows, half), BF16)
    out_spec = pl.BlockSpec((m, 1, rows, half), lambda t, ids: (0, t, 0, 0))
    got = pl.BlockSpec((1, m, 1, rows, half), lambda t, ids: (0, 0, t, 0, 0))
    return call(
        kernel, [out, out], (SIDE,), [spec(1, 1), spec(-1, 0), got, got], [out_spec, out_spec], after=after
    )(ids, parts, parts, from_down, from_up)


def first_sum(ids, parts, from_up, from_down, late_up, late_down, chunk, after):
    m, _, _, rows, width = parts.shape
    half = width // 2

    def kernel(ids, own, below, above, late_above, late_below, mine, *others):
        t = pl.program_id(0)
        left = (wide(own[:, 0, 0, :, :half]) + wide(below[0, :, 0]) + wide(late_above[:, 0])).astype(BF16)
        right = (wide(own[:, 0, 0, :, half:]) + wide(above[0, :, 0]) + wide(late_below[:, 0])).astype(BF16)
        for number, out in enumerate((*others, mine)):

            @pl.when(t == number)
            def _(out=out):
                out[:, :, :half] = left
                out[:, :, half:] = right

    def at(t, ids):
        return lax.rem(ids[1] + 1 + t, SIDE)

    raw = from_up.shape[0] - 1
    got = pl.BlockSpec((1, m, 1, rows, half), lambda t, ids: (raw, 0, at(t, ids), 0, 0))
    late = pl.BlockSpec((m, 1, rows, half), lambda t, ids: (0, at(t, ids), 0, 0))
    whole = pl.BlockSpec((m, rows, width), lambda t, ids: (0, 0, 0))
    return call(
        kernel,
        [jax.ShapeDtypeStruct((m, rows, width), BF16)] * SIDE,
        (SIDE,),
        [grads_spec(m, rows, width, chunk, 0, 0, ahead=1), got, got, late, late],
        [whole] * SIDE,
        after=after,
    )(ids, parts, from_down, from_up, late_up, late_down)


def second_sum(ids, sums, moment, chunk, block, earlier, after):
    m, rows, width = sums[0].shape
    sides = width // block
    last = len(earlier) > 0

    def kernel(ids, *refs):
        terms, known, out = refs[: len(sums)], refs[len(sums)], refs[len(sums) + 1 + len(earlier)]
        for side in range(sides):
            at = side * block
            power = refs[len(sums) + 1][side] if last else jnp.zeros((rows, LANES), F32)
            for k in range(at, at + block, LANES):
                gradient = sum(wide(term[0, :, k : k + LANES]) for term in terms)
                second = BETA_TWO * known[0, 0, :, k : k + LANES] + (1.0 - BETA_TWO) * gradient * gradient
                direction = gradient / (jnp.sqrt(second) + ADAM_EPS)
                power = power + direction * direction
                out[side, :, k - at : k - at + LANES] = gradient.astype(BF16)
            if last:
                out[side, :, block:] = power.astype(BF16)
            else:
                refs[-1][side] = power

    power_spec = pl.BlockSpec((sides, rows, LANES), lambda t, ids: (t, 0, 0))
    columns = block + LANES * last
    shapes = [jax.ShapeDtypeStruct((m * sides, rows, columns), BF16)]
    specs = [pl.BlockSpec((sides, rows, columns), lambda t, ids: (t, 0, 0))]
    if not last:
        shapes.append(jax.ShapeDtypeStruct((m * sides, rows, LANES), F32))
        specs.append(power_spec)
    return call(
        kernel,
        shapes,
        (m,),
        [pl.BlockSpec((1, rows, width), lambda t, ids: (t, 0, 0))] * len(sums)
        + [pl.BlockSpec((1, 1, rows, width), lambda t, ids: (t, chunk, 0, 0))]
        + [power_spec] * len(earlier),
        specs,
        after=after,
    )(ids, *sums, moment, *earlier)


def choose(picks, held, columns, after):
    slots = picks.shape[0] // 2
    count = len(held[0])
    rows = held[0][0].shape[1]

    def kernel(picks, *refs):
        sources, out, sem = refs[: 2 * count], refs[2 * count], refs[-1]

        @pl.loop(0, slots)
        def _(slot):
            for number in range(count):

                @pl.when(picks[2 * slot] == number)
                def _(number=number):
                    for chunk in range(2):
                        piece = sources[chunk * count + number].at[picks[2 * slot + 1]]
                        there = out.at[slot, chunk, :, pl.ds(0, piece.shape[1])]
                        pltpu.make_async_copy(piece, there, sem).start()

        for chunk in range(2):
            there = out.at[:, chunk, :, pl.ds(0, sources[chunk * count].shape[2])]
            pltpu.make_async_copy(there, there, sem).wait()

    anywhere = pl.BlockSpec(memory_space=pl.ANY)
    return call(
        kernel,
        jax.ShapeDtypeStruct((slots, 2, rows, columns), BF16),
        (1,),
        [anywhere] * (2 * count),
        pl.BlockSpec((slots, 2, rows, columns), lambda t, ids: (0, 0, 0, 0)),
        [pltpu.SemaphoreType.DMA],
        after=after,
    )(picks, *held[0], *held[1])


def finish(ids, same, other, left_root, right_root, block):
    dp_count, _, _, rows, _ = same.shape
    tile = 512

    def kernel(ids, same, other, left, right, out, grads, powers, shaped, sem):
        core = ids[0]
        copies = []
        for k, (ref, place) in enumerate(((same, core), (other, 1 - core))):
            source = ref.at[:, k]
            copies.append(pltpu.make_async_copy(source.at[:, :, :, pl.ds(0, block)], grads.at[place], sem.at[0]))
            copies.append(pltpu.make_async_copy(source.at[:, 1, :, pl.ds(block, LANES)], powers.at[k], sem.at[1]))
        for copy in copies:
            copy.start()
        pltpu.make_async_copy(grads, grads, sem.at[0]).wait()

        def step(i, total):
            at = pl.ds(pl.multiple_of(i * tile, tile), tile)
            whole = grads[...].reshape(block, block)
            first = jnp.dot(left[0, at, :], whole, preferred_element_type=F32).astype(BF16)
            value = jnp.dot(first, right[0], preferred_element_type=F32)
            shaped[at, :] = value
            return total + jnp.sum((value * value).reshape(tile // 8, 8, block), axis=0)

        total = lax.fori_loop(0, block // tile, step, jnp.zeros((8, block), F32))
        pltpu.make_async_copy(powers, powers, sem.at[1]).wait()
        power = jnp.sum(wide(powers[...]).reshape(-1, 8, LANES), axis=0)
        scale = jnp.sqrt(jnp.sum(power, keepdims=True)) * lax.rsqrt(jnp.sum(total, keepdims=True) + NORM_EPS)
        owned = ids[1] > 0

        @pl.when(owned)
        def _():
            out[0] = (shaped[...] * scale).astype(BF16)

        @pl.when(jnp.logical_not(owned))
        def _():
            out[0] = jnp.zeros((block, block), BF16)

    root = pl.BlockSpec((1, block, block), lambda t, ids: (0, 0, 0))
    return call(
        kernel,
        jax.ShapeDtypeStruct((1, block, block), BF16),
        (1,),
        [pl.BlockSpec(memory_space=pl.ANY)] * 2 + [root, root],
        root,
        [
            pltpu.VMEM((2, dp_count, 2, rows, block), BF16),
            pltpu.VMEM((2, dp_count, rows, LANES), BF16),
            pltpu.VMEM((block, block), F32),
            pltpu.SemaphoreType.DMA((2,)),
        ],
        cost=1 << 20,
    )(ids, same, other, left_root, right_root)


def slot_blocks(block_owner, slot_count):
    numbers = jnp.arange(block_owner.shape[0], dtype=jnp.int32)
    queries = jnp.arange(slot_count, dtype=jnp.int32)
    matches = (queries[:, None] == block_owner[None, :]).astype(jnp.int32)
    return jnp.sum(matches * numbers[None, :], axis=1), jnp.sum(matches, axis=1)


def shards(grad_parts, moment, left_roots, right_roots, block_owner):
    dp_count = lax.axis_size("dp")
    mp_count = lax.axis_size("mp")
    dp_index = lax.axis_index("dp")
    mp_index = lax.axis_index("mp")
    matrices = grad_parts.shape[1]
    width = grad_parts.shape[3]
    block = left_roots.shape[1]
    sides = width // block
    rows = moment.shape[1] // CHUNKS
    x, y = dp_index // SIDE, dp_index % SIDE
    z, core = mp_index // 2, mp_index % 2
    ids = jnp.stack([jnp.where(core == 0, x, y), jnp.where(core == 0, y, x), core]).astype(jnp.int32)
    parts = grad_parts.reshape(matrices, dp_count, CHUNKS, rows, width)
    known = moment.reshape(matrices, CHUNKS, rows, width)

    block_of, present = slot_blocks(block_owner, dp_count * mp_count)
    of_plane = lax.dynamic_slice_in_dim(block_of.reshape(dp_count, SIDE, 2), z, 1, 1)[:, 0]
    of_plane = jnp.where(core == 0, of_plane, of_plane[:, ::-1])
    column = of_plane // (sides * sides) * sides + of_plane % sides
    plane = of_plane // sides % SIDE
    picks = jnp.stack([(plane - z) % SIDE, column], axis=2).reshape(-1)
    own = jnp.stack([core, present[dp_index * mp_count + mp_index]])

    def along(phase, up, down):
        return send(down, in_plane(phase, -1)), send(up, in_plane(phase, 1))

    def second_axis(mine, up, far, down):
        return [mine, send(far, in_plane(1, 2)), send(up, in_plane(1, 1)), send(down, in_plane(1, -1))]

    last = ()
    sent, late, sums = [], [], []
    for chunk in range(CHUNKS):
        up, down = extract(ids, parts, chunk, ((2, 1), (1, 0), (-2, 0), (-1, 1)), last)
        last = (up,)
        sent.append(along(0, up, down))
    for chunk in range(CHUNKS):
        up, down = relay(ids, parts, *sent[chunk], chunk, last)
        last = (up,)
        late.append(along(0, up, down))
    for chunk in range(CHUNKS):
        terms = first_sum(ids, parts, *sent[chunk], *late[chunk], chunk, last)
        last = (terms[0],)
        sums.append(second_axis(*terms))
    held = []
    power = []
    for chunk in range(CHUNKS):
        pieces, *power = second_sum(ids, sums[chunk], known, chunk, block, power, last)
        last = (pieces,)
        held.append([pieces] + [send(pieces, lambda core, k=k: (0, 0, -k, 0)) for k in (1, 2, 3)])
    outgoing = choose(picks, held, block + LANES, last)
    outgoing = outgoing.reshape(dp_count, 2, CHUNKS, rows, block + LANES)
    same = lax.all_to_all(outgoing, "dp", 0, 0, tiled=True)
    other = send(same, lambda core: (0, 0, 0, 1))
    return finish(own, same, other, left_roots, right_roots, block)


def solution(mesh):
    placed = (
        P("dp", None, "mp", None),
        P(None, ("mp", "dp"), None),
        P(("dp", "mp"), None, None),
        P(("dp", "mp"), None, None),
        P(),
    )
    return jax.shard_map(
        shards, mesh=mesh, in_specs=placed, out_specs=P(("dp", "mp"), None, None), check_vma=False
    )
```

time: 210 us -> 171 us (0.81)
  waiting for transfers between devices: 112 us -> 51.9 us
  blocking collectives: 0 us -> 28.4 us
  Pallas kernels: 44.8 us -> 38.8 us
  local copies, waits for them, and re-layouts: 10.4 us -> 4.43 us
  starting transfers between devices: 40.2 us -> 44.2 us
    ppermute x24 -> x21, waiting for transfers between devices: 97.1 us -> 51.9 us  [send(): return lax.ppermute(value, ('dp', 'mp'), routes(move))]
    all_to_all x0 -> x1, blocking collectives: none -> 28.4 us  [shards(): same = lax.all_to_all(outgoing, 'dp', 0, 0, tiled=True)]
    all_to_all x2 -> x0, waiting for transfers between devices: 15.2 us -> none  [shards(): arrived = lax.all_to_all(outgoing, 'dp', 0, 0, tiled=True)]
    ppermute x24 -> x21, starting transfers between devices: 31.6 us -> 44.2 us  [send(): return lax.ppermute(value, ('dp', 'mp'), routes(move))]
    all_to_all x2 -> x0, starting transfers between devices: 8.62 us -> none  [shards(): arrived = lax.all_to_all(outgoing, 'dp', 0, 0, tiled=True)]
    pallas_call x13 -> x10, Pallas kernels: 44.8 us -> 38.8 us  [call(): return lambda *operands: made(*operands, *after)]
    unnamed x24 -> x18, local copies, waits for them, and re-layouts: 6.09 us -> 3.37 us
  transfers between devices with their start and end apart: 26 -> 21, of which waited for: 14 -> 9; matrix products, arithmetic and copies ran while one was open for 3% -> 1% of each run, Pallas kernels for 15% -> 13%
where the time goes in v3:
time: 171 us; the launch traced here: 169 us
  waiting for transfers between devices  51.9 us (30%)
  starting transfers between devices  44.2 us (26%)
  Pallas kernels  38.8 us (23%)
  blocking collectives  28.4 us (17%)
  local copies, waits for them, and re-layouts  4.43 us (3%)
    ppermute x21, waiting for transfers between devices, send(): return lax.ppermute(value, ('dp', 'mp'), routes(move))  51.9 us
    ppermute x21, starting transfers between devices, send(): return lax.ppermute(value, ('dp', 'mp'), routes(move))  44.2 us
    pallas_call x10, Pallas kernels, call(): return lambda *operands: made(*operands, *after)  38.8 us
    all_to_all x1, blocking collectives, shards(): same = lax.all_to_all(outgoing, 'dp', 0, 0, tiled=True)  28.4 us
  transfers between devices with their start and end apart: 21, of which 9 were waited for; matrix products, arithmetic and copies ran while one was open for 1% of the time, Pallas kernels for 13%

profile of v3, /device:TPU:1, one launch (start us, length us, event | category | flops | bytes accessed | tf_op | source)
XLA Modules:
  0.0 168.8 jit_solution(13191038701884934494)
XLA Ops:
  0.1 3.6 %shard_map.55 = (bf16[2,3,4,16,2048]{4,3,2,1,0:T(8,128)(2,1)S(1)}, bf16[2,3,4,16,2048]{4,3,2,1,0:T(8,128)(2,1)S(1)}) custom-call(s32[3]{0:T(128)S(1)} %pad_add_fusion.2.ids, bf16[3,16,2,16,4096]{4,3,2,1,0:T(8,128)(2,1)} %bitcast.16, bf16[3,16,2,16,4096]{4,3,2,1,0:T(8,128)(2,1)} %bitcast.17, bf16[3,16,2,16,4096]{4,3,2,1,0:T(8,128)(2,1)} %bitcast.18, ...), custom_call_target="tpu_custom_call" | custom-call | flops 1 | bytes 4 | tf_op jit(solution)/shard_map/pallas_call | solution.py:65
  3.7 3.6 %collective-permute-start.1 = (bf16[2,3,4,16,2048]{4,3,2,1,0:T(8,128)(2,1)S(1)}, bf16[2,3,4,16,2048]{4,3,2,1,0:T(8,128)(2,1)S(1)}, u32[]{:S(2)}, u32[]{:S(2)}) collective-permute-start(bf16[2,3,4,16,2048]{4,3,2,1,0:T(8,128)(2,1)S(1)} %get-tuple-element.24), channel_id=1, source_target_pairs={{0,96},{1,25},{2,98},{3,27},{4,100},{5,29},{6,102},{7,31},{8,104},... | collective-permute-start | bytes 4718600 | tf_op jit(solution)/shard_map/ppermute | solution.py:38
  7.3 3.6 %shard_map.56 = (bf16[2,3,4,16,2048]{4,3,2,1,0:T(8,128)(2,1)S(1)}, bf16[2,3,4,16,2048]{4,3,2,1,0:T(8,128)(2,1)S(1)}) custom-call(s32[3]{0:T(128)S(1)} %pad_add_fusion.2.ids, bf16[3,16,2,16,4096]{4,3,2,1,0:T(8,128)(2,1)} %bitcast.20, bf16[3,16,2,16,4096]{4,3,2,1,0:T(8,128)(2,1)} %bitcast.21, bf16[3,16,2,16,4096]{4,3,2,1,0:T(8,128)(2,1)} %bitcast.22, ...), custom_call_target="tpu_custom_call" | custom-call | flops 1 | bytes 4 | tf_op jit(solution)/shard_map/pallas_call | solution.py:65
  10.9 2.7 %collective-permute-start.5 = (bf16[2,3,4,16,2048]{4,3,2,1,0:T(8,128)(2,1)S(1)}, bf16[2,3,4,16,2048]{4,3,2,1,0:T(8,128)(2,1)S(1)}, u32[]{:S(2)}, u32[]{:S(2)}) collective-permute-start(bf16[2,3,4,16,2048]{4,3,2,1,0:T(8,128)(2,1)S(1)} %get-tuple-element.28), channel_id=1, source_target_pairs={{0,96},{1,25},{2,98},{3,27},{4,100},{5,29},{6,102},{7,31},{8,104},... | collective-permute-start | bytes 4718600 | tf_op jit(solution)/shard_map/ppermute | solution.py:38
  13.7 11.0 %collective-permute-done.1.refs_3_.refs_2_ = bf16[2,3,4,16,2048]{4,3,2,1,0:T(8,128)(2,1)S(1)} collective-permute-done((bf16[2,3,4,16,2048]{4,3,2,1,0:T(8,128)(2,1)S(1)}, bf16[2,3,4,16,2048]{4,3,2,1,0:T(8,128)(2,1)S(1)}, u32[]{:S(2)}, u32[]{:S(2)}) %collective-permute-start.1) | collective-permute-done | bytes 1572896 | tf_op jit(solution)/shard_map/ppermute | solution.py:38
  24.7 3.4 %collective-permute-done.refs_2_.refs_1_ = bf16[2,3,4,16,2048]{4,3,2,1,0:T(8,128)(2,1)S(1)} collective-permute-done((bf16[2,3,4,16,2048]{4,3,2,1,0:T(8,128)(2,1)S(1)}, bf16[2,3,4,16,2048]{4,3,2,1,0:T(8,128)(2,1)S(1)}, u32[]{:S(2)}, u32[]{:S(2)}) %collective-permute-start) | collective-permute-done | bytes 1572896 | tf_op jit(solution)/shard_map/ppermute | solution.py:38
  28.1 3.2 %shard_map.57 = (bf16[3,4,16,2048]{3,2,1,0:T(8,128)(2,1)S(1)}, bf16[3,4,16,2048]{3,2,1,0:T(8,128)(2,1)S(1)}) custom-call(s32[3]{0:T(128)S(1)} %pad_add_fusion.2.ids, bf16[3,16,2,16,4096]{4,3,2,1,0:T(8,128)(2,1)} %bitcast.24, bf16[3,16,2,16,4096]{4,3,2,1,0:T(8,128)(2,1)} %bitcast.25, bf16[2,3,4,16,2048]{4,3,2,1,0:T(8,128)(2,1)S(1)} %collective-permute-done.refs_2_.refs_1_, ...), custom_call_target="tpu_custom_call" | custom-call | flops 1 | bytes 4 | tf_op jit(solution)/shard_map/pallas_call | solution.py:65
  31.4 1.5 collective-permute-start.3
  32.9 8.7 %collective-permute-done.5.refs_3_.refs_2_ = bf16[2,3,4,16,2048]{4,3,2,1,0:T(8,128)(2,1)S(1)} collective-permute-done((bf16[2,3,4,16,2048]{4,3,2,1,0:T(8,128)(2,1)S(1)}, bf16[2,3,4,16,2048]{4,3,2,1,0:T(8,128)(2,1)S(1)}, u32[]{:S(2)}, u32[]{:S(2)}) %collective-permute-start.5) | collective-permute-done | bytes 1572896 | tf_op jit(solution)/shard_map/ppermute | solution.py:38
  41.5 3.4 %collective-permute-done.4.refs_2_.refs_1_ = bf16[2,3,4,16,2048]{4,3,2,1,0:T(8,128)(2,1)S(1)} collective-permute-done((bf16[2,3,4,16,2048]{4,3,2,1,0:T(8,128)(2,1)S(1)}, bf16[2,3,4,16,2048]{4,3,2,1,0:T(8,128)(2,1)S(1)}, u32[]{:S(2)}, u32[]{:S(2)}) %collective-permute-start.4) | collective-permute-done | bytes 1572896 | tf_op jit(solution)/shard_map/ppermute | solution.py:38
  44.9 3.2 %shard_map.58 = (bf16[3,4,16,2048]{3,2,1,0:T(8,128)(2,1)S(1)}, bf16[3,4,16,2048]{3,2,1,0:T(8,128)(2,1)S(1)}) custom-call(s32[3]{0:T(128)S(1)} %pad_add_fusion.2.ids, bf16[3,16,2,16,4096]{4,3,2,1,0:T(8,128)(2,1)} %bitcast.26, bf16[3,16,2,16,4096]{4,3,2,1,0:T(8,128)(2,1)} %bitcast.27, bf16[2,3,4,16,2048]{4,3,2,1,0:T(8,128)(2,1)S(1)} %collective-permute-done.4.refs_2_.refs_1_, ...), custom_call_target="tpu_custom_call" | custom-call | flops 1 | bytes 4 | tf_op jit(solution)/shard_map/pallas_call | solution.py:65
  48.3 1.5 collective-permute-start.10
  50.0 3.4 %collective-permute-done.3.refs_4_ = bf16[3,4,16,2048]{3,2,1,0:T(8,128)(2,1)S(1)} collective-permute-done((bf16[3,4,16,2048]{3,2,1,0:T(8,128)(2,1)S(1)}, bf16[3,4,16,2048]{3,2,1,0:T(8,128)(2,1)S(1)}, u32[]{:S(2)}, u32[]{:S(2)}) %collective-permute-start.3) | collective-permute-done | bytes 786464 | tf_op jit(solution)/shard_map/ppermute | solution.py:38
  53.4 3.7 %shard_map.59 = (bf16[3,16,4096]{2,1,0:T(8,128)(2,1)S(1)}, bf16[3,16,4096]{2,1,0:T(8,128)(2,1)S(1)}, bf16[3,16,4096]{2,1,0:T(8,128)(2,1)S(1)}, bf16[3,16,4096]{2,1,0:T(8,128)(2,1)S(1)}) custom-call(s32[3]{0:T(128)S(1)} %pad_add_fusion.2.ids, bf16[3,16,2,16,4096]{4,3,2,1,0:T(8,128)(2,1)} %bitcast.28, ...), custom_call_target="tpu_custom_call" | custom-call | flops 1 | bytes 4 | tf_op jit(solution)/shard_map/pallas_call | solution.py:65
  57.1 2.5 %collective-permute-start.6 = (bf16[3,16,4096]{2,1,0:T(8,128)(2,1)S(1)}, bf16[3,16,4096]{2,1,0:T(8,128)(2,1)S(1)}, u32[]{:S(2)}, u32[]{:S(2)}) collective-permute-start(bf16[3,16,4096]{2,1,0:T(8,128)(2,1)S(1)} %get-tuple-element.31), channel_id=1, source_target_pairs={{0,16},{1,65},{2,18},{3,67},{4,20},{5,69},{6,22},{7,71},{8,24},{9,... | collective-permute-start | bytes 1179656 | tf_op jit(solution)/shard_map/ppermute | solution.py:38
  60.2 2.1 %collective-permute-start.8 = (bf16[3,16,4096]{2,1,0:T(8,128)(2,1)S(1)}, bf16[3,16,4096]{2,1,0:T(8,128)(2,1)S(1)}, u32[]{:S(2)}, u32[]{:S(2)}) collective-permute-start(bf16[3,16,4096]{2,1,0:T(8,128)(2,1)S(1)} %get-tuple-element.33), channel_id=1, source_target_pairs={{0,24},{1,97},{2,26},{3,99},{4,28},{5,101},{6,30},{7,103},{8,0},{9... | collective-permute-start | bytes 1179656 | tf_op jit(solution)/shard_map/ppermute | solution.py:38
  62.3 4.7 %shard_map.60 = (bf16[3,16,4096]{2,1,0:T(8,128)(2,1)S(1)}, bf16[3,16,4096]{2,1,0:T(8,128)(2,1)}, bf16[3,16,4096]{2,1,0:T(8,128)(2,1)}, bf16[3,16,4096]{2,1,0:T(8,128)(2,1)}) custom-call(s32[3]{0:T(128)S(1)} %pad_add_fusion.2.ids, bf16[3,16,2,16,4096]{4,3,2,1,0:T(8,128)(2,1)} %bitcast.29, ...), custom_call_target="tpu_custom_call" | custom-call | flops 1 | bytes 4 | tf_op jit(solution)/shard_map/pallas_call | solution.py:65
  67.0 7.3 %collective-permute-start.14 = (bf16[3,16,4096]{2,1,0:T(8,128)(2,1)}, bf16[3,16,4096]{2,1,0:T(8,128)(2,1)S(1)}, u32[]{:S(2)}, u32[]{:S(2)}) collective-permute-start(bf16[3,16,4096]{2,1,0:T(8,128)(2,1)} %get-tuple-element.37), channel_id=1, source_target_pairs={{0,16},{1,65},{2,18},{3,67},{4,20},{5,69},{6,22},{7,71},{8,24},{9,... | collective-permute-start | bytes 1179656 | tf_op jit(solution)/shard_map/ppermute | solution.py:38
  74.6 2.4 %collective-permute-start.16 = (bf16[3,16,4096]{2,1,0:T(8,128)(2,1)}, bf16[3,16,4096]{2,1,0:T(8,128)(2,1)}, u32[]{:S(2)}, u32[]{:S(2)}) collective-permute-start(bf16[3,16,4096]{2,1,0:T(8,128)(2,1)} %get-tuple-element.39), channel_id=1, source_target_pairs={{0,24},{1,97},{2,26},{3,99},{4,28},{5,101},{6,30},{7,103},{8,0},{9... | collective-permute-start | bytes 1179656 | tf_op jit(solution)/shard_map/ppermute | solution.py:38
  77.0 1.2 shard_map.61
  78.3 1.7 %collective-permute-start.13 = (bf16[12,16,1024]{2,1,0:T(8,128)(2,1)S(1)}, bf16[12,16,1024]{2,1,0:T(8,128)(2,1)S(1)}, u32[]{:S(2)}, u32[]{:S(2)}) collective-permute-start(bf16[12,16,1024]{2,1,0:T(8,128)(2,1)S(1)} %get-tuple-element.36.refs_6_.refs_0_), channel_id=1, source_target_pairs={{0,2},{1,3},{2,4},{3,5},{4,6},{5,7},{6,0},{7,1},{8,10},{9,11},{10,... | collective-permute-start | bytes 1179656 | tf_op jit(solution)/shard_map/ppermute | solution.py:38
  80.2 3.4 %collective-permute-start.12 = (bf16[12,16,1024]{2,1,0:T(8,128)(2,1)S(1)}, bf16[12,16,1024]{2,1,0:T(8,128)(2,1)}, u32[]{:S(2)}, u32[]{:S(2)}) collective-permute-start(bf16[12,16,1024]{2,1,0:T(8,128)(2,1)S(1)} %get-tuple-element.36.refs_6_.refs_0_), channel_id=1, source_target_pairs={{0,4},{1,5},{2,6},{3,7},{4,0},{5,1},{6,2},{7,3},{8,12},{9,13},{10,... | collective-permute-start | bytes 1179656 | tf_op jit(solution)/shard_map/ppermute | solution.py:38
  86.1 2.9 %shard_map.62.refs_4_.refs_8_ = bf16[12,16,1152]{2,1,0:T(8,128)(2,1)S(1)} custom-call(s32[3]{0:T(128)S(1)} %pad_add_fusion.2.ids, bf16[3,16,4096]{2,1,0:T(8,128)(2,1)S(1)} %get-tuple-element.35.refs_5_.refs_0_, bf16[3,16,4096]{2,1,0:T(8,128)(2,1)S(1)} %copy-done.7, bf16[3,16,4096]{2,1,0:T(8,128)(2,1)} %collective-permute-done.15.refs_2_, ...), custom_call_target="tpu_custom_call" | custom-call | flops 1 | bytes 4 | tf_op jit(solution)/shard_map/pallas_call | solution.py:65
  90.0 3.3 %collective-permute-start.18 = (bf16[12,16,1152]{2,1,0:T(8,128)(2,1)S(1)}, bf16[12,16,1152]{2,1,0:T(8,128)(2,1)S(1)}, u32[]{:S(2)}, u32[]{:S(2)}) collective-permute-start(bf16[12,16,1152]{2,1,0:T(8,128)(2,1)S(1)} %shard_map.62.refs_4_.refs_8_), channel_id=1, source_target_pairs={{0,4},{1,5},{2,6},{3,7},{4,0},{5,1},{6,2},{7,3},{8,12},{9,13},{10,... | collective-permute-start | bytes 1327112 | tf_op jit(solution)/shard_map/ppermute | solution.py:38
  94.4 7.6 %collective-permute-done.19.refs_7_ = bf16[12,16,1152]{2,1,0:T(8,128)(2,1)S(1)} collective-permute-done((bf16[12,16,1152]{2,1,0:T(8,128)(2,1)S(1)}, bf16[12,16,1152]{2,1,0:T(8,128)(2,1)S(1)}, u32[]{:S(2)}, u32[]{:S(2)}) %collective-permute-start.19) | collective-permute-done | bytes 442400 | tf_op jit(solution)/shard_map/ppermute | solution.py:38
  102.0 10.9 %collective-permute-done.18.refs_6_ = bf16[12,16,1152]{2,1,0:T(8,128)(2,1)S(1)} collective-permute-done((bf16[12,16,1152]{2,1,0:T(8,128)(2,1)S(1)}, bf16[12,16,1152]{2,1,0:T(8,128)(2,1)S(1)}, u32[]{:S(2)}, u32[]{:S(2)}) %collective-permute-start.18) | collective-permute-done | bytes 442400 | tf_op jit(solution)/shard_map/ppermute | solution.py:38
  112.9 4.1 %shard_map.63 = bf16[32,2,16,1152]{3,2,1,0:T(8,128)(2,1)S(1)} custom-call(s32[64]{0:T(128)S(1)} %reshape.17.ids, bf16[12,16,1024]{2,1,0:T(8,128)(2,1)S(1)} %get-tuple-element.36.refs_6_.refs_0_, bf16[12,16,1024]{2,1,0:T(8,128)(2,1)} %collective-permute-done.11.refs_1_, bf16[12,16,1024]{2,1,0:T(8,128)(2,1)} %collective-permute-done.12.refs_2_, ...), custom_call_target="tpu_custom_call" | custom-call | flops 1 | bytes 4 | tf_op jit(solution)/shard_map/pallas_call | solution.py:65
  117.0 28.4 %all_to_all.5.refs_0_ = bf16[16,2,2,16,1152]{4,3,2,1,0:T(8,128)(2,1)} all-to-all(bf16[16,2,2,16,1152]{4,3,2,1,0:T(8,128)(2,1)S(1)} %bitcast.13), channel_id=1, replica_groups=mesh['dp'=16,'mp'=8] {'dp'}, dimensions={0} | all-to-all | bytes 4718592 | tf_op jit(solution)/shard_map/all_to_all | solution.py:341
  145.5 8.8 %collective-permute-start.20 = (bf16[16,2,2,16,1152]{4,3,2,1,0:T(8,128)(2,1)}, bf16[16,2,2,16,1152]{4,3,2,1,0:T(8,128)(2,1)}, u32[]{:S(2)}, u32[]{:S(2)}) collective-permute-start(bf16[16,2,2,16,1152]{4,3,2,1,0:T(8,128)(2,1)} %all_to_all.5.refs_0_), channel_id=1, source_target_pairs={{0,1},{1,0},{2,3},{3,2},{4,5},{5,4},{6,7},{7,6},{8,9},{9,8},{10,11... | collective-permute-start | bytes 7077896 | tf_op jit(solution)/shard_map/ppermute | solution.py:38
  155.6 3.2 %collective-permute-done.20.refs_1_ = bf16[16,2,2,16,1152]{4,3,2,1,0:T(8,128)(2,1)} collective-permute-done((bf16[16,2,2,16,1152]{4,3,2,1,0:T(8,128)(2,1)}, bf16[16,2,2,16,1152]{4,3,2,1,0:T(8,128)(2,1)}, u32[]{:S(2)}, u32[]{:S(2)}) %collective-permute-start.20) | collective-permute-done | bytes 2359328 | tf_op jit(solution)/shard_map/ppermute | solution.py:38
  158.8 1.6 copy-done.4
  160.4 8.5 %shard_map.64 = bf16[1,1024,1024]{2,1,0:T(8,128)(2,1)} custom-call(s32[2]{0:T(128)S(1)} %pad_add_fusion.1.ids, bf16[16,2,2,16,1152]{4,3,2,1,0:T(8,128)(2,1)} %all_to_all.5.refs_0_, bf16[16,2,2,16,1152]{4,3,2,1,0:T(8,128)(2,1)} %collective-permute-done.20.refs_1_, bf16[1,1024,1024]{2,1,0:T(8,128)(2,1)S(1)} %copy-done.3, bf16[1,1024,1024]{2,1,0:T(8,128)(2,1)S(1)} %copy-done.4), custom_call_target="tpu_custom_call" | custom-call | flops 1048576 | bytes 4194304 | tf_op jit(solution)/shard_map/pallas_call | solution.py:65
  (51 shorter events, 7.5 us)
Async XLA Ops:
  3.7 21.0 %collective-permute-start.1 = (bf16[2,3,4,16,2048]{4,3,2,1,0:T(8,128)(2,1)S(1)}, bf16[2,3,4,16,2048]{4,3,2,1,0:T(8,128)(2,1)S(1)}, u32[]{:S(2)}, u32[]{:S(2)}) collective-permute-start(bf16[2,3,4,16,2048]{4,3,2,1,0:T(8,128)(2,1)S(1)} %get-tuple-element.24), channel_id=1, source_target_pairs={{0,96},{1,25},{2,98},{3,27},{4,100},{5,29},{6,102},{7,31},{8,104},... | collective-permute-start | bytes 4718600 | tf_op jit(solution)/shard_map/ppermute | solution.py:38
  7.3 20.8 %collective-permute-start = (bf16[2,3,4,16,2048]{4,3,2,1,0:T(8,128)(2,1)S(1)}, bf16[2,3,4,16,2048]{4,3,2,1,0:T(8,128)(2,1)S(1)}, u32[]{:S(2)}, u32[]{:S(2)}) collective-permute-start(bf16[2,3,4,16,2048]{4,3,2,1,0:T(8,128)(2,1)S(1)} %get-tuple-element.23.refs_4_), channel_id=1, source_target_pairs={{0,32},{1,9},{2,34},{3,11},{4,36},{5,13},{6,38},{7,15},{8,40},{9,1... | collective-permute-start | bytes 4718600 | tf_op jit(solution)/shard_map/ppermute | solution.py:38
  10.9 17.2 %copy-start.5 = (bf16[2,3,4,16,2048]{4,3,2,1,0:T(8,128)(2,1)}, bf16[2,3,4,16,2048]{4,3,2,1,0:T(8,128)(2,1)S(1)}, u32[]{:S(2)}) copy-start(bf16[2,3,4,16,2048]{4,3,2,1,0:T(8,128)(2,1)S(1)} %get-tuple-element.25.refs_4_) | copy-start | bytes 4718596
  10.9 30.6 %collective-permute-start.5 = (bf16[2,3,4,16,2048]{4,3,2,1,0:T(8,128)(2,1)S(1)}, bf16[2,3,4,16,2048]{4,3,2,1,0:T(8,128)(2,1)S(1)}, u32[]{:S(2)}, u32[]{:S(2)}) collective-permute-start(bf16[2,3,4,16,2048]{4,3,2,1,0:T(8,128)(2,1)S(1)} %get-tuple-element.28), channel_id=1, source_target_pairs={{0,96},{1,25},{2,98},{3,27},{4,100},{5,29},{6,102},{7,31},{8,104},... | collective-permute-start | bytes 4718600 | tf_op jit(solution)/shard_map/ppermute | solution.py:38
  13.7 31.3 %collective-permute-start.4 = (bf16[2,3,4,16,2048]{4,3,2,1,0:T(8,128)(2,1)S(1)}, bf16[2,3,4,16,2048]{4,3,2,1,0:T(8,128)(2,1)S(1)}, u32[]{:S(2)}, u32[]{:S(2)}) collective-permute-start(bf16[2,3,4,16,2048]{4,3,2,1,0:T(8,128)(2,1)S(1)} %get-tuple-element.25.refs_4_), channel_id=1, source_target_pairs={{0,32},{1,9},{2,34},{3,11},{4,36},{5,13},{6,38},{7,15},{8,40},{9,1... | collective-permute-start | bytes 4718600 | tf_op jit(solution)/shard_map/ppermute | solution.py:38
  24.7 6.6 %copy-start = (bf16[2,3,4,16,2048]{4,3,2,1,0:T(8,128)(2,1)}, bf16[2,3,4,16,2048]{4,3,2,1,0:T(8,128)(2,1)S(1)}, u32[]{:S(2)}) copy-start(bf16[2,3,4,16,2048]{4,3,2,1,0:T(8,128)(2,1)S(1)} %collective-permute-done.1.refs_3_.refs_2_) | copy-start | bytes 4718596
  31.3 18.6 %collective-permute-start.2 = (bf16[3,4,16,2048]{3,2,1,0:T(8,128)(2,1)S(1)}, bf16[3,4,16,2048]{3,2,1,0:T(8,128)(2,1)S(1)}, u32[]{:S(2)}, u32[]{:S(2)}) collective-permute-start(bf16[3,4,16,2048]{3,2,1,0:T(8,128)(2,1)S(1)} %get-tuple-element.26), channel_id=1, source_target_pairs={{0,96},{1,25},{2,98},{3,27},{4,100},{5,29},{6,102},{7,31},{8,104},... | collective-permute-start | bytes 2359304 | tf_op jit(solution)/shard_map/ppermute | solution.py:38
  31.4 22.0 %collective-permute-start.3 = (bf16[3,4,16,2048]{3,2,1,0:T(8,128)(2,1)S(1)}, bf16[3,4,16,2048]{3,2,1,0:T(8,128)(2,1)S(1)}, u32[]{:S(2)}, u32[]{:S(2)}) collective-permute-start(bf16[3,4,16,2048]{3,2,1,0:T(8,128)(2,1)S(1)} %get-tuple-element.27.refs_4_), channel_id=1, source_target_pairs={{0,32},{1,9},{2,34},{3,11},{4,36},{5,13},{6,38},{7,15},{8,40},{9,1... | collective-permute-start | bytes 2359304 | tf_op jit(solution)/shard_map/ppermute | solution.py:38
  41.5 6.6 %copy-start.2 = (bf16[2,3,4,16,2048]{4,3,2,1,0:T(8,128)(2,1)}, bf16[2,3,4,16,2048]{4,3,2,1,0:T(8,128)(2,1)S(1)}, u32[]{:S(2)}) copy-start(bf16[2,3,4,16,2048]{4,3,2,1,0:T(8,128)(2,1)S(1)} %collective-permute-done.5.refs_3_.refs_2_) | copy-start | bytes 4718596
  48.2 14.1 %collective-permute-start.9 = (bf16[3,4,16,2048]{3,2,1,0:T(8,128)(2,1)S(1)}, bf16[3,4,16,2048]{3,2,1,0:T(8,128)(2,1)S(1)}, u32[]{:S(2)}, u32[]{:S(2)}) collective-permute-start(bf16[3,4,16,2048]{3,2,1,0:T(8,128)(2,1)S(1)} %get-tuple-element.34), channel_id=1, source_target_pairs={{0,96},{1,25},{2,98},{3,27},{4,100},{5,29},{6,102},{7,31},{8,104},... | collective-permute-start | bytes 2359304 | tf_op jit(solution)/shard_map/ppermute | solution.py:38
  48.3 14.1 %collective-permute-start.10 = (bf16[3,4,16,2048]{3,2,1,0:T(8,128)(2,1)S(1)}, bf16[3,4,16,2048]{3,2,1,0:T(8,128)(2,1)S(1)}, u32[]{:S(2)}, u32[]{:S(2)}) collective-permute-start(bf16[3,4,16,2048]{3,2,1,0:T(8,128)(2,1)S(1)} %get-tuple-element.29.refs_5_), channel_id=1, source_target_pairs={{0,32},{1,9},{2,34},{3,11},{4,36},{5,13},{6,38},{7,15},{8,40},{9,1... | collective-permute-start | bytes 2359304 | tf_op jit(solution)/shard_map/ppermute | solution.py:38
  57.1 17.5 %collective-permute-start.6 = (bf16[3,16,4096]{2,1,0:T(8,128)(2,1)S(1)}, bf16[3,16,4096]{2,1,0:T(8,128)(2,1)S(1)}, u32[]{:S(2)}, u32[]{:S(2)}) collective-permute-start(bf16[3,16,4096]{2,1,0:T(8,128)(2,1)S(1)} %get-tuple-element.31), channel_id=1, source_target_pairs={{0,16},{1,65},{2,18},{3,67},{4,20},{5,69},{6,22},{7,71},{8,24},{9,... | collective-permute-start | bytes 1179656 | tf_op jit(solution)/shard_map/ppermute | solution.py:38
  59.6 17.4 %collective-permute-start.7 = (bf16[3,16,4096]{2,1,0:T(8,128)(2,1)S(1)}, bf16[3,16,4096]{2,1,0:T(8,128)(2,1)S(1)}, u32[]{:S(2)}, u32[]{:S(2)}) collective-permute-start(bf16[3,16,4096]{2,1,0:T(8,128)(2,1)S(1)} %get-tuple-element.32), channel_id=1, source_target_pairs={{0,8},{1,33},{2,10},{3,35},{4,12},{5,37},{6,14},{7,39},{8,16},{9,4... | collective-permute-start | bytes 1179656 | tf_op jit(solution)/shard_map/ppermute | solution.py:38
  60.2 16.8 %collective-permute-start.8 = (bf16[3,16,4096]{2,1,0:T(8,128)(2,1)S(1)}, bf16[3,16,4096]{2,1,0:T(8,128)(2,1)S(1)}, u32[]{:S(2)}, u32[]{:S(2)}) collective-permute-start(bf16[3,16,4096]{2,1,0:T(8,128)(2,1)S(1)} %get-tuple-element.33), channel_id=1, source_target_pairs={{0,24},{1,97},{2,26},{3,99},{4,28},{5,101},{6,30},{7,103},{8,0},{9... | collective-permute-start | bytes 1179656 | tf_op jit(solution)/shard_map/ppermute | solution.py:38
  62.3 14.7 %copy-start.1 = (f32[3,32,4096]{2,1,0:T(8,128)S(1)}, f32[3,32,4096]{2,1,0:T(8,128)}, u32[]{:S(2)}) copy-start(f32[3,32,4096]{2,1,0:T(8,128)} %param.6) | copy-start | bytes 4718596
  67.0 16.6 %collective-permute-start.14 = (bf16[3,16,4096]{2,1,0:T(8,128)(2,1)}, bf16[3,16,4096]{2,1,0:T(8,128)(2,1)S(1)}, u32[]{:S(2)}, u32[]{:S(2)}) collective-permute-start(bf16[3,16,4096]{2,1,0:T(8,128)(2,1)} %get-tuple-element.37), channel_id=1, source_target_pairs={{0,16},{1,65},{2,18},{3,67},{4,20},{5,69},{6,22},{7,71},{8,24},{9,... | collective-permute-start | bytes 1179656 | tf_op jit(solution)/shard_map/ppermute | solution.py:38
  74.3 10.8 %collective-permute-start.15 = (bf16[3,16,4096]{2,1,0:T(8,128)(2,1)}, bf16[3,16,4096]{2,1,0:T(8,128)(2,1)}, u32[]{:S(2)}, u32[]{:S(2)}) collective-permute-start(bf16[3,16,4096]{2,1,0:T(8,128)(2,1)} %get-tuple-element.38), channel_id=1, source_target_pairs={{0,8},{1,33},{2,10},{3,35},{4,12},{5,37},{6,14},{7,39},{8,16},{9,4... | collective-permute-start | bytes 1179656 | tf_op jit(solution)/shard_map/ppermute | solution.py:38
  74.6 10.5 %collective-permute-start.16 = (bf16[3,16,4096]{2,1,0:T(8,128)(2,1)}, bf16[3,16,4096]{2,1,0:T(8,128)(2,1)}, u32[]{:S(2)}, u32[]{:S(2)}) collective-permute-start(bf16[3,16,4096]{2,1,0:T(8,128)(2,1)} %get-tuple-element.39), channel_id=1, source_target_pairs={{0,24},{1,97},{2,26},{3,99},{4,28},{5,101},{6,30},{7,103},{8,0},{9... | collective-permute-start | bytes 1179656 | tf_op jit(solution)/shard_map/ppermute | solution.py:38
  77.0 3.0 %copy-start.8 = (s32[48]{0:T(128)S(1)}, s32[48]{0:T(128)}, u32[]{:S(2)}) copy-start(s32[48]{0:T(128)} %param.9) | copy-start | bytes 580
  78.3 15.0 %collective-permute-start.13 = (bf16[12,16,1024]{2,1,0:T(8,128)(2,1)S(1)}, bf16[12,16,1024]{2,1,0:T(8,128)(2,1)S(1)}, u32[]{:S(2)}, u32[]{:S(2)}) collective-permute-start(bf16[12,16,1024]{2,1,0:T(8,128)(2,1)S(1)} %get-tuple-element.36.refs_6_.refs_0_), channel_id=1, source_target_pairs={{0,2},{1,3},{2,4},{3,5},{4,6},{5,7},{6,0},{7,1},{8,10},{9,11},{10,... | collective-permute-start | bytes 1179656 | tf_op jit(solution)/shard_map/ppermute | solution.py:38
  80.2 14.2 %collective-permute-start.12 = (bf16[12,16,1024]{2,1,0:T(8,128)(2,1)S(1)}, bf16[12,16,1024]{2,1,0:T(8,128)(2,1)}, u32[]{:S(2)}, u32[]{:S(2)}) collective-permute-start(bf16[12,16,1024]{2,1,0:T(8,128)(2,1)S(1)} %get-tuple-element.36.refs_6_.refs_0_), channel_id=1, source_target_pairs={{0,4},{1,5},{2,6},{3,7},{4,0},{5,1},{6,2},{7,3},{8,12},{9,13},{10,... | collective-permute-start | bytes 1179656 | tf_op jit(solution)/shard_map/ppermute | solution.py:38
  83.6 0.8 copy-start.6
  84.4 10.0 %collective-permute-start.11 = (bf16[12,16,1024]{2,1,0:T(8,128)(2,1)S(1)}, bf16[12,16,1024]{2,1,0:T(8,128)(2,1)}, u32[]{:S(2)}, u32[]{:S(2)}) collective-permute-start(bf16[12,16,1024]{2,1,0:T(8,128)(2,1)S(1)} %get-tuple-element.36.refs_6_.refs_0_), channel_id=1, source_target_pairs={{0,6},{1,7},{2,0},{3,1},{4,2},{5,3},{6,4},{7,5},{8,14},{9,15},{10,... | collective-permute-start | bytes 1179656 | tf_op jit(solution)/shard_map/ppermute | solution.py:38
  85.1 1.0 copy-start.7
  89.1 13.0 %collective-permute-start.19 = (bf16[12,16,1152]{2,1,0:T(8,128)(2,1)S(1)}, bf16[12,16,1152]{2,1,0:T(8,128)(2,1)S(1)}, u32[]{:S(2)}, u32[]{:S(2)}) collective-permute-start(bf16[12,16,1152]{2,1,0:T(8,128)(2,1)S(1)} %shard_map.62.refs_4_.refs_8_), channel_id=1, source_target_pairs={{0,2},{1,3},{2,4},{3,5},{4,6},{5,7},{6,0},{7,1},{8,10},{9,11},{10,... | collective-permute-start | bytes 1327112 | tf_op jit(solution)/shard_map/ppermute | solution.py:38
  90.0 23.0 %collective-permute-start.18 = (bf16[12,16,1152]{2,1,0:T(8,128)(2,1)S(1)}, bf16[12,16,1152]{2,1,0:T(8,128)(2,1)S(1)}, u32[]{:S(2)}, u32[]{:S(2)}) collective-permute-start(bf16[12,16,1152]{2,1,0:T(8,128)(2,1)S(1)} %shard_map.62.refs_4_.refs_8_), channel_id=1, source_target_pairs={{0,4},{1,5},{2,6},{3,7},{4,0},{5,1},{6,2},{7,3},{8,12},{9,13},{10,... | collective-permute-start | bytes 1327112 | tf_op jit(solution)/shard_map/ppermute | solution.py:38
  93.3 19.7 %collective-permute-start.17 = (bf16[12,16,1152]{2,1,0:T(8,128)(2,1)S(1)}, bf16[12,16,1152]{2,1,0:T(8,128)(2,1)S(1)}, u32[]{:S(2)}, u32[]{:S(2)}) collective-permute-start(bf16[12,16,1152]{2,1,0:T(8,128)(2,1)S(1)} %shard_map.62.refs_4_.refs_8_), channel_id=1, source_target_pairs={{0,6},{1,7},{2,0},{3,1},{4,2},{5,3},{6,4},{7,5},{8,14},{9,15},{10,... | collective-permute-start | bytes 1327112 | tf_op jit(solution)/shard_map/ppermute | solution.py:38
  117.0 41.7 %copy-start.3 = (bf16[1,1024,1024]{2,1,0:T(8,128)(2,1)S(1)}, bf16[1,1024,1024]{2,1,0:T(8,128)(2,1)}, u32[]{:S(2)}) copy-start(bf16[1,1024,1024]{2,1,0:T(8,128)(2,1)} %refs_2_.1) | copy-start | bytes 6291460
  145.5 13.3 %collective-permute-start.20 = (bf16[16,2,2,16,1152]{4,3,2,1,0:T(8,128)(2,1)}, bf16[16,2,2,16,1152]{4,3,2,1,0:T(8,128)(2,1)}, u32[]{:S(2)}, u32[]{:S(2)}) collective-permute-start(bf16[16,2,2,16,1152]{4,3,2,1,0:T(8,128)(2,1)} %all_to_all.5.refs_0_), channel_id=1, source_target_pairs={{0,1},{1,0},{2,3},{3,2},{4,5},{5,4},{6,7},{7,6},{8,9},{9,8},{10,11... | collective-permute-start | bytes 7077896 | tf_op jit(solution)/shard_map/ppermute | solution.py:38
  158.8 1.6 copy-start.4

commit v4 on v3

v4 whole, which is shorter than its diff:
```python
import functools

import jax
import jax.numpy as jnp
from jax import lax
from jax.experimental import pallas as pl
from jax.experimental.pallas import tpu as pltpu
from jax.sharding import PartitionSpec as P

BETA_TWO = 0.999
ADAM_EPS = 1e-08
NORM_EPS = 1e-06
SIDE = 4
CHUNKS = 2
LANES = 128
PIECES = 12
VMEM_LIMIT = 12 * 1024 * 1024
VMEM_MOST = 48 * 1024 * 1024
F32 = jnp.float32
BF16 = jnp.bfloat16


def device_number(x, y, z, core):
    return ((x * SIDE + y) * SIDE + z) * 2 + core


def routes(move):
    pairs = []
    for x in range(SIDE):
        for y in range(SIDE):
            for z in range(SIDE):
                for core in range(2):
                    dx, dy, dz, swap = move(core)
                    target = device_number((x + dx) % SIDE, (y + dy) % SIDE, (z + dz) % SIDE, core ^ swap)
                    pairs.append((device_number(x, y, z, core), target))
    return pairs


def send(value, move):
    return lax.ppermute(value, ("dp", "z", "core"), routes(move))


def in_plane(phase, sign):
    return lambda core: (sign, 0, 0, 0) if core == phase else (0, sign, 0, 0)


def wide(value):
    return value.astype(F32)


def call(kernel, out_shape, grid, in_specs, out_specs, scratch=(), cost=1, after=(), grant=VMEM_MOST):
    inputs = len(in_specs)
    in_specs = list(in_specs) + [pl.BlockSpec(memory_space=pl.ANY)] * len(after)

    def body(ids, *refs):
        kernel(ids, *refs[:inputs], *refs[len(in_specs) :])

    made = pl.pallas_call(
        body,
        out_shape=out_shape,
        grid_spec=pltpu.PrefetchScalarGridSpec(
            num_scalar_prefetch=1, grid=grid, in_specs=in_specs, out_specs=out_specs, scratch_shapes=list(scratch)
        ),
        compiler_params=pltpu.CompilerParams(vmem_limit_bytes=grant),
        cost_estimate=pl.CostEstimate(flops=cost, bytes_accessed=4 * cost, transcendentals=0),
    )
    return lambda *operands: made(*operands, *after)


def row_block(ids, j, q):
    j, q = lax.rem(j + 2 * SIDE, SIDE), lax.rem(q + 2 * SIDE, SIDE)
    return jnp.where(ids[2] == 0, j * SIDE + q, q * SIDE + j)


def grads_spec(m, rows, half, chunk, offset, column, ahead=0):
    def index(t, ids):
        q = t if not ahead else lax.rem(ids[1] + ahead + t, SIDE)
        return 0, row_block(ids, ids[0] + offset, q), chunk, 0, column

    return pl.BlockSpec((m, 1, 1, rows, half), index)


def extract(ids, parts, chunk, pieces, after):
    m, _, _, rows, width = parts.shape
    half = width // 2
    count = len(pieces) // 2

    def kernel(ids, *refs):
        sources, (up, down) = refs[: 2 * count], refs[2 * count :]
        for k in range(count):
            up[k, :, 0] = sources[k][:, 0, 0]
            down[k, :, 0] = sources[count + k][:, 0, 0]

    out = jax.ShapeDtypeStruct((count, m, SIDE, rows, half), BF16)
    out_spec = pl.BlockSpec((count, m, 1, rows, half), lambda t, ids: (0, 0, t, 0, 0))
    return call(
        kernel,
        [out, out],
        (SIDE,),
        [grads_spec(m, rows, half, chunk, *piece) for piece in pieces],
        [out_spec, out_spec],
        after=after,
    )(ids, *([parts] * len(pieces)))


def relay(ids, parts, from_up, from_down, chunk, after):
    m, _, _, rows, width = parts.shape
    half = width // 2

    def kernel(ids, a, b, below, above, up, down):
        up[:, 0] = (wide(a[:, 0, 0]) + wide(below[0, :, 0])).astype(BF16)
        down[:, 0] = (wide(b[:, 0, 0]) + wide(above[0, :, 0])).astype(BF16)

    spec = functools.partial(grads_spec, m, rows, half, chunk)
    out = jax.ShapeDtypeStruct((m, SIDE, rows, half), BF16)
    out_spec = pl.BlockSpec((m, 1, rows, half), lambda t, ids: (0, t, 0, 0))
    got = pl.BlockSpec((1, m, 1, rows, half), lambda t, ids: (0, 0, t, 0, 0))
    return call(
        kernel, [out, out], (SIDE,), [spec(1, 1), spec(-1, 0), got, got], [out_spec, out_spec], after=after
    )(ids, parts, parts, from_down, from_up)


def first_sum(ids, parts, from_up, from_down, late_up, late_down, chunk, after):
    m, _, _, rows, width = parts.shape
    half = width // 2

    def kernel(ids, own, below, above, late_above, late_below, mine, *others):
        t = pl.program_id(0)
        left = (wide(own[:, 0, 0, :, :half]) + wide(below[0, :, 0]) + wide(late_above[:, 0])).astype(BF16)
        right = (wide(own[:, 0, 0, :, half:]) + wide(above[0, :, 0]) + wide(late_below[:, 0])).astype(BF16)
        for number, out in enumerate((*others, mine)):

            @pl.when(t == number)
            def _(out=out):
                out[:, :, :half] = left
                out[:, :, half:] = right

    def at(t, ids):
        return lax.rem(ids[1] + 1 + t, SIDE)

    raw = from_up.shape[0] - 1
    got = pl.BlockSpec((1, m, 1, rows, half), lambda t, ids: (raw, 0, at(t, ids), 0, 0))
    late = pl.BlockSpec((m, 1, rows, half), lambda t, ids: (0, at(t, ids), 0, 0))
    whole = pl.BlockSpec((m, rows, width), lambda t, ids: (0, 0, 0))
    return call(
        kernel,
        [jax.ShapeDtypeStruct((m, rows, width), BF16)] * SIDE,
        (SIDE,),
        [grads_spec(m, rows, width, chunk, 0, 0, ahead=1), got, got, late, late],
        [whole] * SIDE,
        after=after,
    )(ids, parts, from_down, from_up, late_up, late_down)


def second_sum(ids, sums, moment, chunk, block, earlier, after):
    m, rows, width = sums[0].shape
    sides = width // block
    tiles = block // LANES
    last = len(earlier) > 0

    def kernel(ids, *refs):
        terms, known = refs[: len(sums)], refs[len(sums)]
        t = pl.program_id(0)
        if last:
            before, out, powers = refs[len(sums) + 1 :]
        else:
            out, powers = refs[len(sums) + 1 :]
        for side in range(sides):
            power = before[side] if last else jnp.zeros((rows, LANES), F32)
            for tile in range(tiles):
                at = pl.ds(side * block + tile * LANES, LANES)
                gradient = sum(wide(term[0, :, at]) for term in terms)
                second = BETA_TWO * known[0, 0, :, at] + (1.0 - BETA_TWO) * gradient * gradient
                direction = gradient / (jnp.sqrt(second) + ADAM_EPS)
                power = power + direction * direction
                out[(t * sides + side) * tiles + tile] = gradient.astype(BF16)
            if last:
                row = lax.broadcasted_iota(jnp.int32, (rows, LANES), 0)
                placed = jnp.where(row == t * sides + side, jnp.sum(power, axis=0, keepdims=True), 0.0)
                powers[...] = jnp.where(t + side == 0, 0.0, powers[...]) + placed
            else:
                powers[side] = power
        if last:

            @pl.when(t == m - 1)
            def _():
                out[m * sides * tiles] = powers[...].astype(BF16)

    power_spec = pl.BlockSpec((sides, rows, LANES), lambda t, ids: (t, 0, 0))
    shapes = [jax.ShapeDtypeStruct((m * sides * tiles + last, rows, LANES), BF16)]
    specs = [pl.BlockSpec((m * sides * tiles + last, rows, LANES), lambda t, ids: (0, 0, 0))]
    if not last:
        shapes.append(jax.ShapeDtypeStruct((m * sides, rows, LANES), F32))
        specs.append(power_spec)
    return call(
        kernel,
        shapes,
        (m,),
        [pl.BlockSpec((1, rows, width), lambda t, ids: (t, 0, 0))] * len(sums)
        + [pl.BlockSpec((1, 1, rows, width), lambda t, ids: (t, chunk, 0, 0))]
        + [power_spec] * len(earlier),
        specs,
        [pltpu.VMEM((rows, LANES), F32)] * last,
        after=after,
        grant=VMEM_LIMIT,
    )(ids, *sums, moment, *earlier)


def choose(picks, held, after):
    slots = picks.shape[0] // 2
    count = len(held[0])
    total, rows, _ = held[0][0].shape
    tiles = total // PIECES

    def kernel(picks, *refs):
        first, second, out = refs[:count], refs[count : 2 * count], refs[2 * count]

        @pl.loop(0, slots)
        def _(slot):
            piece = pl.ds(picks[2 * slot + 1] * tiles, tiles)
            for number in range(count):

                @pl.when(picks[2 * slot] == number)
                def _(number=number):
                    out[slot, :tiles] = first[number][piece]
                    out[slot, tiles : 2 * tiles] = second[number][piece]
                    out[slot, 2 * tiles] = second[number][total]

    def whole(shape):
        return pl.BlockSpec(shape, lambda t, ids: (0,) * len(shape))

    shape = (slots, 2 * tiles + 1, rows, LANES)
    return call(
        kernel,
        jax.ShapeDtypeStruct(shape, BF16),
        (1,),
        [whole(v.shape) for v in (*held[0], *held[1])],
        whole(shape),
        after=after,
        grant=VMEM_LIMIT,
    )(picks, *held[0], *held[1])


def finish(ids, received, left_root, right_root, block):
    dp_count, _, _, rows, _ = received.shape
    tiles = block // LANES
    step = block // 2

    def kernel(ids, received, left, right, out, landed, grads, lefts, rights, shaped, results, sem):
        get = pltpu.make_async_copy(received, landed, sem.at[0])
        get_left = pltpu.make_async_copy(left.at[0], lefts, sem.at[1])
        get_right = pltpu.make_async_copy(right.at[0], rights, sem.at[2])
        get.start()
        get_left.start()
        get_right.start()
        get.wait()

        @pl.loop(0, dp_count)
        def _(group):
            for core in range(2):
                for tile in range(2 * tiles):
                    columns = slice(tile % tiles * LANES, (tile % tiles + 1) * LANES)
                    grads[core, group, tile // tiles, :, columns] = landed[group, core, tile]

        get_left.wait()
        total = jnp.zeros((8, block), F32)
        for at in range(0, block, step):
            whole = grads[...].reshape(block, block)
            first = jnp.dot(lefts[at : at + step, :], whole, preferred_element_type=F32).astype(BF16)
            if at == 0:
                get_right.wait()
            value = jnp.dot(first, rights[...], preferred_element_type=F32)
            shaped[at : at + step, :] = value
            total = total + jnp.sum((value * value).reshape(step // 8, 8, block), axis=0)
        powers = wide(landed[:, :, 2 * tiles])
        row = lax.broadcasted_iota(jnp.int32, powers.shape, 2)
        power = jnp.sum(jnp.where(row == ids[1], powers, 0.0).reshape(-1, 8, LANES), axis=0)
        scale = jnp.sqrt(jnp.sum(power, keepdims=True)) * lax.rsqrt(jnp.sum(total, keepdims=True) + NORM_EPS)
        owned = ids[0] > 0
        for at in range(0, block, step):
            here = pl.ds(at, step)

            @pl.when(owned)
            def _():
                results[here] = (shaped[here] * scale).astype(BF16)

            @pl.when(jnp.logical_not(owned))
            def _():
                results[here] = jnp.zeros((step, block), BF16)

            pltpu.make_async_copy(results.at[here], out.at[0, here], sem.at[3]).start()
        pltpu.make_async_copy(results, out.at[0], sem.at[3]).wait()

    anywhere = pl.BlockSpec(memory_space=pl.ANY)
    return call(
        kernel,
        jax.ShapeDtypeStruct((1, block, block), BF16),
        (1,),
        [anywhere] * 3,
        anywhere,
        [
            pltpu.VMEM(received.shape, BF16),
            pltpu.VMEM((2, dp_count, 2, rows, block), BF16),
            pltpu.VMEM((block, block), BF16),
            pltpu.VMEM((block, block), BF16),
            pltpu.VMEM((block, block), F32),
            pltpu.VMEM((block, block), BF16),
            pltpu.SemaphoreType.DMA((4,)),
        ],
        cost=1 << 20,
        grant=60 * 1024 * 1024,
    )(ids, received, left_root, right_root)


def slot_blocks(block_owner, slot_count):
    numbers = jnp.arange(block_owner.shape[0], dtype=jnp.int32)
    queries = jnp.arange(slot_count, dtype=jnp.int32)
    matches = (queries[:, None] == block_owner[None, :]).astype(jnp.int32)
    return jnp.sum(matches * numbers[None, :], axis=1), jnp.sum(matches, axis=1)


def shards(grad_parts, moment, left_roots, right_roots, block_owner):
    dp_count = lax.axis_size("dp")
    dp_index = lax.axis_index("dp")
    matrices = grad_parts.shape[1]
    width = grad_parts.shape[3]
    block = left_roots.shape[1]
    sides = width // block
    rows = moment.shape[1] // CHUNKS
    x, y = dp_index // SIDE, dp_index % SIDE
    z, core = lax.axis_index("z"), lax.axis_index("core")
    ids = jnp.stack([jnp.where(core == 0, x, y), jnp.where(core == 0, y, x), core]).astype(jnp.int32)
    parts = grad_parts.reshape(matrices, dp_count, CHUNKS, rows, width)
    known = moment.reshape(matrices, CHUNKS, rows, width)

    block_of, present = slot_blocks(block_owner, dp_count * SIDE * 2)
    of_plane = lax.dynamic_slice_in_dim(block_of.reshape(dp_count, SIDE, 2), z, 1, 1).reshape(-1)
    column = of_plane // (sides * sides) * sides + of_plane % sides
    plane = of_plane // sides % SIDE
    picks = jnp.stack([(plane - z) % SIDE, column], axis=1).reshape(-1)
    mine = device_number(x, y, z, core)
    own_block = block_of[mine]
    own = jnp.stack([present[mine], own_block // (sides * sides) * sides + own_block % sides])

    def along(phase, up, down):
        return send(down, in_plane(phase, -1)), send(up, in_plane(phase, 1))

    def second_axis(mine, up, far, down):
        return [mine, send(down, in_plane(1, -1)), send(up, in_plane(1, 1)), send(far, in_plane(1, 2))]

    last = ()
    sent, late, sums = [], [], []
    for chunk in range(CHUNKS):
        up, down = extract(ids, parts, chunk, ((2, 1), (1, 0), (-2, 0), (-1, 1)), last)
        last = (up,)
        sent.append(along(0, up, down))
    for chunk in range(CHUNKS):
        up, down = relay(ids, parts, *sent[chunk], chunk, last)
        last = (up,)
        late.append(along(0, up, down))
    for chunk in range(CHUNKS):
        terms = first_sum(ids, parts, *sent[chunk], *late[chunk], chunk, last)
        last = (terms[0],)
        sums.append(second_axis(*terms))
    held = []
    power = []
    for chunk in range(CHUNKS):
        pieces, *power = second_sum(ids, sums[chunk], known, chunk, block, power, last)
        last = (pieces,)
        held.append([pieces] + [send(pieces, lambda core, k=k: (0, 0, -k, 0)) for k in (1, 2, 3)])
    outgoing = choose(picks, held, last)
    received = lax.all_to_all(outgoing, ("dp", "core"), 0, 0, tiled=True)
    received = received.reshape((dp_count, 2) + received.shape[1:])
    return finish(own, received, left_roots, right_roots, block)


def solution(mesh):
    split = jax.sharding.Mesh(mesh.devices.reshape(-1, SIDE, 2), ("dp", "z", "core"))
    placed = (
        P("dp", None, ("z", "core"), None),
        P(None, ("z", "core", "dp"), None),
        P(("dp", "z", "core"), None, None),
        P(("dp", "z", "core"), None, None),
        P(),
    )
    return jax.shard_map(
        shards, mesh=split, in_specs=placed, out_specs=P(("dp", "z", "core"), None, None), check_vma=False
    )
```

time: 171 us -> 163 us (0.953); the launches traced: 169 us -> 163 us
  waiting for transfers between devices: 51.9 us -> 80.4 us
  blocking collectives: 28.4 us -> 0 us
  starting transfers between devices: 44.2 us -> 38.8 us
  Pallas kernels: 38.8 us -> 35.9 us
  between operations: 0.19 us -> 2.96 us
    all_to_all x1 -> x0, blocking collectives: 28.4 us -> none  [shards(): same = lax.all_to_all(outgoing, 'dp', 0, 0, tiled=True)]
    all_to_all x0 -> x1, waiting for transfers between devices: none -> 24.5 us  [shards(): received = lax.all_to_all(outgoing, ('dp', 'core'), 0, 0, tiled=True)]
    ppermute x21 -> x20, starting transfers between devices: 44.2 us -> 28.9 us  [send(): return lax.ppermute(value, ('dp', 'z', 'core'), routes(move))]
    all_to_all x0 -> x1, starting transfers between devices: none -> 9.9 us  [shards(): received = lax.all_to_all(outgoing, ('dp', 'core'), 0, 0, tiled=True)]
    ppermute x21 -> x20, waiting for transfers between devices: 51.9 us -> 55.9 us  [send(): return lax.ppermute(value, ('dp', 'z', 'core'), routes(move))]
    pallas_call x10, Pallas kernels: 38.8 us -> 35.9 us  [call(): return lambda *operands: made(*operands, *after)]
    unnamed x18 -> x12, local copies, waits for them, and re-layouts: 3.37 us -> 1.4 us
  transfers between devices with their start and end apart: 21 -> 21, of which waited for: 9 -> 15; matrix products, arithmetic and copies ran while one was open for 1% -> 2% of each run, Pallas kernels for 13% -> 12%
where the time goes in v4:
time: 163 us
  waiting for transfers between devices  80.4 us (49%)
  starting transfers between devices  38.8 us (24%)
  Pallas kernels  35.9 us (22%)
  local copies, waits for them, and re-layouts  3.11 us (2%)
  between operations  2.96 us (2%)
    ppermute x20, waiting for transfers between devices, send(): return lax.ppermute(value, ('dp', 'z', 'core'), routes(move))  55.9 us
    pallas_call x10, Pallas kernels, call(): return lambda *operands: made(*operands, *after)  35.9 us
    ppermute x20, starting transfers between devices, send(): return lax.ppermute(value, ('dp', 'z', 'core'), routes(move))  28.9 us
    all_to_all x1, waiting for transfers between devices, shards(): received = lax.all_to_all(outgoing, ('dp', 'core'), 0, 0, tiled=True)  24.5 us
    all_to_all x1, starting transfers between devices, shards(): received = lax.all_to_all(outgoing, ('dp', 'core'), 0, 0, tiled=True)  9.9 us
  transfers between devices with their start and end apart: 21, of which 15 were waited for; matrix products, arithmetic and copies ran while one was open for 2% of the time, Pallas kernels for 12%

profile of v4, /device:TPU:1, one launch (start us, length us, event | category | flops | bytes accessed | tf_op | source)
XLA Modules:
  0.0 162.7 jit_solution(12160153475951667127)
XLA Ops:
  0.1 3.6 %shard_map.55 = (bf16[2,3,4,16,2048]{4,3,2,1,0:T(8,128)(2,1)S(1)}, bf16[2,3,4,16,2048]{4,3,2,1,0:T(8,128)(2,1)S(1)}) custom-call(s32[3]{0:T(128)S(1)} %pad_add_fusion.2.ids, bf16[3,16,2,16,4096]{4,3,2,1,0:T(8,128)(2,1)} %bitcast.10, bf16[3,16,2,16,4096]{4,3,2,1,0:T(8,128)(2,1)} %bitcast.11, bf16[3,16,2,16,4096]{4,3,2,1,0:T(8,128)(2,1)} %bitcast.12, ...), custom_call_target="tpu_custom_call" | custom-call | flops 1 | bytes 4 | tf_op jit(solution)/shard_map/pallas_call | solution.py:67
  3.7 3.6 %collective-permute-start.1 = (bf16[2,3,4,16,2048]{4,3,2,1,0:T(8,128)(2,1)S(1)}, bf16[2,3,4,16,2048]{4,3,2,1,0:T(8,128)(2,1)S(1)}, u32[]{:S(2)}, u32[]{:S(2)}) collective-permute-start(bf16[2,3,4,16,2048]{4,3,2,1,0:T(8,128)(2,1)S(1)} %get-tuple-element.24), channel_id=1, source_target_pairs={{0,96},{1,25},{2,98},{3,27},{4,100},{5,29},{6,102},{7,31},{8,104},... | collective-permute-start | bytes 4718600 | tf_op jit(solution)/shard_map/ppermute | solution.py:40
  7.3 3.6 %shard_map.56 = (bf16[2,3,4,16,2048]{4,3,2,1,0:T(8,128)(2,1)S(1)}, bf16[2,3,4,16,2048]{4,3,2,1,0:T(8,128)(2,1)S(1)}) custom-call(s32[3]{0:T(128)S(1)} %pad_add_fusion.2.ids, bf16[3,16,2,16,4096]{4,3,2,1,0:T(8,128)(2,1)} %bitcast.14, bf16[3,16,2,16,4096]{4,3,2,1,0:T(8,128)(2,1)} %bitcast.15, bf16[3,16,2,16,4096]{4,3,2,1,0:T(8,128)(2,1)} %bitcast.16, ...), custom_call_target="tpu_custom_call" | custom-call | flops 1 | bytes 4 | tf_op jit(solution)/shard_map/pallas_call | solution.py:67
  10.9 2.7 %collective-permute-start.5 = (bf16[2,3,4,16,2048]{4,3,2,1,0:T(8,128)(2,1)S(1)}, bf16[2,3,4,16,2048]{4,3,2,1,0:T(8,128)(2,1)S(1)}, u32[]{:S(2)}, u32[]{:S(2)}) collective-permute-start(bf16[2,3,4,16,2048]{4,3,2,1,0:T(8,128)(2,1)S(1)} %get-tuple-element.28), channel_id=1, source_target_pairs={{0,96},{1,25},{2,98},{3,27},{4,100},{5,29},{6,102},{7,31},{8,104},... | collective-permute-start | bytes 4718600 | tf_op jit(solution)/shard_map/ppermute | solution.py:40
  13.7 11.0 %collective-permute-done.1.refs_3_.refs_2_ = bf16[2,3,4,16,2048]{4,3,2,1,0:T(8,128)(2,1)S(1)} collective-permute-done((bf16[2,3,4,16,2048]{4,3,2,1,0:T(8,128)(2,1)S(1)}, bf16[2,3,4,16,2048]{4,3,2,1,0:T(8,128)(2,1)S(1)}, u32[]{:S(2)}, u32[]{:S(2)}) %collective-permute-start.1) | collective-permute-done | bytes 1572896 | tf_op jit(solution)/shard_map/ppermute | solution.py:40
  24.7 3.4 %collective-permute-done.refs_2_.refs_1_ = bf16[2,3,4,16,2048]{4,3,2,1,0:T(8,128)(2,1)S(1)} collective-permute-done((bf16[2,3,4,16,2048]{4,3,2,1,0:T(8,128)(2,1)S(1)}, bf16[2,3,4,16,2048]{4,3,2,1,0:T(8,128)(2,1)S(1)}, u32[]{:S(2)}, u32[]{:S(2)}) %collective-permute-start) | collective-permute-done | bytes 1572896 | tf_op jit(solution)/shard_map/ppermute | solution.py:40
  28.1 3.2 %shard_map.57 = (bf16[3,4,16,2048]{3,2,1,0:T(8,128)(2,1)S(1)}, bf16[3,4,16,2048]{3,2,1,0:T(8,128)(2,1)S(1)}) custom-call(s32[3]{0:T(128)S(1)} %pad_add_fusion.2.ids, bf16[3,16,2,16,4096]{4,3,2,1,0:T(8,128)(2,1)} %bitcast.18, bf16[3,16,2,16,4096]{4,3,2,1,0:T(8,128)(2,1)} %bitcast.19, bf16[2,3,4,16,2048]{4,3,2,1,0:T(8,128)(2,1)S(1)} %collective-permute-done.refs_2_.refs_1_, ...), custom_call_target="tpu_custom_call" | custom-call | flops 1 | bytes 4 | tf_op jit(solution)/shard_map/pallas_call | solution.py:67
  31.4 1.5 collective-permute-start.3
  32.9 8.7 %collective-permute-done.5.refs_3_.refs_2_ = bf16[2,3,4,16,2048]{4,3,2,1,0:T(8,128)(2,1)S(1)} collective-permute-done((bf16[2,3,4,16,2048]{4,3,2,1,0:T(8,128)(2,1)S(1)}, bf16[2,3,4,16,2048]{4,3,2,1,0:T(8,128)(2,1)S(1)}, u32[]{:S(2)}, u32[]{:S(2)}) %collective-permute-start.5) | collective-permute-done | bytes 1572896 | tf_op jit(solution)/shard_map/ppermute | solution.py:40
  41.5 3.4 %collective-permute-done.4.refs_2_.refs_1_ = bf16[2,3,4,16,2048]{4,3,2,1,0:T(8,128)(2,1)S(1)} collective-permute-done((bf16[2,3,4,16,2048]{4,3,2,1,0:T(8,128)(2,1)S(1)}, bf16[2,3,4,16,2048]{4,3,2,1,0:T(8,128)(2,1)S(1)}, u32[]{:S(2)}, u32[]{:S(2)}) %collective-permute-start.4) | collective-permute-done | bytes 1572896 | tf_op jit(solution)/shard_map/ppermute | solution.py:40
  44.9 3.2 %shard_map.58 = (bf16[3,4,16,2048]{3,2,1,0:T(8,128)(2,1)S(1)}, bf16[3,4,16,2048]{3,2,1,0:T(8,128)(2,1)S(1)}) custom-call(s32[3]{0:T(128)S(1)} %pad_add_fusion.2.ids, bf16[3,16,2,16,4096]{4,3,2,1,0:T(8,128)(2,1)} %bitcast.20, bf16[3,16,2,16,4096]{4,3,2,1,0:T(8,128)(2,1)} %bitcast.21, bf16[2,3,4,16,2048]{4,3,2,1,0:T(8,128)(2,1)S(1)} %collective-permute-done.4.refs_2_.refs_1_, ...), custom_call_target="tpu_custom_call" | custom-call | flops 1 | bytes 4 | tf_op jit(solution)/shard_map/pallas_call | solution.py:67
  48.3 1.5 collective-permute-start.10
  50.0 3.4 %collective-permute-done.3.refs_4_ = bf16[3,4,16,2048]{3,2,1,0:T(8,128)(2,1)S(1)} collective-permute-done((bf16[3,4,16,2048]{3,2,1,0:T(8,128)(2,1)S(1)}, bf16[3,4,16,2048]{3,2,1,0:T(8,128)(2,1)S(1)}, u32[]{:S(2)}, u32[]{:S(2)}) %collective-permute-start.3) | collective-permute-done | bytes 786464 | tf_op jit(solution)/shard_map/ppermute | solution.py:40
  53.4 3.7 %shard_map.59 = (bf16[3,16,4096]{2,1,0:T(8,128)(2,1)S(1)}, bf16[3,16,4096]{2,1,0:T(8,128)(2,1)S(1)}, bf16[3,16,4096]{2,1,0:T(8,128)(2,1)S(1)}, bf16[3,16,4096]{2,1,0:T(8,128)(2,1)S(1)}) custom-call(s32[3]{0:T(128)S(1)} %pad_add_fusion.2.ids, bf16[3,16,2,16,4096]{4,3,2,1,0:T(8,128)(2,1)} %bitcast.22, ...), custom_call_target="tpu_custom_call" | custom-call | flops 1 | bytes 4 | tf_op jit(solution)/shard_map/pallas_call | solution.py:67
  57.1 2.5 %collective-permute-start.6 = (bf16[3,16,4096]{2,1,0:T(8,128)(2,1)S(1)}, bf16[3,16,4096]{2,1,0:T(8,128)(2,1)S(1)}, u32[]{:S(2)}, u32[]{:S(2)}) collective-permute-start(bf16[3,16,4096]{2,1,0:T(8,128)(2,1)S(1)} %get-tuple-element.31), channel_id=1, source_target_pairs={{0,24},{1,97},{2,26},{3,99},{4,28},{5,101},{6,30},{7,103},{8,0},{9... | collective-permute-start | bytes 1179656 | tf_op jit(solution)/shard_map/ppermute | solution.py:40
  61.8 3.7 %shard_map.60 = (bf16[3,16,4096]{2,1,0:T(8,128)(2,1)S(1)}, bf16[3,16,4096]{2,1,0:T(8,128)(2,1)S(1)}, bf16[3,16,4096]{2,1,0:T(8,128)(2,1)S(1)}, bf16[3,16,4096]{2,1,0:T(8,128)(2,1)S(1)}) custom-call(s32[3]{0:T(128)S(1)} %pad_add_fusion.2.ids, bf16[3,16,2,16,4096]{4,3,2,1,0:T(8,128)(2,1)} %bitcast.23, ...), custom_call_target="tpu_custom_call" | custom-call | flops 1 | bytes 4 | tf_op jit(solution)/shard_map/pallas_call | solution.py:67
  65.5 2.3 %collective-permute-start.14 = (bf16[3,16,4096]{2,1,0:T(8,128)(2,1)S(1)}, bf16[3,16,4096]{2,1,0:T(8,128)(2,1)S(1)}, u32[]{:S(2)}, u32[]{:S(2)}) collective-permute-start(bf16[3,16,4096]{2,1,0:T(8,128)(2,1)S(1)} %get-tuple-element.37), channel_id=1, source_target_pairs={{0,24},{1,97},{2,26},{3,99},{4,28},{5,101},{6,30},{7,103},{8,0},{9... | collective-permute-start | bytes 1179656 | tf_op jit(solution)/shard_map/ppermute | solution.py:40
  67.8 1.7 %collective-permute-start.16 = (bf16[3,16,4096]{2,1,0:T(8,128)(2,1)S(1)}, bf16[3,16,4096]{2,1,0:T(8,128)(2,1)S(1)}, u32[]{:S(2)}, u32[]{:S(2)}) collective-permute-start(bf16[3,16,4096]{2,1,0:T(8,128)(2,1)S(1)} %get-tuple-element.39), channel_id=1, source_target_pairs={{0,16},{1,65},{2,18},{3,67},{4,20},{5,69},{6,22},{7,71},{8,24},{9,... | collective-permute-start | bytes 1179656 | tf_op jit(solution)/shard_map/ppermute | solution.py:40
  69.5 2.5 %collective-permute-done.7.refs_2_ = bf16[3,16,4096]{2,1,0:T(8,128)(2,1)S(1)} collective-permute-done((bf16[3,16,4096]{2,1,0:T(8,128)(2,1)S(1)}, bf16[3,16,4096]{2,1,0:T(8,128)(2,1)S(1)}, u32[]{:S(2)}, u32[]{:S(2)}) %collective-permute-start.7) | collective-permute-done | bytes 393248 | tf_op jit(solution)/shard_map/ppermute | solution.py:40
  73.2 1.7 %collective-permute-start.13 = (bf16[96,16,128]{2,1,0:T(8,128)(2,1)S(1)}, bf16[96,16,128]{2,1,0:T(8,128)(2,1)S(1)}, u32[]{:S(2)}, u32[]{:S(2)}) collective-permute-start(bf16[96,16,128]{2,1,0:T(8,128)(2,1)S(1)} %get-tuple-element.36.refs_6_.refs_0_), channel_id=1, source_target_pairs={{0,2},{1,3},{2,4},{3,5},{4,6},{5,7},{6,0},{7,1},{8,10},{9,11},{10,... | collective-permute-start | bytes 1179656 | tf_op jit(solution)/shard_map/ppermute | solution.py:40
  74.9 3.3 %collective-permute-start.12 = (bf16[96,16,128]{2,1,0:T(8,128)(2,1)S(1)}, bf16[96,16,128]{2,1,0:T(8,128)(2,1)S(1)}, u32[]{:S(2)}, u32[]{:S(2)}) collective-permute-start(bf16[96,16,128]{2,1,0:T(8,128)(2,1)S(1)} %get-tuple-element.36.refs_6_.refs_0_), channel_id=1, source_target_pairs={{0,4},{1,5},{2,6},{3,7},{4,0},{5,1},{6,2},{7,3},{8,12},{9,13},{10,... | collective-permute-start | bytes 1179656 | tf_op jit(solution)/shard_map/ppermute | solution.py:40
  79.0 1.5 collective-permute-done.15.refs_2_
  81.7 1.7 %collective-permute-start.19 = (bf16[97,16,128]{2,1,0:T(8,128)(2,1)S(1)}, bf16[97,16,128]{2,1,0:T(8,128)(2,1)S(1)}, u32[]{:S(2)}, u32[]{:S(2)}) collective-permute-start(bf16[97,16,128]{2,1,0:T(8,128)(2,1)S(1)} %shard_map.62.refs_4_.refs_8_), channel_id=1, source_target_pairs={{0,2},{1,3},{2,4},{3,5},{4,6},{5,7},{6,0},{7,1},{8,10},{9,11},{10,... | collective-permute-start | bytes 1191944 | tf_op jit(solution)/shard_map/ppermute | solution.py:40
  83.4 3.3 %collective-permute-start.18 = (bf16[97,16,128]{2,1,0:T(8,128)(2,1)S(1)}, bf16[97,16,128]{2,1,0:T(8,128)(2,1)S(1)}, u32[]{:S(2)}, u32[]{:S(2)}) collective-permute-start(bf16[97,16,128]{2,1,0:T(8,128)(2,1)S(1)} %shard_map.62.refs_4_.refs_8_), channel_id=1, source_target_pairs={{0,4},{1,5},{2,6},{3,7},{4,0},{5,1},{6,2},{7,3},{8,12},{9,13},{10,... | collective-permute-start | bytes 1191944 | tf_op jit(solution)/shard_map/ppermute | solution.py:40
  88.1 3.4 %collective-permute-done.12.refs_2_ = bf16[96,16,128]{2,1,0:T(8,128)(2,1)S(1)} collective-permute-done((bf16[96,16,128]{2,1,0:T(8,128)(2,1)S(1)}, bf16[96,16,128]{2,1,0:T(8,128)(2,1)S(1)}, u32[]{:S(2)}, u32[]{:S(2)}) %collective-permute-start.12) | collective-permute-done | bytes 393248 | tf_op jit(solution)/shard_map/ppermute | solution.py:40
  91.5 1.9 %collective-permute-done.11.refs_1_ = bf16[96,16,128]{2,1,0:T(8,128)(2,1)S(1)} collective-permute-done((bf16[96,16,128]{2,1,0:T(8,128)(2,1)S(1)}, bf16[96,16,128]{2,1,0:T(8,128)(2,1)S(1)}, u32[]{:S(2)}, u32[]{:S(2)}) %collective-permute-start.11) | collective-permute-done | bytes 393248 | tf_op jit(solution)/shard_map/ppermute | solution.py:40
  93.4 10.4 %collective-permute-done.19.refs_7_ = bf16[97,16,128]{2,1,0:T(8,128)(2,1)S(1)} collective-permute-done((bf16[97,16,128]{2,1,0:T(8,128)(2,1)S(1)}, bf16[97,16,128]{2,1,0:T(8,128)(2,1)S(1)}, u32[]{:S(2)}, u32[]{:S(2)}) %collective-permute-start.19) | collective-permute-done | bytes 397344 | tf_op jit(solution)/shard_map/ppermute | solution.py:40
  103.8 4.7 %collective-permute-done.18.refs_6_ = bf16[97,16,128]{2,1,0:T(8,128)(2,1)S(1)} collective-permute-done((bf16[97,16,128]{2,1,0:T(8,128)(2,1)S(1)}, bf16[97,16,128]{2,1,0:T(8,128)(2,1)S(1)}, u32[]{:S(2)}, u32[]{:S(2)}) %collective-permute-start.18) | collective-permute-done | bytes 397344 | tf_op jit(solution)/shard_map/ppermute | solution.py:40
  109.1 3.3 %shard_map.63 = bf16[32,17,16,128]{3,2,1,0:T(8,128)(2,1)} custom-call(s32[64]{0:T(128)S(1)} %reshape.234.ids, bf16[96,16,128]{2,1,0:T(8,128)(2,1)S(1)} %get-tuple-element.36.refs_6_.refs_0_, bf16[96,16,128]{2,1,0:T(8,128)(2,1)S(1)} %collective-permute-done.11.refs_1_, bf16[96,16,128]{2,1,0:T(8,128)(2,1)S(1)} %collective-permute-done.12.refs_2_, ...), custom_call_target="tpu_custom_call" | custom-call | flops 1 | bytes 4 | tf_op jit(solution)/shard_map/pallas_call | solution.py:67
  112.4 9.9 %all-to-all-start = ((bf16[32,17,16,128]{3,2,1,0:T(8,128)(2,1)}), bf16[32,17,16,128]{3,2,1,0:T(8,128)(2,1)S(1)}, u32[]{:S(2)}, u32[]{:S(2)}) async-start(bf16[32,17,16,128]{3,2,1,0:T(8,128)(2,1)} %shard_map.63), calls=%async_computation | async-start | bytes 4456448 | tf_op jit(solution)/shard_map/all_to_all | solution.py:372
  127.5 24.5 %all-to-all-done = bf16[32,17,16,128]{3,2,1,0:T(8,128)(2,1)S(1)} async-done(((bf16[32,17,16,128]{3,2,1,0:T(8,128)(2,1)}), bf16[32,17,16,128]{3,2,1,0:T(8,128)(2,1)S(1)}, u32[]{:S(2)}, u32[]{:S(2)}) %all-to-all-start) | async-done | bytes 2228256 | tf_op jit(solution)/shard_map/all_to_all | solution.py:372
  153.4 9.1 %shard_map.64 = bf16[1,1024,1024]{2,1,0:T(8,128)(2,1)} custom-call(s32[2]{0:T(128)} %pad_add_fusion.1.ids, bf16[16,2,17,16,128]{4,3,2,1,0:T(8,128)(2,1)} %bitcast.24, bf16[1,1024,1024]{2,1,0:T(8,128)(2,1)} %refs_1_.1, bf16[1,1024,1024]{2,1,0:T(8,128)(2,1)} %refs_2_.1), custom_call_target="tpu_custom_call" | custom-call | flops 1048576 | bytes 4194304 | tf_op jit(solution)/shard_map/pallas_call | solution.py:67
  (44 shorter events, 11.8 us)
Async XLA Ops:
  3.7 21.0 %collective-permute-start.1 = (bf16[2,3,4,16,2048]{4,3,2,1,0:T(8,128)(2,1)S(1)}, bf16[2,3,4,16,2048]{4,3,2,1,0:T(8,128)(2,1)S(1)}, u32[]{:S(2)}, u32[]{:S(2)}) collective-permute-start(bf16[2,3,4,16,2048]{4,3,2,1,0:T(8,128)(2,1)S(1)} %get-tuple-element.24), channel_id=1, source_target_pairs={{0,96},{1,25},{2,98},{3,27},{4,100},{5,29},{6,102},{7,31},{8,104},... | collective-permute-start | bytes 4718600 | tf_op jit(solution)/shard_map/ppermute | solution.py:40
  7.3 20.8 %collective-permute-start = (bf16[2,3,4,16,2048]{4,3,2,1,0:T(8,128)(2,1)S(1)}, bf16[2,3,4,16,2048]{4,3,2,1,0:T(8,128)(2,1)S(1)}, u32[]{:S(2)}, u32[]{:S(2)}) collective-permute-start(bf16[2,3,4,16,2048]{4,3,2,1,0:T(8,128)(2,1)S(1)} %get-tuple-element.23.refs_4_), channel_id=1, source_target_pairs={{0,32},{1,9},{2,34},{3,11},{4,36},{5,13},{6,38},{7,15},{8,40},{9,1... | collective-permute-start | bytes 4718600 | tf_op jit(solution)/shard_map/ppermute | solution.py:40
  10.9 17.2 %copy-start.3 = (bf16[2,3,4,16,2048]{4,3,2,1,0:T(8,128)(2,1)}, bf16[2,3,4,16,2048]{4,3,2,1,0:T(8,128)(2,1)S(1)}, u32[]{:S(2)}) copy-start(bf16[2,3,4,16,2048]{4,3,2,1,0:T(8,128)(2,1)S(1)} %get-tuple-element.25.refs_4_) | copy-start | bytes 4718596
  10.9 30.6 %collective-permute-start.5 = (bf16[2,3,4,16,2048]{4,3,2,1,0:T(8,128)(2,1)S(1)}, bf16[2,3,4,16,2048]{4,3,2,1,0:T(8,128)(2,1)S(1)}, u32[]{:S(2)}, u32[]{:S(2)}) collective-permute-start(bf16[2,3,4,16,2048]{4,3,2,1,0:T(8,128)(2,1)S(1)} %get-tuple-element.28), channel_id=1, source_target_pairs={{0,96},{1,25},{2,98},{3,27},{4,100},{5,29},{6,102},{7,31},{8,104},... | collective-permute-start | bytes 4718600 | tf_op jit(solution)/shard_map/ppermute | solution.py:40
  13.7 31.3 %collective-permute-start.4 = (bf16[2,3,4,16,2048]{4,3,2,1,0:T(8,128)(2,1)S(1)}, bf16[2,3,4,16,2048]{4,3,2,1,0:T(8,128)(2,1)S(1)}, u32[]{:S(2)}, u32[]{:S(2)}) collective-permute-start(bf16[2,3,4,16,2048]{4,3,2,1,0:T(8,128)(2,1)S(1)} %get-tuple-element.25.refs_4_), channel_id=1, source_target_pairs={{0,32},{1,9},{2,34},{3,11},{4,36},{5,13},{6,38},{7,15},{8,40},{9,1... | collective-permute-start | bytes 4718600 | tf_op jit(solution)/shard_map/ppermute | solution.py:40
  24.7 6.6 %copy-start = (bf16[2,3,4,16,2048]{4,3,2,1,0:T(8,128)(2,1)}, bf16[2,3,4,16,2048]{4,3,2,1,0:T(8,128)(2,1)S(1)}, u32[]{:S(2)}) copy-start(bf16[2,3,4,16,2048]{4,3,2,1,0:T(8,128)(2,1)S(1)} %collective-permute-done.1.refs_3_.refs_2_) | copy-start | bytes 4718596
  31.3 18.6 %collective-permute-start.2 = (bf16[3,4,16,2048]{3,2,1,0:T(8,128)(2,1)S(1)}, bf16[3,4,16,2048]{3,2,1,0:T(8,128)(2,1)S(1)}, u32[]{:S(2)}, u32[]{:S(2)}) collective-permute-start(bf16[3,4,16,2048]{3,2,1,0:T(8,128)(2,1)S(1)} %get-tuple-element.26), channel_id=1, source_target_pairs={{0,96},{1,25},{2,98},{3,27},{4,100},{5,29},{6,102},{7,31},{8,104},... | collective-permute-start | bytes 2359304 | tf_op jit(solution)/shard_map/ppermute | solution.py:40
  31.4 22.0 %collective-permute-start.3 = (bf16[3,4,16,2048]{3,2,1,0:T(8,128)(2,1)S(1)}, bf16[3,4,16,2048]{3,2,1,0:T(8,128)(2,1)S(1)}, u32[]{:S(2)}, u32[]{:S(2)}) collective-permute-start(bf16[3,4,16,2048]{3,2,1,0:T(8,128)(2,1)S(1)} %get-tuple-element.27.refs_4_), channel_id=1, source_target_pairs={{0,32},{1,9},{2,34},{3,11},{4,36},{5,13},{6,38},{7,15},{8,40},{9,1... | collective-permute-start | bytes 2359304 | tf_op jit(solution)/shard_map/ppermute | solution.py:40
  41.5 6.6 %copy-start.2 = (bf16[2,3,4,16,2048]{4,3,2,1,0:T(8,128)(2,1)}, bf16[2,3,4,16,2048]{4,3,2,1,0:T(8,128)(2,1)S(1)}, u32[]{:S(2)}) copy-start(bf16[2,3,4,16,2048]{4,3,2,1,0:T(8,128)(2,1)S(1)} %collective-permute-done.5.refs_3_.refs_2_) | copy-start | bytes 4718596
  48.2 12.9 %collective-permute-start.9 = (bf16[3,4,16,2048]{3,2,1,0:T(8,128)(2,1)S(1)}, bf16[3,4,16,2048]{3,2,1,0:T(8,128)(2,1)S(1)}, u32[]{:S(2)}, u32[]{:S(2)}) collective-permute-start(bf16[3,4,16,2048]{3,2,1,0:T(8,128)(2,1)S(1)} %get-tuple-element.34), channel_id=1, source_target_pairs={{0,96},{1,25},{2,98},{3,27},{4,100},{5,29},{6,102},{7,31},{8,104},... | collective-permute-start | bytes 2359304 | tf_op jit(solution)/shard_map/ppermute | solution.py:40
  48.3 13.5 %collective-permute-start.10 = (bf16[3,4,16,2048]{3,2,1,0:T(8,128)(2,1)S(1)}, bf16[3,4,16,2048]{3,2,1,0:T(8,128)(2,1)S(1)}, u32[]{:S(2)}, u32[]{:S(2)}) collective-permute-start(bf16[3,4,16,2048]{3,2,1,0:T(8,128)(2,1)S(1)} %get-tuple-element.29.refs_5_), channel_id=1, source_target_pairs={{0,32},{1,9},{2,34},{3,11},{4,36},{5,13},{6,38},{7,15},{8,40},{9,1... | collective-permute-start | bytes 2359304 | tf_op jit(solution)/shard_map/ppermute | solution.py:40
  57.1 10.7 %collective-permute-start.6 = (bf16[3,16,4096]{2,1,0:T(8,128)(2,1)S(1)}, bf16[3,16,4096]{2,1,0:T(8,128)(2,1)S(1)}, u32[]{:S(2)}, u32[]{:S(2)}) collective-permute-start(bf16[3,16,4096]{2,1,0:T(8,128)(2,1)S(1)} %get-tuple-element.31), channel_id=1, source_target_pairs={{0,24},{1,97},{2,26},{3,99},{4,28},{5,101},{6,30},{7,103},{8,0},{9... | collective-permute-start | bytes 1179656 | tf_op jit(solution)/shard_map/ppermute | solution.py:40
  59.6 12.3 %collective-permute-start.7 = (bf16[3,16,4096]{2,1,0:T(8,128)(2,1)S(1)}, bf16[3,16,4096]{2,1,0:T(8,128)(2,1)S(1)}, u32[]{:S(2)}, u32[]{:S(2)}) collective-permute-start(bf16[3,16,4096]{2,1,0:T(8,128)(2,1)S(1)} %get-tuple-element.32), channel_id=1, source_target_pairs={{0,8},{1,33},{2,10},{3,35},{4,12},{5,37},{6,14},{7,39},{8,16},{9,4... | collective-permute-start | bytes 1179656 | tf_op jit(solution)/shard_map/ppermute | solution.py:40
  59.6 12.3 %collective-permute-start.8 = (bf16[3,16,4096]{2,1,0:T(8,128)(2,1)S(1)}, bf16[3,16,4096]{2,1,0:T(8,128)(2,1)S(1)}, u32[]{:S(2)}, u32[]{:S(2)}) collective-permute-start(bf16[3,16,4096]{2,1,0:T(8,128)(2,1)S(1)} %get-tuple-element.33), channel_id=1, source_target_pairs={{0,16},{1,65},{2,18},{3,67},{4,20},{5,69},{6,22},{7,71},{8,24},{9,... | collective-permute-start | bytes 1179656 | tf_op jit(solution)/shard_map/ppermute | solution.py:40
  61.8 10.2 %copy-start.1 = (f32[3,32,4096]{2,1,0:T(8,128)S(1)}, f32[3,32,4096]{2,1,0:T(8,128)}, u32[]{:S(2)}) copy-start(f32[3,32,4096]{2,1,0:T(8,128)} %param.6) | copy-start | bytes 4718596
  65.5 12.7 %collective-permute-start.14 = (bf16[3,16,4096]{2,1,0:T(8,128)(2,1)S(1)}, bf16[3,16,4096]{2,1,0:T(8,128)(2,1)S(1)}, u32[]{:S(2)}, u32[]{:S(2)}) collective-permute-start(bf16[3,16,4096]{2,1,0:T(8,128)(2,1)S(1)} %get-tuple-element.37), channel_id=1, source_target_pairs={{0,24},{1,97},{2,26},{3,99},{4,28},{5,101},{6,30},{7,103},{8,0},{9... | collective-permute-start | bytes 1179656 | tf_op jit(solution)/shard_map/ppermute | solution.py:40
  67.8 12.6 %collective-permute-start.15 = (bf16[3,16,4096]{2,1,0:T(8,128)(2,1)S(1)}, bf16[3,16,4096]{2,1,0:T(8,128)(2,1)S(1)}, u32[]{:S(2)}, u32[]{:S(2)}) collective-permute-start(bf16[3,16,4096]{2,1,0:T(8,128)(2,1)S(1)} %get-tuple-element.38), channel_id=1, source_target_pairs={{0,8},{1,33},{2,10},{3,35},{4,12},{5,37},{6,14},{7,39},{8,16},{9,4... | collective-permute-start | bytes 1179656 | tf_op jit(solution)/shard_map/ppermute | solution.py:40
  67.8 12.6 %collective-permute-start.16 = (bf16[3,16,4096]{2,1,0:T(8,128)(2,1)S(1)}, bf16[3,16,4096]{2,1,0:T(8,128)(2,1)S(1)}, u32[]{:S(2)}, u32[]{:S(2)}) collective-permute-start(bf16[3,16,4096]{2,1,0:T(8,128)(2,1)S(1)} %get-tuple-element.39), channel_id=1, source_target_pairs={{0,16},{1,65},{2,18},{3,67},{4,20},{5,69},{6,22},{7,71},{8,24},{9,... | collective-permute-start | bytes 1179656 | tf_op jit(solution)/shard_map/ppermute | solution.py:40
  73.2 13.5 %collective-permute-start.13 = (bf16[96,16,128]{2,1,0:T(8,128)(2,1)S(1)}, bf16[96,16,128]{2,1,0:T(8,128)(2,1)S(1)}, u32[]{:S(2)}, u32[]{:S(2)}) collective-permute-start(bf16[96,16,128]{2,1,0:T(8,128)(2,1)S(1)} %get-tuple-element.36.refs_6_.refs_0_), channel_id=1, source_target_pairs={{0,2},{1,3},{2,4},{3,5},{4,6},{5,7},{6,0},{7,1},{8,10},{9,11},{10,... | collective-permute-start | bytes 1179656 | tf_op jit(solution)/shard_map/ppermute | solution.py:40
  74.9 16.5 %collective-permute-start.12 = (bf16[96,16,128]{2,1,0:T(8,128)(2,1)S(1)}, bf16[96,16,128]{2,1,0:T(8,128)(2,1)S(1)}, u32[]{:S(2)}, u32[]{:S(2)}) collective-permute-start(bf16[96,16,128]{2,1,0:T(8,128)(2,1)S(1)} %get-tuple-element.36.refs_6_.refs_0_), channel_id=1, source_target_pairs={{0,4},{1,5},{2,6},{3,7},{4,0},{5,1},{6,2},{7,3},{8,12},{9,13},{10,... | collective-permute-start | bytes 1179656 | tf_op jit(solution)/shard_map/ppermute | solution.py:40
  78.2 15.2 %collective-permute-start.11 = (bf16[96,16,128]{2,1,0:T(8,128)(2,1)S(1)}, bf16[96,16,128]{2,1,0:T(8,128)(2,1)S(1)}, u32[]{:S(2)}, u32[]{:S(2)}) collective-permute-start(bf16[96,16,128]{2,1,0:T(8,128)(2,1)S(1)} %get-tuple-element.36.refs_6_.refs_0_), channel_id=1, source_target_pairs={{0,6},{1,7},{2,0},{3,1},{4,2},{5,3},{6,4},{7,5},{8,14},{9,15},{10,... | collective-permute-start | bytes 1179656 | tf_op jit(solution)/shard_map/ppermute | solution.py:40
  80.4 7.0 %copy-start.5 = (s32[48]{0:T(128)S(1)}, s32[48]{0:T(128)}, u32[]{:S(2)}) copy-start(s32[48]{0:T(128)} %param.9) | copy-start | bytes 580
  81.7 22.1 %collective-permute-start.19 = (bf16[97,16,128]{2,1,0:T(8,128)(2,1)S(1)}, bf16[97,16,128]{2,1,0:T(8,128)(2,1)S(1)}, u32[]{:S(2)}, u32[]{:S(2)}) collective-permute-start(bf16[97,16,128]{2,1,0:T(8,128)(2,1)S(1)} %shard_map.62.refs_4_.refs_8_), channel_id=1, source_target_pairs={{0,2},{1,3},{2,4},{3,5},{4,6},{5,7},{6,0},{7,1},{8,10},{9,11},{10,... | collective-permute-start | bytes 1191944 | tf_op jit(solution)/shard_map/ppermute | solution.py:40
  83.4 25.1 %collective-permute-start.18 = (bf16[97,16,128]{2,1,0:T(8,128)(2,1)S(1)}, bf16[97,16,128]{2,1,0:T(8,128)(2,1)S(1)}, u32[]{:S(2)}, u32[]{:S(2)}) collective-permute-start(bf16[97,16,128]{2,1,0:T(8,128)(2,1)S(1)} %shard_map.62.refs_4_.refs_8_), channel_id=1, source_target_pairs={{0,4},{1,5},{2,6},{3,7},{4,0},{5,1},{6,2},{7,3},{8,12},{9,13},{10,... | collective-permute-start | bytes 1191944 | tf_op jit(solution)/shard_map/ppermute | solution.py:40
  86.7 22.4 %collective-permute-start.17 = (bf16[97,16,128]{2,1,0:T(8,128)(2,1)S(1)}, bf16[97,16,128]{2,1,0:T(8,128)(2,1)S(1)}, u32[]{:S(2)}, u32[]{:S(2)}) collective-permute-start(bf16[97,16,128]{2,1,0:T(8,128)(2,1)S(1)} %shard_map.62.refs_4_.refs_8_), channel_id=1, source_target_pairs={{0,6},{1,7},{2,0},{3,1},{4,2},{5,3},{6,4},{7,5},{8,14},{9,15},{10,... | collective-permute-start | bytes 1191944 | tf_op jit(solution)/shard_map/ppermute | solution.py:40
  112.4 39.6 %all-to-all-start = ((bf16[32,17,16,128]{3,2,1,0:T(8,128)(2,1)}), bf16[32,17,16,128]{3,2,1,0:T(8,128)(2,1)S(1)}, u32[]{:S(2)}, u32[]{:S(2)}) async-start(bf16[32,17,16,128]{3,2,1,0:T(8,128)(2,1)} %shard_map.63), calls=%async_computation | async-start | bytes 4456448 | tf_op jit(solution)/shard_map/all_to_all | solution.py:372
  152.0 1.4 copy-start.4

commit v5 on v4

--- a/solution.py
+++ b/solution.py
@@ -1,5 +1,3 @@
-import functools
-
 import jax
 import jax.numpy as jnp
 from jax import lax
@@ -15,7 +13,7 @@
 LANES = 128
 PIECES = 12
 VMEM_LIMIT = 12 * 1024 * 1024
-VMEM_MOST = 48 * 1024 * 1024
+VMEM_MOST = 20 * 1024 * 1024
 F32 = jnp.float32
 BF16 = jnp.bfloat16
 
@@ -48,6 +46,10 @@
     return value.astype(F32)
 
 
+def in_vmem(value):
+    return pltpu.with_memory_space_constraint(value, pltpu.VMEM)
+
+
 def call(kernel, out_shape, grid, in_specs, out_specs, scratch=(), cost=1, after=(), grant=VMEM_MOST):
     inputs = len(in_specs)
     in_specs = list(in_specs) + [pl.BlockSpec(memory_space=pl.ANY)] * len(after)
@@ -72,62 +74,63 @@
     return jnp.where(ids[2] == 0, j * SIDE + q, q * SIDE + j)
 
 
-def grads_spec(m, rows, half, chunk, offset, column, ahead=0):
-    def index(t, ids):
-        q = t if not ahead else lax.rem(ids[1] + ahead + t, SIDE)
-        return 0, row_block(ids, ids[0] + offset, q), chunk, 0, column
-
-    return pl.BlockSpec((m, 1, 1, rows, half), index)
-
-
 def extract(ids, parts, chunk, pieces, after):
     m, _, _, rows, width = parts.shape
     half = width // 2
     count = len(pieces) // 2
 
-    def kernel(ids, *refs):
-        sources, (up, down) = refs[: 2 * count], refs[2 * count :]
-        for k in range(count):
-            up[k, :, 0] = sources[k][:, 0, 0]
-            down[k, :, 0] = sources[count + k][:, 0, 0]
-
-    out = jax.ShapeDtypeStruct((count, m, SIDE, rows, half), BF16)
-    out_spec = pl.BlockSpec((count, m, 1, rows, half), lambda t, ids: (0, 0, t, 0, 0))
-    return call(
-        kernel,
-        [out, out],
+    def kernel(ids, source, up, down, sem):
+        copies = []
+        for number, (offset, column) in enumerate(pieces):
+            out, part = (up, down)[number // count], number % count
+            for q in range(SIDE):
+                block = row_block(ids, ids[0] + offset, q)
+                place = source.at[:, block, chunk, :, pl.ds(column * half, half)]
+                copies.append(pltpu.make_async_copy(place, out.at[part, :, q], sem.at[number, q]))
+        for copy in copies:
+            copy.start()
+        for copy in copies:
+            copy.wait()
+
+    here = pl.BlockSpec(memory_space=pltpu.VMEM)
+    return call(
+        kernel,
+        [pltpu.VMEM((count, m, SIDE, rows, half), BF16)] * 2,
+        (1,),
+        [pl.BlockSpec(memory_space=pl.ANY)],
+        [here, here],
+        [pltpu.SemaphoreType.DMA((2 * count, SIDE))],
+        after=after,
+    )(ids, parts)
+
+
+def relay(ids, own_up, own_down, from_up, from_down, after):
+    _, m, _, rows, half = own_up.shape
+
+    def kernel(ids, a, b, below, above, up, down):
+        q = pl.program_id(0)
+        up[:, q] = (wide(a[0, :, q]) + wide(below[0, :, q])).astype(BF16)
+        down[:, q] = (wide(b[0, :, q]) + wide(above[0, :, q])).astype(BF16)
+
+    here = pl.BlockSpec(memory_space=pltpu.VMEM)
+    return call(
+        kernel,
+        [pltpu.VMEM((m, SIDE, rows, half), BF16)] * 2,
         (SIDE,),
-        [grads_spec(m, rows, half, chunk, *piece) for piece in pieces],
-        [out_spec, out_spec],
-        after=after,
-    )(ids, *([parts] * len(pieces)))
-
-
-def relay(ids, parts, from_up, from_down, chunk, after):
-    m, _, _, rows, width = parts.shape
-    half = width // 2
-
-    def kernel(ids, a, b, below, above, up, down):
-        up[:, 0] = (wide(a[:, 0, 0]) + wide(below[0, :, 0])).astype(BF16)
-        down[:, 0] = (wide(b[:, 0, 0]) + wide(above[0, :, 0])).astype(BF16)
-
-    spec = functools.partial(grads_spec, m, rows, half, chunk)
-    out = jax.ShapeDtypeStruct((m, SIDE, rows, half), BF16)
-    out_spec = pl.BlockSpec((m, 1, rows, half), lambda t, ids: (0, t, 0, 0))
-    got = pl.BlockSpec((1, m, 1, rows, half), lambda t, ids: (0, 0, t, 0, 0))
-    return call(
-        kernel, [out, out], (SIDE,), [spec(1, 1), spec(-1, 0), got, got], [out_spec, out_spec], after=after
-    )(ids, parts, parts, from_down, from_up)
-
-
-def first_sum(ids, parts, from_up, from_down, late_up, late_down, chunk, after):
-    m, _, _, rows, width = parts.shape
-    half = width // 2
-
-    def kernel(ids, own, below, above, late_above, late_below, mine, *others):
+        [here] * 4,
+        [here, here],
+        after=after,
+    )(ids, *(in_vmem(value) for value in (own_up, own_down, from_down, from_up)))
+
+
+def first_sum(ids, own_up, own_down, from_up, from_down, late_up, late_down, after):
+    _, m, _, rows, half = own_up.shape
+
+    def kernel(ids, own_left, own_right, below, above, late_above, late_below, mine, *others):
         t = pl.program_id(0)
-        left = (wide(own[:, 0, 0, :, :half]) + wide(below[0, :, 0]) + wide(late_above[:, 0])).astype(BF16)
-        right = (wide(own[:, 0, 0, :, half:]) + wide(above[0, :, 0]) + wide(late_below[:, 0])).astype(BF16)
+        q = lax.rem(ids[1] + 1 + t, SIDE)
+        left = (wide(own_left[1, :, q]) + wide(below[1, :, q]) + wide(late_above[:, q])).astype(BF16)
+        right = (wide(own_right[1, :, q]) + wide(above[1, :, q]) + wide(late_below[:, q])).astype(BF16)
         for number, out in enumerate((*others, mine)):
 
             @pl.when(t == number)
@@ -135,21 +138,15 @@
                 out[:, :, :half] = left
                 out[:, :, half:] = right
 
-    def at(t, ids):
-        return lax.rem(ids[1] + 1 + t, SIDE)
-
-    raw = from_up.shape[0] - 1
-    got = pl.BlockSpec((1, m, 1, rows, half), lambda t, ids: (raw, 0, at(t, ids), 0, 0))
-    late = pl.BlockSpec((m, 1, rows, half), lambda t, ids: (0, at(t, ids), 0, 0))
-    whole = pl.BlockSpec((m, rows, width), lambda t, ids: (0, 0, 0))
-    return call(
-        kernel,
-        [jax.ShapeDtypeStruct((m, rows, width), BF16)] * SIDE,
+    here = pl.BlockSpec(memory_space=pltpu.VMEM)
+    return call(
+        kernel,
+        [pltpu.VMEM((m, rows, 2 * half), BF16)] * SIDE,
         (SIDE,),
-        [grads_spec(m, rows, width, chunk, 0, 0, ahead=1), got, got, late, late],
-        [whole] * SIDE,
-        after=after,
-    )(ids, parts, from_down, from_up, late_up, late_down)
+        [here] * 6,
+        [here] * SIDE,
+        after=after,
+    )(ids, *(in_vmem(value) for value in (own_up, own_down, from_down, from_up, late_up, late_down)))
 
 
 def second_sum(ids, sums, moment, chunk, block, earlier, after):
@@ -211,34 +208,33 @@
     count = len(held[0])
     total, rows, _ = held[0][0].shape
     tiles = total // PIECES
+    steps = 4
 
     def kernel(picks, *refs):
         first, second, out = refs[:count], refs[count : 2 * count], refs[2 * count]
 
-        @pl.loop(0, slots)
-        def _(slot):
+        @pl.loop(0, slots // steps)
+        def _(k):
+            slot = pl.program_id(0) * (slots // steps) + k
             piece = pl.ds(picks[2 * slot + 1] * tiles, tiles)
             for number in range(count):
 
                 @pl.when(picks[2 * slot] == number)
                 def _(number=number):
-                    out[slot, :tiles] = first[number][piece]
-                    out[slot, tiles : 2 * tiles] = second[number][piece]
-                    out[slot, 2 * tiles] = second[number][total]
-
-    def whole(shape):
-        return pl.BlockSpec(shape, lambda t, ids: (0,) * len(shape))
+                    out[k, :tiles] = first[number][piece]
+                    out[k, tiles : 2 * tiles] = second[number][piece]
+                    out[k, 2 * tiles] = second[number][total]
 
     shape = (slots, 2 * tiles + 1, rows, LANES)
     return call(
         kernel,
         jax.ShapeDtypeStruct(shape, BF16),
-        (1,),
-        [whole(v.shape) for v in (*held[0], *held[1])],
-        whole(shape),
+        (steps,),
+        [pl.BlockSpec(memory_space=pltpu.VMEM)] * (2 * count),
+        pl.BlockSpec((slots // steps,) + shape[1:], lambda t, ids: (t, 0, 0, 0)),
         after=after,
         grant=VMEM_LIMIT,
-    )(picks, *held[0], *held[1])
+    )(picks, *(in_vmem(value) for value in (*held[0], *held[1])))
 
 
 def finish(ids, received, left_root, right_root, block):
@@ -246,33 +242,34 @@
     tiles = block // LANES
     step = block // 2
 
-    def kernel(ids, received, left, right, out, landed, grads, lefts, rights, shaped, results, sem):
-        get = pltpu.make_async_copy(received, landed, sem.at[0])
-        get_left = pltpu.make_async_copy(left.at[0], lefts, sem.at[1])
+    def kernel(ids, received, left, right, out, grads, lefts, rights, shaped, results, sem):
+        get_lefts = [
+            pltpu.make_async_copy(left.at[0, pl.ds(at, step)], lefts.at[pl.ds(at, step)], sem.at[at // step])
+            for at in range(0, block, step)
+        ]
         get_right = pltpu.make_async_copy(right.at[0], rights, sem.at[2])
-        get.start()
-        get_left.start()
+        get_lefts[0].start()
         get_right.start()
-        get.wait()
+        get_lefts[1].start()
 
         @pl.loop(0, dp_count)
         def _(group):
             for core in range(2):
                 for tile in range(2 * tiles):
                     columns = slice(tile % tiles * LANES, (tile % tiles + 1) * LANES)
-                    grads[core, group, tile // tiles, :, columns] = landed[group, core, tile]
-
-        get_left.wait()
+                    grads[core, group, tile // tiles, :, columns] = received[group, core, tile]
+
         total = jnp.zeros((8, block), F32)
         for at in range(0, block, step):
             whole = grads[...].reshape(block, block)
+            get_lefts[at // step].wait()
             first = jnp.dot(lefts[at : at + step, :], whole, preferred_element_type=F32).astype(BF16)
             if at == 0:
                 get_right.wait()
             value = jnp.dot(first, rights[...], preferred_element_type=F32)
             shaped[at : at + step, :] = value
             total = total + jnp.sum((value * value).reshape(step // 8, 8, block), axis=0)
-        powers = wide(landed[:, :, 2 * tiles])
+        powers = wide(received[:, :, 2 * tiles])
         row = lax.broadcasted_iota(jnp.int32, powers.shape, 2)
         power = jnp.sum(jnp.where(row == ids[1], powers, 0.0).reshape(-1, 8, LANES), axis=0)
         scale = jnp.sqrt(jnp.sum(power, keepdims=True)) * lax.rsqrt(jnp.sum(total, keepdims=True) + NORM_EPS)
@@ -296,10 +293,9 @@
         kernel,
         jax.ShapeDtypeStruct((1, block, block), BF16),
         (1,),
-        [anywhere] * 3,
+        [pl.BlockSpec(memory_space=pltpu.VMEM), anywhere, anywhere],
         anywhere,
         [
-            pltpu.VMEM(received.shape, BF16),
             pltpu.VMEM((2, dp_count, 2, rows, block), BF16),
             pltpu.VMEM((block, block), BF16),
             pltpu.VMEM((block, block), BF16),
@@ -308,8 +304,8 @@
             pltpu.SemaphoreType.DMA((4,)),
         ],
         cost=1 << 20,
-        grant=60 * 1024 * 1024,
-    )(ids, received, left_root, right_root)
+        grant=24 * 1024 * 1024,
+    )(ids, in_vmem(received), left_root, right_root)
 
 
 def slot_blocks(block_owner, slot_count):
@@ -331,6 +327,7 @@
     z, core = lax.axis_index("z"), lax.axis_index("core")
     ids = jnp.stack([jnp.where(core == 0, x, y), jnp.where(core == 0, y, x), core]).astype(jnp.int32)
     parts = grad_parts.reshape(matrices, dp_count, CHUNKS, rows, width)
+    parts = pltpu.with_memory_space_constraint(parts, pltpu.HBM)
     known = moment.reshape(matrices, CHUNKS, rows, width)
 
     block_of, present = slot_blocks(block_owner, dp_count * SIDE * 2)
@@ -340,7 +337,7 @@
     picks = jnp.stack([(plane - z) % SIDE, column], axis=1).reshape(-1)
     mine = device_number(x, y, z, core)
     own_block = block_of[mine]
-    own = jnp.stack([present[mine], own_block // (sides * sides) * sides + own_block % sides])
+    owned = jnp.stack([present[mine], own_block // (sides * sides) * sides + own_block % sides])
 
     def along(phase, up, down):
         return send(down, in_plane(phase, -1)), send(up, in_plane(phase, 1))
@@ -349,17 +346,20 @@
         return [mine, send(down, in_plane(1, -1)), send(up, in_plane(1, 1)), send(far, in_plane(1, 2))]
 
     last = ()
-    sent, late, sums = [], [], []
+    sent, own, late, sums = [], [], [], []
     for chunk in range(CHUNKS):
         up, down = extract(ids, parts, chunk, ((2, 1), (1, 0), (-2, 0), (-1, 1)), last)
         last = (up,)
         sent.append(along(0, up, down))
     for chunk in range(CHUNKS):
-        up, down = relay(ids, parts, *sent[chunk], chunk, last)
+        own.append(extract(ids, parts, chunk, ((1, 1), (0, 0), (-1, 0), (0, 1)), last))
+        last = (own[chunk][0],)
+    for chunk in range(CHUNKS):
+        up, down = relay(ids, *own[chunk], *sent[chunk], last)
         last = (up,)
         late.append(along(0, up, down))
     for chunk in range(CHUNKS):
-        terms = first_sum(ids, parts, *sent[chunk], *late[chunk], chunk, last)
+        terms = first_sum(ids, *own[chunk], *sent[chunk], *late[chunk], last)
         last = (terms[0],)
         sums.append(second_axis(*terms))
     held = []
@@ -371,7 +371,8 @@
     outgoing = choose(picks, held, last)
     received = lax.all_to_all(outgoing, ("dp", "core"), 0, 0, tiled=True)
     received = received.reshape((dp_count, 2) + received.shape[1:])
-    return finish(own, received, left_roots, right_roots, block)
+    left, right = (pltpu.with_memory_space_constraint(value, pltpu.HBM) for value in (left_roots, right_roots))
+    return finish(owned, received, left, right, block)
 
 
 def solution(mesh):

time: 163 us -> 158 us (0.969)
  Pallas kernels: 35.9 us -> 29.7 us
  starting transfers between devices: 38.8 us -> 42.9 us
    pallas_call x10 -> x12, Pallas kernels: 35.9 us -> 29.7 us  [call(): return lambda *operands: made(*operands, *after)]
    all_to_all x1, starting transfers between devices: 9.9 us -> 13.8 us  [shards(): received = lax.all_to_all(outgoing, ('dp', 'core'), 0, 0, tiled=True)]
  transfers between devices with their start and end apart: 21 -> 21, of which waited for: 15 -> 14; matrix products, arithmetic and copies ran while one was open for 2% -> 2% of each run, Pallas kernels for 12% -> 10%
where the time goes in v5:
time: 158 us
  waiting for transfers between devices  79.9 us (51%)
  starting transfers between devices  42.9 us (27%)
  Pallas kernels  29.7 us (19%)
  between operations  2.95 us (2%)
  local copies, waits for them, and re-layouts  1.71 us (1%)
    ppermute x20, waiting for transfers between devices, send(): return lax.ppermute(value, ('dp', 'z', 'core'), routes(move))  54.9 us
    pallas_call x12, Pallas kernels, call(): return lambda *operands: made(*operands, *after)  29.7 us
    ppermute x20, starting transfers between devices, send(): return lax.ppermute(value, ('dp', 'z', 'core'), routes(move))  29.1 us
    all_to_all x1, waiting for transfers between devices, shards(): received = lax.all_to_all(outgoing, ('dp', 'core'), 0, 0, tiled=True)  25.1 us
    all_to_all x1, starting transfers between devices, shards(): received = lax.all_to_all(outgoing, ('dp', 'core'), 0, 0, tiled=True)  13.8 us
  transfers between devices with their start and end apart: 21, of which 14 were waited for; matrix products, arithmetic and copies ran while one was open for 2% of the time, Pallas kernels for 10%

profile of v5, /device:TPU:1, one launch (start us, length us, event | category | flops | bytes accessed | tf_op | source)
XLA Modules:
  0.0 158.1 jit_solution(2131605040382316216)
XLA Ops:
  0.1 2.6 %shard_map.55 = (bf16[2,3,4,16,2048]{4,3,2,1,0:T(8,128)(2,1)S(1)}, bf16[2,3,4,16,2048]{4,3,2,1,0:T(8,128)(2,1)S(1)}) custom-call(s32[3]{0:T(128)S(1)} %pad_add_fusion.2.ids, bf16[3,16,2,16,4096]{4,3,2,1,0:T(8,128)(2,1)} %bitcast.11), custom_call_target="tpu_custom_call" | custom-call | flops 1 | bytes 4 | tf_op jit(solution)/shard_map/pallas_call | solution.py:69
  2.7 3.6 %collective-permute-start.1 = (bf16[2,3,4,16,2048]{4,3,2,1,0:T(8,128)(2,1)S(1)}, bf16[2,3,4,16,2048]{4,3,2,1,0:T(8,128)(2,1)S(1)}, u32[]{:S(2)}, u32[]{:S(2)}) collective-permute-start(bf16[2,3,4,16,2048]{4,3,2,1,0:T(8,128)(2,1)S(1)} %get-tuple-element.31), channel_id=1, source_target_pairs={{0,96},{1,25},{2,98},{3,27},{4,100},{5,29},{6,102},{7,31},{8,104},... | collective-permute-start | bytes 4718600 | tf_op jit(solution)/shard_map/ppermute | solution.py:38
  6.4 2.6 %shard_map.56 = (bf16[2,3,4,16,2048]{4,3,2,1,0:T(8,128)(2,1)S(1)}, bf16[2,3,4,16,2048]{4,3,2,1,0:T(8,128)(2,1)S(1)}) custom-call(s32[3]{0:T(128)S(1)} %pad_add_fusion.2.ids, bf16[3,16,2,16,4096]{4,3,2,1,0:T(8,128)(2,1)} %bitcast.12, bf16[2,3,4,16,2048]{4,3,2,1,0:T(8,128)(2,1)S(1)} %get-tuple-element.27.refs_1_), custom_call_target="tpu_custom_call" | custom-call | flops 1 | bytes 4 | tf_op jit(solution)/shard_map/pallas_call | solution.py:69
  9.0 2.7 %collective-permute-start.5 = (bf16[2,3,4,16,2048]{4,3,2,1,0:T(8,128)(2,1)S(1)}, bf16[2,3,4,16,2048]{4,3,2,1,0:T(8,128)(2,1)S(1)}, u32[]{:S(2)}, u32[]{:S(2)}) collective-permute-start(bf16[2,3,4,16,2048]{4,3,2,1,0:T(8,128)(2,1)S(1)} %get-tuple-element.36), channel_id=1, source_target_pairs={{0,96},{1,25},{2,98},{3,27},{4,100},{5,29},{6,102},{7,31},{8,104},... | collective-permute-start | bytes 4718600 | tf_op jit(solution)/shard_map/ppermute | solution.py:38
  11.8 2.6 %shard_map.57 = (bf16[2,3,4,16,2048]{4,3,2,1,0:T(8,128)(2,1)S(1)}, bf16[2,3,4,16,2048]{4,3,2,1,0:T(8,128)(2,1)S(1)}) custom-call(s32[3]{0:T(128)S(1)} %pad_add_fusion.2.ids, bf16[3,16,2,16,4096]{4,3,2,1,0:T(8,128)(2,1)} %bitcast.13, bf16[2,3,4,16,2048]{4,3,2,1,0:T(8,128)(2,1)S(1)} %get-tuple-element.28.refs_1_), custom_call_target="tpu_custom_call" | custom-call | flops 1 | bytes 4 | tf_op jit(solution)/shard_map/pallas_call | solution.py:69
  14.4 2.6 %shard_map.58 = (bf16[2,3,4,16,2048]{4,3,2,1,0:T(8,128)(2,1)S(1)}, bf16[2,3,4,16,2048]{4,3,2,1,0:T(8,128)(2,1)S(1)}) custom-call(s32[3]{0:T(128)S(1)} %pad_add_fusion.2.ids, bf16[3,16,2,16,4096]{4,3,2,1,0:T(8,128)(2,1)} %bitcast.14, bf16[2,3,4,16,2048]{4,3,2,1,0:T(8,128)(2,1)S(1)} %get-tuple-element.29.refs_1_.refs_0_), custom_call_target="tpu_custom_call" | custom-call | flops 1 | bytes 4 | tf_op jit(solution)/shard_map/pallas_call | solution.py:69
  17.1 6.7 %collective-permute-done.1.refs_3_ = bf16[2,3,4,16,2048]{4,3,2,1,0:T(8,128)(2,1)S(1)} collective-permute-done((bf16[2,3,4,16,2048]{4,3,2,1,0:T(8,128)(2,1)S(1)}, bf16[2,3,4,16,2048]{4,3,2,1,0:T(8,128)(2,1)S(1)}, u32[]{:S(2)}, u32[]{:S(2)}) %collective-permute-start.1) | collective-permute-done | bytes 1572896 | tf_op jit(solution)/shard_map/ppermute | solution.py:38
  23.7 3.4 %collective-permute-done.refs_2_ = bf16[2,3,4,16,2048]{4,3,2,1,0:T(8,128)(2,1)S(1)} collective-permute-done((bf16[2,3,4,16,2048]{4,3,2,1,0:T(8,128)(2,1)S(1)}, bf16[2,3,4,16,2048]{4,3,2,1,0:T(8,128)(2,1)S(1)}, u32[]{:S(2)}, u32[]{:S(2)}) %collective-permute-start) | collective-permute-done | bytes 1572896 | tf_op jit(solution)/shard_map/ppermute | solution.py:38
  28.2 1.5 collective-permute-start.3
  29.6 10.9 %collective-permute-done.5.refs_3_ = bf16[2,3,4,16,2048]{4,3,2,1,0:T(8,128)(2,1)S(1)} collective-permute-done((bf16[2,3,4,16,2048]{4,3,2,1,0:T(8,128)(2,1)S(1)}, bf16[2,3,4,16,2048]{4,3,2,1,0:T(8,128)(2,1)S(1)}, u32[]{:S(2)}, u32[]{:S(2)}) %collective-permute-start.5) | collective-permute-done | bytes 1572896 | tf_op jit(solution)/shard_map/ppermute | solution.py:38
  40.6 3.4 %collective-permute-done.4.refs_2_ = bf16[2,3,4,16,2048]{4,3,2,1,0:T(8,128)(2,1)S(1)} collective-permute-done((bf16[2,3,4,16,2048]{4,3,2,1,0:T(8,128)(2,1)S(1)}, bf16[2,3,4,16,2048]{4,3,2,1,0:T(8,128)(2,1)S(1)}, u32[]{:S(2)}, u32[]{:S(2)}) %collective-permute-start.4) | collective-permute-done | bytes 1572896 | tf_op jit(solution)/shard_map/ppermute | solution.py:38
  45.0 1.5 collective-permute-start.10
  46.5 2.5 %collective-permute-done.2.refs_4_ = bf16[3,4,16,2048]{3,2,1,0:T(8,128)(2,1)S(1)} collective-permute-done((bf16[3,4,16,2048]{3,2,1,0:T(8,128)(2,1)S(1)}, bf16[3,4,16,2048]{3,2,1,0:T(8,128)(2,1)S(1)}, u32[]{:S(2)}, u32[]{:S(2)}) %collective-permute-start.2) | collective-permute-done | bytes 786464 | tf_op jit(solution)/shard_map/ppermute | solution.py:38
  49.0 3.4 %collective-permute-done.3.refs_5_ = bf16[3,4,16,2048]{3,2,1,0:T(8,128)(2,1)S(1)} collective-permute-done((bf16[3,4,16,2048]{3,2,1,0:T(8,128)(2,1)S(1)}, bf16[3,4,16,2048]{3,2,1,0:T(8,128)(2,1)S(1)}, u32[]{:S(2)}, u32[]{:S(2)}) %collective-permute-start.3) | collective-permute-done | bytes 786464 | tf_op jit(solution)/shard_map/ppermute | solution.py:38
  52.4 1.6 %shard_map.61 = (bf16[3,16,4096]{2,1,0:T(8,128)(2,1)S(1)}, bf16[3,16,4096]{2,1,0:T(8,128)(2,1)S(1)}, bf16[3,16,4096]{2,1,0:T(8,128)(2,1)S(1)}, bf16[3,16,4096]{2,1,0:T(8,128)(2,1)S(1)}) custom-call(s32[3]{0:T(128)S(1)} %pad_add_fusion.2.ids, bf16[2,3,4,16,2048]{4,3,2,1,0:T(8,128)(2,1)S(1)} %get-tuple-element.29.refs_1_.refs_0_, ...), custom_call_target="tpu_custom_call" | custom-call | flops 1 | bytes 4 | tf_op jit(solution)/shard_map/pallas_call | solution.py:69
  54.0 2.5 %collective-permute-start.6 = (bf16[3,16,4096]{2,1,0:T(8,128)(2,1)S(1)}, bf16[3,16,4096]{2,1,0:T(8,128)(2,1)S(1)}, u32[]{:S(2)}, u32[]{:S(2)}) collective-permute-start(bf16[3,16,4096]{2,1,0:T(8,128)(2,1)S(1)} %get-tuple-element.39), channel_id=1, source_target_pairs={{0,24},{1,97},{2,26},{3,99},{4,28},{5,101},{6,30},{7,103},{8,0},{9... | collective-permute-start | bytes 1179656 | tf_op jit(solution)/shard_map/ppermute | solution.py:38
  56.6 1.4 collective-permute-start.8
  58.0 2.8 %collective-permute-done.10.refs_5_ = bf16[3,4,16,2048]{3,2,1,0:T(8,128)(2,1)S(1)} collective-permute-done((bf16[3,4,16,2048]{3,2,1,0:T(8,128)(2,1)S(1)}, bf16[3,4,16,2048]{3,2,1,0:T(8,128)(2,1)S(1)}, u32[]{:S(2)}, u32[]{:S(2)}) %collective-permute-start.10) | collective-permute-done | bytes 786464 | tf_op jit(solution)/shard_map/ppermute | solution.py:38
  60.8 1.6 %shard_map.62 = (bf16[3,16,4096]{2,1,0:T(8,128)(2,1)S(1)}, bf16[3,16,4096]{2,1,0:T(8,128)(2,1)S(1)}, bf16[3,16,4096]{2,1,0:T(8,128)(2,1)S(1)}, bf16[3,16,4096]{2,1,0:T(8,128)(2,1)S(1)}) custom-call(s32[3]{0:T(128)S(1)} %pad_add_fusion.2.ids, bf16[2,3,4,16,2048]{4,3,2,1,0:T(8,128)(2,1)S(1)} %get-tuple-element.32.refs_4_.refs_0_, ...), custom_call_target="tpu_custom_call" | custom-call | flops 1 | bytes 4 | tf_op jit(solution)/shard_map/pallas_call | solution.py:69
  62.5 3.0 %collective-permute-start.14 = (bf16[3,16,4096]{2,1,0:T(8,128)(2,1)S(1)}, bf16[3,16,4096]{2,1,0:T(8,128)(2,1)S(1)}, u32[]{:S(2)}, u32[]{:S(2)}) collective-permute-start(bf16[3,16,4096]{2,1,0:T(8,128)(2,1)S(1)} %get-tuple-element.45), channel_id=1, source_target_pairs={{0,24},{1,97},{2,26},{3,99},{4,28},{5,101},{6,30},{7,103},{8,0},{9... | collective-permute-start | bytes 1179656 | tf_op jit(solution)/shard_map/ppermute | solution.py:38
  67.9 2.5 %collective-permute-done.7.refs_2_ = bf16[3,16,4096]{2,1,0:T(8,128)(2,1)S(1)} collective-permute-done((bf16[3,16,4096]{2,1,0:T(8,128)(2,1)S(1)}, bf16[3,16,4096]{2,1,0:T(8,128)(2,1)S(1)}, u32[]{:S(2)}, u32[]{:S(2)}) %collective-permute-start.7) | collective-permute-done | bytes 393248 | tf_op jit(solution)/shard_map/ppermute | solution.py:38
  71.7 1.7 %collective-permute-start.13 = (bf16[96,16,128]{2,1,0:T(8,128)(2,1)S(1)}, bf16[96,16,128]{2,1,0:T(8,128)(2,1)S(1)}, u32[]{:S(2)}, u32[]{:S(2)}) collective-permute-start(bf16[96,16,128]{2,1,0:T(8,128)(2,1)S(1)} %get-tuple-element.44.refs_6_.refs_0_), channel_id=1, source_target_pairs={{0,2},{1,3},{2,4},{3,5},{4,6},{5,7},{6,0},{7,1},{8,10},{9,11},{10,... | collective-permute-start | bytes 1179656 | tf_op jit(solution)/shard_map/ppermute | solution.py:38
  73.4 3.3 %collective-permute-start.12 = (bf16[96,16,128]{2,1,0:T(8,128)(2,1)S(1)}, bf16[96,16,128]{2,1,0:T(8,128)(2,1)S(1)}, u32[]{:S(2)}, u32[]{:S(2)}) collective-permute-start(bf16[96,16,128]{2,1,0:T(8,128)(2,1)S(1)} %get-tuple-element.44.refs_6_.refs_0_), channel_id=1, source_target_pairs={{0,4},{1,5},{2,6},{3,7},{4,0},{5,1},{6,2},{7,3},{8,12},{9,13},{10,... | collective-permute-start | bytes 1179656 | tf_op jit(solution)/shard_map/ppermute | solution.py:38
  78.6 1.3 shard_map.64.refs_4_.refs_8_
  79.8 1.7 %collective-permute-start.19 = (bf16[97,16,128]{2,1,0:T(8,128)(2,1)S(1)}, bf16[97,16,128]{2,1,0:T(8,128)(2,1)S(1)}, u32[]{:S(2)}, u32[]{:S(2)}) collective-permute-start(bf16[97,16,128]{2,1,0:T(8,128)(2,1)S(1)} %shard_map.64.refs_4_.refs_8_), channel_id=1, source_target_pairs={{0,2},{1,3},{2,4},{3,5},{4,6},{5,7},{6,0},{7,1},{8,10},{9,11},{10,... | collective-permute-start | bytes 1191944 | tf_op jit(solution)/shard_map/ppermute | solution.py:38
  81.5 3.3 %collective-permute-start.18 = (bf16[97,16,128]{2,1,0:T(8,128)(2,1)S(1)}, bf16[97,16,128]{2,1,0:T(8,128)(2,1)S(1)}, u32[]{:S(2)}, u32[]{:S(2)}) collective-permute-start(bf16[97,16,128]{2,1,0:T(8,128)(2,1)S(1)} %shard_map.64.refs_4_.refs_8_), channel_id=1, source_target_pairs={{0,4},{1,5},{2,6},{3,7},{4,0},{5,1},{6,2},{7,3},{8,12},{9,13},{10,... | collective-permute-start | bytes 1191944 | tf_op jit(solution)/shard_map/ppermute | solution.py:38
  86.3 8.8 %collective-permute-done.19.refs_7_ = bf16[97,16,128]{2,1,0:T(8,128)(2,1)S(1)} collective-permute-done((bf16[97,16,128]{2,1,0:T(8,128)(2,1)S(1)}, bf16[97,16,128]{2,1,0:T(8,128)(2,1)S(1)}, u32[]{:S(2)}, u32[]{:S(2)}) %collective-permute-start.19) | collective-permute-done | bytes 397344 | tf_op jit(solution)/shard_map/ppermute | solution.py:38
  95.1 7.8 %collective-permute-done.18.refs_6_ = bf16[97,16,128]{2,1,0:T(8,128)(2,1)S(1)} collective-permute-done((bf16[97,16,128]{2,1,0:T(8,128)(2,1)S(1)}, bf16[97,16,128]{2,1,0:T(8,128)(2,1)S(1)}, u32[]{:S(2)}, u32[]{:S(2)}) %collective-permute-start.18) | collective-permute-done | bytes 397344 | tf_op jit(solution)/shard_map/ppermute | solution.py:38
  103.0 3.2 %shard_map.65 = bf16[32,17,16,128]{3,2,1,0:T(8,128)(2,1)} custom-call(s32[64]{0:T(128)S(1)} %reshape.234.ids, bf16[96,16,128]{2,1,0:T(8,128)(2,1)S(1)} %get-tuple-element.44.refs_6_.refs_0_, bf16[96,16,128]{2,1,0:T(8,128)(2,1)S(1)} %collective-permute-done.11.refs_1_, bf16[96,16,128]{2,1,0:T(8,128)(2,1)S(1)} %collective-permute-done.12.refs_2_, ...), custom_call_target="tpu_custom_call" | custom-call | flops 1 | bytes 4 | tf_op jit(solution)/shard_map/pallas_call | solution.py:69
  106.1 13.8 %all-to-all-start = ((bf16[32,17,16,128]{3,2,1,0:T(8,128)(2,1)}), bf16[32,17,16,128]{3,2,1,0:T(8,128)(2,1)S(1)}, u32[]{:S(2)}, u32[]{:S(2)}) async-start(bf16[32,17,16,128]{3,2,1,0:T(8,128)(2,1)} %shard_map.65), calls=%async_computation | async-start | bytes 4456448 | tf_op jit(solution)/shard_map/all_to_all | solution.py:372
  124.6 25.1 %all-to-all-done = bf16[32,17,16,128]{3,2,1,0:T(8,128)(2,1)S(1)} async-done(((bf16[32,17,16,128]{3,2,1,0:T(8,128)(2,1)}), bf16[32,17,16,128]{3,2,1,0:T(8,128)(2,1)S(1)}, u32[]{:S(2)}, u32[]{:S(2)}) %all-to-all-start) | async-done | bytes 2228256 | tf_op jit(solution)/shard_map/all_to_all | solution.py:372
  149.7 8.3 %shard_map.66 = bf16[1,1024,1024]{2,1,0:T(8,128)(2,1)} custom-call(s32[2]{0:T(128)S(1)} %pad_add_fusion.1.ids, bf16[16,2,17,16,128]{4,3,2,1,0:T(8,128)(2,1)S(1)} %bitcast.8, bf16[1,1024,1024]{2,1,0:T(8,128)(2,1)} %refs_1_.1, bf16[1,1024,1024]{2,1,0:T(8,128)(2,1)} %refs_2_.1), custom_call_target="tpu_custom_call" | custom-call | flops 1048576 | bytes 4194304 | tf_op jit(solution)/shard_map/pallas_call | solution.py:69
  (38 shorter events, 11.1 us)
Async XLA Ops:
  2.7 21.0 %collective-permute-start.1 = (bf16[2,3,4,16,2048]{4,3,2,1,0:T(8,128)(2,1)S(1)}, bf16[2,3,4,16,2048]{4,3,2,1,0:T(8,128)(2,1)S(1)}, u32[]{:S(2)}, u32[]{:S(2)}) collective-permute-start(bf16[2,3,4,16,2048]{4,3,2,1,0:T(8,128)(2,1)S(1)} %get-tuple-element.31), channel_id=1, source_target_pairs={{0,96},{1,25},{2,98},{3,27},{4,100},{5,29},{6,102},{7,31},{8,104},... | collective-permute-start | bytes 4718600 | tf_op jit(solution)/shard_map/ppermute | solution.py:38
  6.4 20.8 %collective-permute-start = (bf16[2,3,4,16,2048]{4,3,2,1,0:T(8,128)(2,1)S(1)}, bf16[2,3,4,16,2048]{4,3,2,1,0:T(8,128)(2,1)S(1)}, u32[]{:S(2)}, u32[]{:S(2)}) collective-permute-start(bf16[2,3,4,16,2048]{4,3,2,1,0:T(8,128)(2,1)S(1)} %get-tuple-element.27.refs_1_), channel_id=1, source_target_pairs={{0,32},{1,9},{2,34},{3,11},{4,36},{5,13},{6,38},{7,15},{8,40},{9,1... | collective-permute-start | bytes 4718600 | tf_op jit(solution)/shard_map/ppermute | solution.py:38
  9.0 31.6 %collective-permute-start.5 = (bf16[2,3,4,16,2048]{4,3,2,1,0:T(8,128)(2,1)S(1)}, bf16[2,3,4,16,2048]{4,3,2,1,0:T(8,128)(2,1)S(1)}, u32[]{:S(2)}, u32[]{:S(2)}) collective-permute-start(bf16[2,3,4,16,2048]{4,3,2,1,0:T(8,128)(2,1)S(1)} %get-tuple-element.36), channel_id=1, source_target_pairs={{0,96},{1,25},{2,98},{3,27},{4,100},{5,29},{6,102},{7,31},{8,104},... | collective-permute-start | bytes 4718600 | tf_op jit(solution)/shard_map/ppermute | solution.py:38
  11.8 32.2 %collective-permute-start.4 = (bf16[2,3,4,16,2048]{4,3,2,1,0:T(8,128)(2,1)S(1)}, bf16[2,3,4,16,2048]{4,3,2,1,0:T(8,128)(2,1)S(1)}, u32[]{:S(2)}, u32[]{:S(2)}) collective-permute-start(bf16[2,3,4,16,2048]{4,3,2,1,0:T(8,128)(2,1)S(1)} %get-tuple-element.28.refs_1_), channel_id=1, source_target_pairs={{0,32},{1,9},{2,34},{3,11},{4,36},{5,13},{6,38},{7,15},{8,40},{9,1... | collective-permute-start | bytes 4718600 | tf_op jit(solution)/shard_map/ppermute | solution.py:38
  28.1 20.9 %collective-permute-start.2 = (bf16[3,4,16,2048]{3,2,1,0:T(8,128)(2,1)S(1)}, bf16[3,4,16,2048]{3,2,1,0:T(8,128)(2,1)S(1)}, u32[]{:S(2)}, u32[]{:S(2)}) collective-permute-start(bf16[3,4,16,2048]{3,2,1,0:T(8,128)(2,1)S(1)} %get-tuple-element.33), channel_id=1, source_target_pairs={{0,96},{1,25},{2,98},{3,27},{4,100},{5,29},{6,102},{7,31},{8,104},... | collective-permute-start | bytes 2359304 | tf_op jit(solution)/shard_map/ppermute | solution.py:38
  28.2 24.2 %collective-permute-start.3 = (bf16[3,4,16,2048]{3,2,1,0:T(8,128)(2,1)S(1)}, bf16[3,4,16,2048]{3,2,1,0:T(8,128)(2,1)S(1)}, u32[]{:S(2)}, u32[]{:S(2)}) collective-permute-start(bf16[3,4,16,2048]{3,2,1,0:T(8,128)(2,1)S(1)} %get-tuple-element.34.refs_4_), channel_id=1, source_target_pairs={{0,32},{1,9},{2,34},{3,11},{4,36},{5,13},{6,38},{7,15},{8,40},{9,1... | collective-permute-start | bytes 2359304 | tf_op jit(solution)/shard_map/ppermute | solution.py:38
  45.0 13.1 %collective-permute-start.9 = (bf16[3,4,16,2048]{3,2,1,0:T(8,128)(2,1)S(1)}, bf16[3,4,16,2048]{3,2,1,0:T(8,128)(2,1)S(1)}, u32[]{:S(2)}, u32[]{:S(2)}) collective-permute-start(bf16[3,4,16,2048]{3,2,1,0:T(8,128)(2,1)S(1)} %get-tuple-element.42), channel_id=1, source_target_pairs={{0,96},{1,25},{2,98},{3,27},{4,100},{5,29},{6,102},{7,31},{8,104},... | collective-permute-start | bytes 2359304 | tf_op jit(solution)/shard_map/ppermute | solution.py:38
  45.0 15.8 %collective-permute-start.10 = (bf16[3,4,16,2048]{3,2,1,0:T(8,128)(2,1)S(1)}, bf16[3,4,16,2048]{3,2,1,0:T(8,128)(2,1)S(1)}, u32[]{:S(2)}, u32[]{:S(2)}) collective-permute-start(bf16[3,4,16,2048]{3,2,1,0:T(8,128)(2,1)S(1)} %get-tuple-element.37.refs_6_), channel_id=1, source_target_pairs={{0,32},{1,9},{2,34},{3,11},{4,36},{5,13},{6,38},{7,15},{8,40},{9,1... | collective-permute-start | bytes 2359304 | tf_op jit(solution)/shard_map/ppermute | solution.py:38
  54.0 12.7 %collective-permute-start.6 = (bf16[3,16,4096]{2,1,0:T(8,128)(2,1)S(1)}, bf16[3,16,4096]{2,1,0:T(8,128)(2,1)S(1)}, u32[]{:S(2)}, u32[]{:S(2)}) collective-permute-start(bf16[3,16,4096]{2,1,0:T(8,128)(2,1)S(1)} %get-tuple-element.39), channel_id=1, source_target_pairs={{0,24},{1,97},{2,26},{3,99},{4,28},{5,101},{6,30},{7,103},{8,0},{9... | collective-permute-start | bytes 1179656 | tf_op jit(solution)/shard_map/ppermute | solution.py:38
  56.6 13.8 %collective-permute-start.7 = (bf16[3,16,4096]{2,1,0:T(8,128)(2,1)S(1)}, bf16[3,16,4096]{2,1,0:T(8,128)(2,1)S(1)}, u32[]{:S(2)}, u32[]{:S(2)}) collective-permute-start(bf16[3,16,4096]{2,1,0:T(8,128)(2,1)S(1)} %get-tuple-element.40), channel_id=1, source_target_pairs={{0,8},{1,33},{2,10},{3,35},{4,12},{5,37},{6,14},{7,39},{8,16},{9,4... | collective-permute-start | bytes 1179656 | tf_op jit(solution)/shard_map/ppermute | solution.py:38
  56.6 13.8 %collective-permute-start.8 = (bf16[3,16,4096]{2,1,0:T(8,128)(2,1)S(1)}, bf16[3,16,4096]{2,1,0:T(8,128)(2,1)S(1)}, u32[]{:S(2)}, u32[]{:S(2)}) collective-permute-start(bf16[3,16,4096]{2,1,0:T(8,128)(2,1)S(1)} %get-tuple-element.41), channel_id=1, source_target_pairs={{0,16},{1,65},{2,18},{3,67},{4,20},{5,69},{6,22},{7,71},{8,24},{9,... | collective-permute-start | bytes 1179656 | tf_op jit(solution)/shard_map/ppermute | solution.py:38
  60.8 9.6 %copy-start = (f32[3,32,4096]{2,1,0:T(8,128)S(1)}, f32[3,32,4096]{2,1,0:T(8,128)}, u32[]{:S(2)}) copy-start(f32[3,32,4096]{2,1,0:T(8,128)} %param.6) | copy-start | bytes 4718596
  62.5 14.2 %collective-permute-start.14 = (bf16[3,16,4096]{2,1,0:T(8,128)(2,1)S(1)}, bf16[3,16,4096]{2,1,0:T(8,128)(2,1)S(1)}, u32[]{:S(2)}, u32[]{:S(2)}) collective-permute-start(bf16[3,16,4096]{2,1,0:T(8,128)(2,1)S(1)} %get-tuple-element.45), channel_id=1, source_target_pairs={{0,24},{1,97},{2,26},{3,99},{4,28},{5,101},{6,30},{7,103},{8,0},{9... | collective-permute-start | bytes 1179656 | tf_op jit(solution)/shard_map/ppermute | solution.py:38
  65.5 13.1 %collective-permute-start.15 = (bf16[3,16,4096]{2,1,0:T(8,128)(2,1)S(1)}, bf16[3,16,4096]{2,1,0:T(8,128)(2,1)S(1)}, u32[]{:S(2)}, u32[]{:S(2)}) collective-permute-start(bf16[3,16,4096]{2,1,0:T(8,128)(2,1)S(1)} %get-tuple-element.46), channel_id=1, source_target_pairs={{0,8},{1,33},{2,10},{3,35},{4,12},{5,37},{6,14},{7,39},{8,16},{9,4... | collective-permute-start | bytes 1179656 | tf_op jit(solution)/shard_map/ppermute | solution.py:38
  66.7 11.8 %collective-permute-start.16 = (bf16[3,16,4096]{2,1,0:T(8,128)(2,1)S(1)}, bf16[3,16,4096]{2,1,0:T(8,128)(2,1)S(1)}, u32[]{:S(2)}, u32[]{:S(2)}) collective-permute-start(bf16[3,16,4096]{2,1,0:T(8,128)(2,1)S(1)} %get-tuple-element.47), channel_id=1, source_target_pairs={{0,16},{1,65},{2,18},{3,67},{4,20},{5,69},{6,22},{7,71},{8,24},{9,... | collective-permute-start | bytes 1179656 | tf_op jit(solution)/shard_map/ppermute | solution.py:38
  71.7 13.2 %collective-permute-start.13 = (bf16[96,16,128]{2,1,0:T(8,128)(2,1)S(1)}, bf16[96,16,128]{2,1,0:T(8,128)(2,1)S(1)}, u32[]{:S(2)}, u32[]{:S(2)}) collective-permute-start(bf16[96,16,128]{2,1,0:T(8,128)(2,1)S(1)} %get-tuple-element.44.refs_6_.refs_0_), channel_id=1, source_target_pairs={{0,2},{1,3},{2,4},{3,5},{4,6},{5,7},{6,0},{7,1},{8,10},{9,11},{10,... | collective-permute-start | bytes 1179656 | tf_op jit(solution)/shard_map/ppermute | solution.py:38
  73.4 13.0 %collective-permute-start.12 = (bf16[96,16,128]{2,1,0:T(8,128)(2,1)S(1)}, bf16[96,16,128]{2,1,0:T(8,128)(2,1)S(1)}, u32[]{:S(2)}, u32[]{:S(2)}) collective-permute-start(bf16[96,16,128]{2,1,0:T(8,128)(2,1)S(1)} %get-tuple-element.44.refs_6_.refs_0_), channel_id=1, source_target_pairs={{0,4},{1,5},{2,6},{3,7},{4,0},{5,1},{6,2},{7,3},{8,12},{9,13},{10,... | collective-permute-start | bytes 1179656 | tf_op jit(solution)/shard_map/ppermute | solution.py:38
  76.7 9.7 %collective-permute-start.11 = (bf16[96,16,128]{2,1,0:T(8,128)(2,1)S(1)}, bf16[96,16,128]{2,1,0:T(8,128)(2,1)S(1)}, u32[]{:S(2)}, u32[]{:S(2)}) collective-permute-start(bf16[96,16,128]{2,1,0:T(8,128)(2,1)S(1)} %get-tuple-element.44.refs_6_.refs_0_), channel_id=1, source_target_pairs={{0,6},{1,7},{2,0},{3,1},{4,2},{5,3},{6,4},{7,5},{8,14},{9,15},{10,... | collective-permute-start | bytes 1179656 | tf_op jit(solution)/shard_map/ppermute | solution.py:38
  78.6 7.0 %copy-start.1 = (s32[48]{0:T(128)S(1)}, s32[48]{0:T(128)}, u32[]{:S(2)}) copy-start(s32[48]{0:T(128)} %param.9) | copy-start | bytes 580
  79.8 15.3 %collective-permute-start.19 = (bf16[97,16,128]{2,1,0:T(8,128)(2,1)S(1)}, bf16[97,16,128]{2,1,0:T(8,128)(2,1)S(1)}, u32[]{:S(2)}, u32[]{:S(2)}) collective-permute-start(bf16[97,16,128]{2,1,0:T(8,128)(2,1)S(1)} %shard_map.64.refs_4_.refs_8_), channel_id=1, source_target_pairs={{0,2},{1,3},{2,4},{3,5},{4,6},{5,7},{6,0},{7,1},{8,10},{9,11},{10,... | collective-permute-start | bytes 1191944 | tf_op jit(solution)/shard_map/ppermute | solution.py:38
  81.5 21.4 %collective-permute-start.18 = (bf16[97,16,128]{2,1,0:T(8,128)(2,1)S(1)}, bf16[97,16,128]{2,1,0:T(8,128)(2,1)S(1)}, u32[]{:S(2)}, u32[]{:S(2)}) collective-permute-start(bf16[97,16,128]{2,1,0:T(8,128)(2,1)S(1)} %shard_map.64.refs_4_.refs_8_), channel_id=1, source_target_pairs={{0,4},{1,5},{2,6},{3,7},{4,0},{5,1},{6,2},{7,3},{8,12},{9,13},{10,... | collective-permute-start | bytes 1191944 | tf_op jit(solution)/shard_map/ppermute | solution.py:38
  84.9 18.1 %collective-permute-start.17 = (bf16[97,16,128]{2,1,0:T(8,128)(2,1)S(1)}, bf16[97,16,128]{2,1,0:T(8,128)(2,1)S(1)}, u32[]{:S(2)}, u32[]{:S(2)}) collective-permute-start(bf16[97,16,128]{2,1,0:T(8,128)(2,1)S(1)} %shard_map.64.refs_4_.refs_8_), channel_id=1, source_target_pairs={{0,6},{1,7},{2,0},{3,1},{4,2},{5,3},{6,4},{7,5},{8,14},{9,15},{10,... | collective-permute-start | bytes 1191944 | tf_op jit(solution)/shard_map/ppermute | solution.py:38
  106.1 43.6 %all-to-all-start = ((bf16[32,17,16,128]{3,2,1,0:T(8,128)(2,1)}), bf16[32,17,16,128]{3,2,1,0:T(8,128)(2,1)S(1)}, u32[]{:S(2)}, u32[]{:S(2)}) async-start(bf16[32,17,16,128]{3,2,1,0:T(8,128)(2,1)} %shard_map.65), calls=%async_computation | async-start | bytes 4456448 | tf_op jit(solution)/shard_map/all_to_all | solution.py:372

commit v6 on v5

--- a/solution.py
+++ b/solution.py
@@ -208,30 +208,33 @@
     count = len(held[0])
     total, rows, _ = held[0][0].shape
     tiles = total // PIECES
-    steps = 4
 
     def kernel(picks, *refs):
-        first, second, out = refs[:count], refs[count : 2 * count], refs[2 * count]
-
-        @pl.loop(0, slots // steps)
-        def _(k):
-            slot = pl.program_id(0) * (slots // steps) + k
+        first, second, out, staged, sem = refs[:count], refs[count : 2 * count], *refs[2 * count :]
+
+        @pl.loop(0, slots)
+        def _(slot):
             piece = pl.ds(picks[2 * slot + 1] * tiles, tiles)
             for number in range(count):
 
                 @pl.when(picks[2 * slot] == number)
                 def _(number=number):
-                    out[k, :tiles] = first[number][piece]
-                    out[k, tiles : 2 * tiles] = second[number][piece]
-                    out[k, 2 * tiles] = second[number][total]
+                    staged[slot, :tiles] = first[number][piece]
+                    staged[slot, tiles : 2 * tiles] = second[number][piece]
+                    staged[slot, 2 * tiles] = second[number][total]
+
+            pltpu.make_async_copy(staged.at[slot], out.at[slot], sem).start()
+
+        pltpu.make_async_copy(staged, out, sem).wait()
 
     shape = (slots, 2 * tiles + 1, rows, LANES)
     return call(
         kernel,
         jax.ShapeDtypeStruct(shape, BF16),
-        (steps,),
+        (1,),
         [pl.BlockSpec(memory_space=pltpu.VMEM)] * (2 * count),
-        pl.BlockSpec((slots // steps,) + shape[1:], lambda t, ids: (t, 0, 0, 0)),
+        pl.BlockSpec(memory_space=pl.ANY),
+        [pltpu.VMEM(shape, BF16), pltpu.SemaphoreType.DMA],
         after=after,
         grant=VMEM_LIMIT,
     )(picks, *(in_vmem(value) for value in (*held[0], *held[1])))
@@ -240,7 +243,7 @@
 def finish(ids, received, left_root, right_root, block):
     dp_count, _, _, rows, _ = received.shape
     tiles = block // LANES
-    step = block // 2
+    step, part = block // 2, block // 4
 
     def kernel(ids, received, left, right, out, grads, lefts, rights, shaped, results, sem):
         get_lefts = [
@@ -250,7 +253,8 @@
         get_right = pltpu.make_async_copy(right.at[0], rights, sem.at[2])
         get_lefts[0].start()
         get_right.start()
-        get_lefts[1].start()
+        for get in get_lefts[1:]:
+            get.start()
 
         @pl.loop(0, dp_count)
         def _(group):
@@ -274,8 +278,8 @@
         power = jnp.sum(jnp.where(row == ids[1], powers, 0.0).reshape(-1, 8, LANES), axis=0)
         scale = jnp.sqrt(jnp.sum(power, keepdims=True)) * lax.rsqrt(jnp.sum(total, keepdims=True) + NORM_EPS)
         owned = ids[0] > 0
-        for at in range(0, block, step):
-            here = pl.ds(at, step)
+        for at in range(0, block, part):
+            here = pl.ds(at, part)
 
             @pl.when(owned)
             def _():
@@ -283,7 +287,7 @@
 
             @pl.when(jnp.logical_not(owned))
             def _():
-                results[here] = jnp.zeros((step, block), BF16)
+                results[here] = jnp.zeros((part, block), BF16)
 
             pltpu.make_async_copy(results.at[here], out.at[0, here], sem.at[3]).start()
         pltpu.make_async_copy(results, out.at[0], sem.at[3]).wait()

time: 158 us -> 158 us (level)
  no operation moved by 1% of the time
where the time goes in v6:
time: 158 us; the launch traced here: 157 us
  waiting for transfers between devices  79.9 us (51%)
  starting transfers between devices  42.9 us (27%)
  Pallas kernels  28.9 us (18%)
  between operations  2.96 us (2%)
  local copies, waits for them, and re-layouts  1.71 us (1%)
    ppermute x20, waiting for transfers between devices, send(): return lax.ppermute(value, ('dp', 'z', 'core'), routes(move))  54.9 us
    ppermute x20, starting transfers between devices, send(): return lax.ppermute(value, ('dp', 'z', 'core'), routes(move))  29.1 us
    pallas_call x12, Pallas kernels, call(): return lambda *operands: made(*operands, *after)  28.9 us
    all_to_all x1, waiting for transfers between devices, shards(): received = lax.all_to_all(outgoing, ('dp', 'core'), 0, 0, tiled=True)  25.1 us
    all_to_all x1, starting transfers between devices, shards(): received = lax.all_to_all(outgoing, ('dp', 'core'), 0, 0, tiled=True)  13.9 us
  transfers between devices with their start and end apart: 21, of which 14 were waited for; matrix products, arithmetic and copies ran while one was open for 2% of the time, Pallas kernels for 10%

profile of v6, /device:TPU:1, one launch (start us, length us, event | category | flops | bytes accessed | tf_op | source)
XLA Modules:
  0.0 157.5 jit_solution(9607824907181707236)
XLA Ops:
  0.1 2.6 %shard_map.55 = (bf16[2,3,4,16,2048]{4,3,2,1,0:T(8,128)(2,1)S(1)}, bf16[2,3,4,16,2048]{4,3,2,1,0:T(8,128)(2,1)S(1)}) custom-call(s32[3]{0:T(128)S(1)} %pad_add_fusion.2.ids, bf16[3,16,2,16,4096]{4,3,2,1,0:T(8,128)(2,1)} %bitcast.11), custom_call_target="tpu_custom_call" | custom-call | flops 1 | bytes 4 | tf_op jit(solution)/shard_map/pallas_call | solution.py:69
  2.7 3.6 %collective-permute-start.1 = (bf16[2,3,4,16,2048]{4,3,2,1,0:T(8,128)(2,1)S(1)}, bf16[2,3,4,16,2048]{4,3,2,1,0:T(8,128)(2,1)S(1)}, u32[]{:S(2)}, u32[]{:S(2)}) collective-permute-start(bf16[2,3,4,16,2048]{4,3,2,1,0:T(8,128)(2,1)S(1)} %get-tuple-element.31), channel_id=1, source_target_pairs={{0,96},{1,25},{2,98},{3,27},{4,100},{5,29},{6,102},{7,31},{8,104},... | collective-permute-start | bytes 4718600 | tf_op jit(solution)/shard_map/ppermute | solution.py:38
  6.4 2.6 %shard_map.56 = (bf16[2,3,4,16,2048]{4,3,2,1,0:T(8,128)(2,1)S(1)}, bf16[2,3,4,16,2048]{4,3,2,1,0:T(8,128)(2,1)S(1)}) custom-call(s32[3]{0:T(128)S(1)} %pad_add_fusion.2.ids, bf16[3,16,2,16,4096]{4,3,2,1,0:T(8,128)(2,1)} %bitcast.12, bf16[2,3,4,16,2048]{4,3,2,1,0:T(8,128)(2,1)S(1)} %get-tuple-element.27.refs_1_), custom_call_target="tpu_custom_call" | custom-call | flops 1 | bytes 4 | tf_op jit(solution)/shard_map/pallas_call | solution.py:69
  9.0 2.7 %collective-permute-start.5 = (bf16[2,3,4,16,2048]{4,3,2,1,0:T(8,128)(2,1)S(1)}, bf16[2,3,4,16,2048]{4,3,2,1,0:T(8,128)(2,1)S(1)}, u32[]{:S(2)}, u32[]{:S(2)}) collective-permute-start(bf16[2,3,4,16,2048]{4,3,2,1,0:T(8,128)(2,1)S(1)} %get-tuple-element.36), channel_id=1, source_target_pairs={{0,96},{1,25},{2,98},{3,27},{4,100},{5,29},{6,102},{7,31},{8,104},... | collective-permute-start | bytes 4718600 | tf_op jit(solution)/shard_map/ppermute | solution.py:38
  11.8 2.6 %shard_map.57 = (bf16[2,3,4,16,2048]{4,3,2,1,0:T(8,128)(2,1)S(1)}, bf16[2,3,4,16,2048]{4,3,2,1,0:T(8,128)(2,1)S(1)}) custom-call(s32[3]{0:T(128)S(1)} %pad_add_fusion.2.ids, bf16[3,16,2,16,4096]{4,3,2,1,0:T(8,128)(2,1)} %bitcast.13, bf16[2,3,4,16,2048]{4,3,2,1,0:T(8,128)(2,1)S(1)} %get-tuple-element.28.refs_1_), custom_call_target="tpu_custom_call" | custom-call | flops 1 | bytes 4 | tf_op jit(solution)/shard_map/pallas_call | solution.py:69
  14.4 2.6 %shard_map.58 = (bf16[2,3,4,16,2048]{4,3,2,1,0:T(8,128)(2,1)S(1)}, bf16[2,3,4,16,2048]{4,3,2,1,0:T(8,128)(2,1)S(1)}) custom-call(s32[3]{0:T(128)S(1)} %pad_add_fusion.2.ids, bf16[3,16,2,16,4096]{4,3,2,1,0:T(8,128)(2,1)} %bitcast.14, bf16[2,3,4,16,2048]{4,3,2,1,0:T(8,128)(2,1)S(1)} %get-tuple-element.29.refs_1_.refs_0_), custom_call_target="tpu_custom_call" | custom-call | flops 1 | bytes 4 | tf_op jit(solution)/shard_map/pallas_call | solution.py:69
  17.1 6.7 %collective-permute-done.1.refs_3_ = bf16[2,3,4,16,2048]{4,3,2,1,0:T(8,128)(2,1)S(1)} collective-permute-done((bf16[2,3,4,16,2048]{4,3,2,1,0:T(8,128)(2,1)S(1)}, bf16[2,3,4,16,2048]{4,3,2,1,0:T(8,128)(2,1)S(1)}, u32[]{:S(2)}, u32[]{:S(2)}) %collective-permute-start.1) | collective-permute-done | bytes 1572896 | tf_op jit(solution)/shard_map/ppermute | solution.py:38
  23.7 3.4 %collective-permute-done.refs_2_ = bf16[2,3,4,16,2048]{4,3,2,1,0:T(8,128)(2,1)S(1)} collective-permute-done((bf16[2,3,4,16,2048]{4,3,2,1,0:T(8,128)(2,1)S(1)}, bf16[2,3,4,16,2048]{4,3,2,1,0:T(8,128)(2,1)S(1)}, u32[]{:S(2)}, u32[]{:S(2)}) %collective-permute-start) | collective-permute-done | bytes 1572896 | tf_op jit(solution)/shard_map/ppermute | solution.py:38
  28.2 1.5 collective-permute-start.3
  29.6 10.9 %collective-permute-done.5.refs_3_ = bf16[2,3,4,16,2048]{4,3,2,1,0:T(8,128)(2,1)S(1)} collective-permute-done((bf16[2,3,4,16,2048]{4,3,2,1,0:T(8,128)(2,1)S(1)}, bf16[2,3,4,16,2048]{4,3,2,1,0:T(8,128)(2,1)S(1)}, u32[]{:S(2)}, u32[]{:S(2)}) %collective-permute-start.5) | collective-permute-done | bytes 1572896 | tf_op jit(solution)/shard_map/ppermute | solution.py:38
  40.6 3.4 %collective-permute-done.4.refs_2_ = bf16[2,3,4,16,2048]{4,3,2,1,0:T(8,128)(2,1)S(1)} collective-permute-done((bf16[2,3,4,16,2048]{4,3,2,1,0:T(8,128)(2,1)S(1)}, bf16[2,3,4,16,2048]{4,3,2,1,0:T(8,128)(2,1)S(1)}, u32[]{:S(2)}, u32[]{:S(2)}) %collective-permute-start.4) | collective-permute-done | bytes 1572896 | tf_op jit(solution)/shard_map/ppermute | solution.py:38
  45.0 1.5 collective-permute-start.10
  46.5 2.5 %collective-permute-done.2.refs_4_ = bf16[3,4,16,2048]{3,2,1,0:T(8,128)(2,1)S(1)} collective-permute-done((bf16[3,4,16,2048]{3,2,1,0:T(8,128)(2,1)S(1)}, bf16[3,4,16,2048]{3,2,1,0:T(8,128)(2,1)S(1)}, u32[]{:S(2)}, u32[]{:S(2)}) %collective-permute-start.2) | collective-permute-done | bytes 786464 | tf_op jit(solution)/shard_map/ppermute | solution.py:38
  49.0 3.4 %collective-permute-done.3.refs_5_ = bf16[3,4,16,2048]{3,2,1,0:T(8,128)(2,1)S(1)} collective-permute-done((bf16[3,4,16,2048]{3,2,1,0:T(8,128)(2,1)S(1)}, bf16[3,4,16,2048]{3,2,1,0:T(8,128)(2,1)S(1)}, u32[]{:S(2)}, u32[]{:S(2)}) %collective-permute-start.3) | collective-permute-done | bytes 786464 | tf_op jit(solution)/shard_map/ppermute | solution.py:38
  52.4 1.6 %shard_map.61 = (bf16[3,16,4096]{2,1,0:T(8,128)(2,1)S(1)}, bf16[3,16,4096]{2,1,0:T(8,128)(2,1)S(1)}, bf16[3,16,4096]{2,1,0:T(8,128)(2,1)S(1)}, bf16[3,16,4096]{2,1,0:T(8,128)(2,1)S(1)}) custom-call(s32[3]{0:T(128)S(1)} %pad_add_fusion.2.ids, bf16[2,3,4,16,2048]{4,3,2,1,0:T(8,128)(2,1)S(1)} %get-tuple-element.29.refs_1_.refs_0_, ...), custom_call_target="tpu_custom_call" | custom-call | flops 1 | bytes 4 | tf_op jit(solution)/shard_map/pallas_call | solution.py:69
  54.0 2.5 %collective-permute-start.6 = (bf16[3,16,4096]{2,1,0:T(8,128)(2,1)S(1)}, bf16[3,16,4096]{2,1,0:T(8,128)(2,1)S(1)}, u32[]{:S(2)}, u32[]{:S(2)}) collective-permute-start(bf16[3,16,4096]{2,1,0:T(8,128)(2,1)S(1)} %get-tuple-element.39), channel_id=1, source_target_pairs={{0,24},{1,97},{2,26},{3,99},{4,28},{5,101},{6,30},{7,103},{8,0},{9... | collective-permute-start | bytes 1179656 | tf_op jit(solution)/shard_map/ppermute | solution.py:38
  56.6 1.4 collective-permute-start.8
  58.0 2.8 %collective-permute-done.10.refs_5_ = bf16[3,4,16,2048]{3,2,1,0:T(8,128)(2,1)S(1)} collective-permute-done((bf16[3,4,16,2048]{3,2,1,0:T(8,128)(2,1)S(1)}, bf16[3,4,16,2048]{3,2,1,0:T(8,128)(2,1)S(1)}, u32[]{:S(2)}, u32[]{:S(2)}) %collective-permute-start.10) | collective-permute-done | bytes 786464 | tf_op jit(solution)/shard_map/ppermute | solution.py:38
  60.8 1.6 %shard_map.62 = (bf16[3,16,4096]{2,1,0:T(8,128)(2,1)S(1)}, bf16[3,16,4096]{2,1,0:T(8,128)(2,1)S(1)}, bf16[3,16,4096]{2,1,0:T(8,128)(2,1)S(1)}, bf16[3,16,4096]{2,1,0:T(8,128)(2,1)S(1)}) custom-call(s32[3]{0:T(128)S(1)} %pad_add_fusion.2.ids, bf16[2,3,4,16,2048]{4,3,2,1,0:T(8,128)(2,1)S(1)} %get-tuple-element.32.refs_4_.refs_0_, ...), custom_call_target="tpu_custom_call" | custom-call | flops 1 | bytes 4 | tf_op jit(solution)/shard_map/pallas_call | solution.py:69
  62.5 3.0 %collective-permute-start.14 = (bf16[3,16,4096]{2,1,0:T(8,128)(2,1)S(1)}, bf16[3,16,4096]{2,1,0:T(8,128)(2,1)S(1)}, u32[]{:S(2)}, u32[]{:S(2)}) collective-permute-start(bf16[3,16,4096]{2,1,0:T(8,128)(2,1)S(1)} %get-tuple-element.45), channel_id=1, source_target_pairs={{0,24},{1,97},{2,26},{3,99},{4,28},{5,101},{6,30},{7,103},{8,0},{9... | collective-permute-start | bytes 1179656 | tf_op jit(solution)/shard_map/ppermute | solution.py:38
  67.9 2.5 %collective-permute-done.7.refs_2_ = bf16[3,16,4096]{2,1,0:T(8,128)(2,1)S(1)} collective-permute-done((bf16[3,16,4096]{2,1,0:T(8,128)(2,1)S(1)}, bf16[3,16,4096]{2,1,0:T(8,128)(2,1)S(1)}, u32[]{:S(2)}, u32[]{:S(2)}) %collective-permute-start.7) | collective-permute-done | bytes 393248 | tf_op jit(solution)/shard_map/ppermute | solution.py:38
  71.7 1.7 %collective-permute-start.13 = (bf16[96,16,128]{2,1,0:T(8,128)(2,1)S(1)}, bf16[96,16,128]{2,1,0:T(8,128)(2,1)S(1)}, u32[]{:S(2)}, u32[]{:S(2)}) collective-permute-start(bf16[96,16,128]{2,1,0:T(8,128)(2,1)S(1)} %get-tuple-element.44.refs_6_.refs_0_), channel_id=1, source_target_pairs={{0,2},{1,3},{2,4},{3,5},{4,6},{5,7},{6,0},{7,1},{8,10},{9,11},{10,... | collective-permute-start | bytes 1179656 | tf_op jit(solution)/shard_map/ppermute | solution.py:38
  73.4 3.3 %collective-permute-start.12 = (bf16[96,16,128]{2,1,0:T(8,128)(2,1)S(1)}, bf16[96,16,128]{2,1,0:T(8,128)(2,1)S(1)}, u32[]{:S(2)}, u32[]{:S(2)}) collective-permute-start(bf16[96,16,128]{2,1,0:T(8,128)(2,1)S(1)} %get-tuple-element.44.refs_6_.refs_0_), channel_id=1, source_target_pairs={{0,4},{1,5},{2,6},{3,7},{4,0},{5,1},{6,2},{7,3},{8,12},{9,13},{10,... | collective-permute-start | bytes 1179656 | tf_op jit(solution)/shard_map/ppermute | solution.py:38
  78.6 1.3 shard_map.64.refs_4_.refs_8_
  79.8 1.7 %collective-permute-start.19 = (bf16[97,16,128]{2,1,0:T(8,128)(2,1)S(1)}, bf16[97,16,128]{2,1,0:T(8,128)(2,1)S(1)}, u32[]{:S(2)}, u32[]{:S(2)}) collective-permute-start(bf16[97,16,128]{2,1,0:T(8,128)(2,1)S(1)} %shard_map.64.refs_4_.refs_8_), channel_id=1, source_target_pairs={{0,2},{1,3},{2,4},{3,5},{4,6},{5,7},{6,0},{7,1},{8,10},{9,11},{10,... | collective-permute-start | bytes 1191944 | tf_op jit(solution)/shard_map/ppermute | solution.py:38
  81.5 3.3 %collective-permute-start.18 = (bf16[97,16,128]{2,1,0:T(8,128)(2,1)S(1)}, bf16[97,16,128]{2,1,0:T(8,128)(2,1)S(1)}, u32[]{:S(2)}, u32[]{:S(2)}) collective-permute-start(bf16[97,16,128]{2,1,0:T(8,128)(2,1)S(1)} %shard_map.64.refs_4_.refs_8_), channel_id=1, source_target_pairs={{0,4},{1,5},{2,6},{3,7},{4,0},{5,1},{6,2},{7,3},{8,12},{9,13},{10,... | collective-permute-start | bytes 1191944 | tf_op jit(solution)/shard_map/ppermute | solution.py:38
  86.3 8.8 %collective-permute-done.19.refs_7_ = bf16[97,16,128]{2,1,0:T(8,128)(2,1)S(1)} collective-permute-done((bf16[97,16,128]{2,1,0:T(8,128)(2,1)S(1)}, bf16[97,16,128]{2,1,0:T(8,128)(2,1)S(1)}, u32[]{:S(2)}, u32[]{:S(2)}) %collective-permute-start.19) | collective-permute-done | bytes 397344 | tf_op jit(solution)/shard_map/ppermute | solution.py:38
  95.1 7.8 %collective-permute-done.18.refs_6_ = bf16[97,16,128]{2,1,0:T(8,128)(2,1)S(1)} collective-permute-done((bf16[97,16,128]{2,1,0:T(8,128)(2,1)S(1)}, bf16[97,16,128]{2,1,0:T(8,128)(2,1)S(1)}, u32[]{:S(2)}, u32[]{:S(2)}) %collective-permute-start.18) | collective-permute-done | bytes 397344 | tf_op jit(solution)/shard_map/ppermute | solution.py:38
  103.0 2.5 %shard_map.65 = bf16[32,17,16,128]{3,2,1,0:T(8,128)(2,1)} custom-call(s32[64]{0:T(128)S(1)} %reshape.234.ids, bf16[96,16,128]{2,1,0:T(8,128)(2,1)S(1)} %get-tuple-element.44.refs_6_.refs_0_, bf16[96,16,128]{2,1,0:T(8,128)(2,1)S(1)} %collective-permute-done.11.refs_1_, bf16[96,16,128]{2,1,0:T(8,128)(2,1)S(1)} %collective-permute-done.12.refs_2_, ...), custom_call_target="tpu_custom_call" | custom-call | flops 1 | bytes 4 | tf_op jit(solution)/shard_map/pallas_call | solution.py:69
  105.5 13.9 %all-to-all-start = ((bf16[32,17,16,128]{3,2,1,0:T(8,128)(2,1)}), bf16[32,17,16,128]{3,2,1,0:T(8,128)(2,1)S(1)}, u32[]{:S(2)}, u32[]{:S(2)}) async-start(bf16[32,17,16,128]{3,2,1,0:T(8,128)(2,1)} %shard_map.65), calls=%async_computation | async-start | bytes 4456448 | tf_op jit(solution)/shard_map/all_to_all | solution.py:376
  124.0 25.1 %all-to-all-done = bf16[32,17,16,128]{3,2,1,0:T(8,128)(2,1)S(1)} async-done(((bf16[32,17,16,128]{3,2,1,0:T(8,128)(2,1)}), bf16[32,17,16,128]{3,2,1,0:T(8,128)(2,1)S(1)}, u32[]{:S(2)}, u32[]{:S(2)}) %all-to-all-start) | async-done | bytes 2228256 | tf_op jit(solution)/shard_map/all_to_all | solution.py:376
  149.0 8.2 %shard_map.66 = bf16[1,1024,1024]{2,1,0:T(8,128)(2,1)} custom-call(s32[2]{0:T(128)S(1)} %pad_add_fusion.1.ids, bf16[16,2,17,16,128]{4,3,2,1,0:T(8,128)(2,1)S(1)} %bitcast.8, bf16[1,1024,1024]{2,1,0:T(8,128)(2,1)} %refs_1_.1, bf16[1,1024,1024]{2,1,0:T(8,128)(2,1)} %refs_2_.1), custom_call_target="tpu_custom_call" | custom-call | flops 1048576 | bytes 4194304 | tf_op jit(solution)/shard_map/pallas_call | solution.py:69
  (38 shorter events, 11.1 us)
Async XLA Ops:
  2.7 21.0 %collective-permute-start.1 = (bf16[2,3,4,16,2048]{4,3,2,1,0:T(8,128)(2,1)S(1)}, bf16[2,3,4,16,2048]{4,3,2,1,0:T(8,128)(2,1)S(1)}, u32[]{:S(2)}, u32[]{:S(2)}) collective-permute-start(bf16[2,3,4,16,2048]{4,3,2,1,0:T(8,128)(2,1)S(1)} %get-tuple-element.31), channel_id=1, source_target_pairs={{0,96},{1,25},{2,98},{3,27},{4,100},{5,29},{6,102},{7,31},{8,104},... | collective-permute-start | bytes 4718600 | tf_op jit(solution)/shard_map/ppermute | solution.py:38
  6.4 20.8 %collective-permute-start = (bf16[2,3,4,16,2048]{4,3,2,1,0:T(8,128)(2,1)S(1)}, bf16[2,3,4,16,2048]{4,3,2,1,0:T(8,128)(2,1)S(1)}, u32[]{:S(2)}, u32[]{:S(2)}) collective-permute-start(bf16[2,3,4,16,2048]{4,3,2,1,0:T(8,128)(2,1)S(1)} %get-tuple-element.27.refs_1_), channel_id=1, source_target_pairs={{0,32},{1,9},{2,34},{3,11},{4,36},{5,13},{6,38},{7,15},{8,40},{9,1... | collective-permute-start | bytes 4718600 | tf_op jit(solution)/shard_map/ppermute | solution.py:38
  9.0 31.6 %collective-permute-start.5 = (bf16[2,3,4,16,2048]{4,3,2,1,0:T(8,128)(2,1)S(1)}, bf16[2,3,4,16,2048]{4,3,2,1,0:T(8,128)(2,1)S(1)}, u32[]{:S(2)}, u32[]{:S(2)}) collective-permute-start(bf16[2,3,4,16,2048]{4,3,2,1,0:T(8,128)(2,1)S(1)} %get-tuple-element.36), channel_id=1, source_target_pairs={{0,96},{1,25},{2,98},{3,27},{4,100},{5,29},{6,102},{7,31},{8,104},... | collective-permute-start | bytes 4718600 | tf_op jit(solution)/shard_map/ppermute | solution.py:38
  11.8 32.2 %collective-permute-start.4 = (bf16[2,3,4,16,2048]{4,3,2,1,0:T(8,128)(2,1)S(1)}, bf16[2,3,4,16,2048]{4,3,2,1,0:T(8,128)(2,1)S(1)}, u32[]{:S(2)}, u32[]{:S(2)}) collective-permute-start(bf16[2,3,4,16,2048]{4,3,2,1,0:T(8,128)(2,1)S(1)} %get-tuple-element.28.refs_1_), channel_id=1, source_target_pairs={{0,32},{1,9},{2,34},{3,11},{4,36},{5,13},{6,38},{7,15},{8,40},{9,1... | collective-permute-start | bytes 4718600 | tf_op jit(solution)/shard_map/ppermute | solution.py:38
  28.1 20.9 %collective-permute-start.2 = (bf16[3,4,16,2048]{3,2,1,0:T(8,128)(2,1)S(1)}, bf16[3,4,16,2048]{3,2,1,0:T(8,128)(2,1)S(1)}, u32[]{:S(2)}, u32[]{:S(2)}) collective-permute-start(bf16[3,4,16,2048]{3,2,1,0:T(8,128)(2,1)S(1)} %get-tuple-element.33), channel_id=1, source_target_pairs={{0,96},{1,25},{2,98},{3,27},{4,100},{5,29},{6,102},{7,31},{8,104},... | collective-permute-start | bytes 2359304 | tf_op jit(solution)/shard_map/ppermute | solution.py:38
  28.2 24.2 %collective-permute-start.3 = (bf16[3,4,16,2048]{3,2,1,0:T(8,128)(2,1)S(1)}, bf16[3,4,16,2048]{3,2,1,0:T(8,128)(2,1)S(1)}, u32[]{:S(2)}, u32[]{:S(2)}) collective-permute-start(bf16[3,4,16,2048]{3,2,1,0:T(8,128)(2,1)S(1)} %get-tuple-element.34.refs_4_), channel_id=1, source_target_pairs={{0,32},{1,9},{2,34},{3,11},{4,36},{5,13},{6,38},{7,15},{8,40},{9,1... | collective-permute-start | bytes 2359304 | tf_op jit(solution)/shard_map/ppermute | solution.py:38
  45.0 13.1 %collective-permute-start.9 = (bf16[3,4,16,2048]{3,2,1,0:T(8,128)(2,1)S(1)}, bf16[3,4,16,2048]{3,2,1,0:T(8,128)(2,1)S(1)}, u32[]{:S(2)}, u32[]{:S(2)}) collective-permute-start(bf16[3,4,16,2048]{3,2,1,0:T(8,128)(2,1)S(1)} %get-tuple-element.42), channel_id=1, source_target_pairs={{0,96},{1,25},{2,98},{3,27},{4,100},{5,29},{6,102},{7,31},{8,104},... | collective-permute-start | bytes 2359304 | tf_op jit(solution)/shard_map/ppermute | solution.py:38
  45.0 15.8 %collective-permute-start.10 = (bf16[3,4,16,2048]{3,2,1,0:T(8,128)(2,1)S(1)}, bf16[3,4,16,2048]{3,2,1,0:T(8,128)(2,1)S(1)}, u32[]{:S(2)}, u32[]{:S(2)}) collective-permute-start(bf16[3,4,16,2048]{3,2,1,0:T(8,128)(2,1)S(1)} %get-tuple-element.37.refs_6_), channel_id=1, source_target_pairs={{0,32},{1,9},{2,34},{3,11},{4,36},{5,13},{6,38},{7,15},{8,40},{9,1... | collective-permute-start | bytes 2359304 | tf_op jit(solution)/shard_map/ppermute | solution.py:38
  54.0 12.7 %collective-permute-start.6 = (bf16[3,16,4096]{2,1,0:T(8,128)(2,1)S(1)}, bf16[3,16,4096]{2,1,0:T(8,128)(2,1)S(1)}, u32[]{:S(2)}, u32[]{:S(2)}) collective-permute-start(bf16[3,16,4096]{2,1,0:T(8,128)(2,1)S(1)} %get-tuple-element.39), channel_id=1, source_target_pairs={{0,24},{1,97},{2,26},{3,99},{4,28},{5,101},{6,30},{7,103},{8,0},{9... | collective-permute-start | bytes 1179656 | tf_op jit(solution)/shard_map/ppermute | solution.py:38
  56.6 13.8 %collective-permute-start.7 = (bf16[3,16,4096]{2,1,0:T(8,128)(2,1)S(1)}, bf16[3,16,4096]{2,1,0:T(8,128)(2,1)S(1)}, u32[]{:S(2)}, u32[]{:S(2)}) collective-permute-start(bf16[3,16,4096]{2,1,0:T(8,128)(2,1)S(1)} %get-tuple-element.40), channel_id=1, source_target_pairs={{0,8},{1,33},{2,10},{3,35},{4,12},{5,37},{6,14},{7,39},{8,16},{9,4... | collective-permute-start | bytes 1179656 | tf_op jit(solution)/shard_map/ppermute | solution.py:38
  56.6 13.8 %collective-permute-start.8 = (bf16[3,16,4096]{2,1,0:T(8,128)(2,1)S(1)}, bf16[3,16,4096]{2,1,0:T(8,128)(2,1)S(1)}, u32[]{:S(2)}, u32[]{:S(2)}) collective-permute-start(bf16[3,16,4096]{2,1,0:T(8,128)(2,1)S(1)} %get-tuple-element.41), channel_id=1, source_target_pairs={{0,16},{1,65},{2,18},{3,67},{4,20},{5,69},{6,22},{7,71},{8,24},{9,... | collective-permute-start | bytes 1179656 | tf_op jit(solution)/shard_map/ppermute | solution.py:38
  60.8 9.6 %copy-start = (f32[3,32,4096]{2,1,0:T(8,128)S(1)}, f32[3,32,4096]{2,1,0:T(8,128)}, u32[]{:S(2)}) copy-start(f32[3,32,4096]{2,1,0:T(8,128)} %param.6) | copy-start | bytes 4718596
  62.5 14.2 %collective-permute-start.14 = (bf16[3,16,4096]{2,1,0:T(8,128)(2,1)S(1)}, bf16[3,16,4096]{2,1,0:T(8,128)(2,1)S(1)}, u32[]{:S(2)}, u32[]{:S(2)}) collective-permute-start(bf16[3,16,4096]{2,1,0:T(8,128)(2,1)S(1)} %get-tuple-element.45), channel_id=1, source_target_pairs={{0,24},{1,97},{2,26},{3,99},{4,28},{5,101},{6,30},{7,103},{8,0},{9... | collective-permute-start | bytes 1179656 | tf_op jit(solution)/shard_map/ppermute | solution.py:38
  65.5 13.1 %collective-permute-start.15 = (bf16[3,16,4096]{2,1,0:T(8,128)(2,1)S(1)}, bf16[3,16,4096]{2,1,0:T(8,128)(2,1)S(1)}, u32[]{:S(2)}, u32[]{:S(2)}) collective-permute-start(bf16[3,16,4096]{2,1,0:T(8,128)(2,1)S(1)} %get-tuple-element.46), channel_id=1, source_target_pairs={{0,8},{1,33},{2,10},{3,35},{4,12},{5,37},{6,14},{7,39},{8,16},{9,4... | collective-permute-start | bytes 1179656 | tf_op jit(solution)/shard_map/ppermute | solution.py:38
  66.7 11.8 %collective-permute-start.16 = (bf16[3,16,4096]{2,1,0:T(8,128)(2,1)S(1)}, bf16[3,16,4096]{2,1,0:T(8,128)(2,1)S(1)}, u32[]{:S(2)}, u32[]{:S(2)}) collective-permute-start(bf16[3,16,4096]{2,1,0:T(8,128)(2,1)S(1)} %get-tuple-element.47), channel_id=1, source_target_pairs={{0,16},{1,65},{2,18},{3,67},{4,20},{5,69},{6,22},{7,71},{8,24},{9,... | collective-permute-start | bytes 1179656 | tf_op jit(solution)/shard_map/ppermute | solution.py:38
  71.7 13.2 %collective-permute-start.13 = (bf16[96,16,128]{2,1,0:T(8,128)(2,1)S(1)}, bf16[96,16,128]{2,1,0:T(8,128)(2,1)S(1)}, u32[]{:S(2)}, u32[]{:S(2)}) collective-permute-start(bf16[96,16,128]{2,1,0:T(8,128)(2,1)S(1)} %get-tuple-element.44.refs_6_.refs_0_), channel_id=1, source_target_pairs={{0,2},{1,3},{2,4},{3,5},{4,6},{5,7},{6,0},{7,1},{8,10},{9,11},{10,... | collective-permute-start | bytes 1179656 | tf_op jit(solution)/shard_map/ppermute | solution.py:38
  73.4 13.0 %collective-permute-start.12 = (bf16[96,16,128]{2,1,0:T(8,128)(2,1)S(1)}, bf16[96,16,128]{2,1,0:T(8,128)(2,1)S(1)}, u32[]{:S(2)}, u32[]{:S(2)}) collective-permute-start(bf16[96,16,128]{2,1,0:T(8,128)(2,1)S(1)} %get-tuple-element.44.refs_6_.refs_0_), channel_id=1, source_target_pairs={{0,4},{1,5},{2,6},{3,7},{4,0},{5,1},{6,2},{7,3},{8,12},{9,13},{10,... | collective-permute-start | bytes 1179656 | tf_op jit(solution)/shard_map/ppermute | solution.py:38
  76.7 9.7 %collective-permute-start.11 = (bf16[96,16,128]{2,1,0:T(8,128)(2,1)S(1)}, bf16[96,16,128]{2,1,0:T(8,128)(2,1)S(1)}, u32[]{:S(2)}, u32[]{:S(2)}) collective-permute-start(bf16[96,16,128]{2,1,0:T(8,128)(2,1)S(1)} %get-tuple-element.44.refs_6_.refs_0_), channel_id=1, source_target_pairs={{0,6},{1,7},{2,0},{3,1},{4,2},{5,3},{6,4},{7,5},{8,14},{9,15},{10,... | collective-permute-start | bytes 1179656 | tf_op jit(solution)/shard_map/ppermute | solution.py:38
  78.6 7.0 %copy-start.1 = (s32[48]{0:T(128)S(1)}, s32[48]{0:T(128)}, u32[]{:S(2)}) copy-start(s32[48]{0:T(128)} %param.9) | copy-start | bytes 580
  79.8 15.3 %collective-permute-start.19 = (bf16[97,16,128]{2,1,0:T(8,128)(2,1)S(1)}, bf16[97,16,128]{2,1,0:T(8,128)(2,1)S(1)}, u32[]{:S(2)}, u32[]{:S(2)}) collective-permute-start(bf16[97,16,128]{2,1,0:T(8,128)(2,1)S(1)} %shard_map.64.refs_4_.refs_8_), channel_id=1, source_target_pairs={{0,2},{1,3},{2,4},{3,5},{4,6},{5,7},{6,0},{7,1},{8,10},{9,11},{10,... | collective-permute-start | bytes 1191944 | tf_op jit(solution)/shard_map/ppermute | solution.py:38
  81.5 21.4 %collective-permute-start.18 = (bf16[97,16,128]{2,1,0:T(8,128)(2,1)S(1)}, bf16[97,16,128]{2,1,0:T(8,128)(2,1)S(1)}, u32[]{:S(2)}, u32[]{:S(2)}) collective-permute-start(bf16[97,16,128]{2,1,0:T(8,128)(2,1)S(1)} %shard_map.64.refs_4_.refs_8_), channel_id=1, source_target_pairs={{0,4},{1,5},{2,6},{3,7},{4,0},{5,1},{6,2},{7,3},{8,12},{9,13},{10,... | collective-permute-start | bytes 1191944 | tf_op jit(solution)/shard_map/ppermute | solution.py:38
  84.9 18.1 %collective-permute-start.17 = (bf16[97,16,128]{2,1,0:T(8,128)(2,1)S(1)}, bf16[97,16,128]{2,1,0:T(8,128)(2,1)S(1)}, u32[]{:S(2)}, u32[]{:S(2)}) collective-permute-start(bf16[97,16,128]{2,1,0:T(8,128)(2,1)S(1)} %shard_map.64.refs_4_.refs_8_), channel_id=1, source_target_pairs={{0,6},{1,7},{2,0},{3,1},{4,2},{5,3},{6,4},{7,5},{8,14},{9,15},{10,... | collective-permute-start | bytes 1191944 | tf_op jit(solution)/shard_map/ppermute | solution.py:38
  105.5 43.6 %all-to-all-start = ((bf16[32,17,16,128]{3,2,1,0:T(8,128)(2,1)}), bf16[32,17,16,128]{3,2,1,0:T(8,128)(2,1)S(1)}, u32[]{:S(2)}, u32[]{:S(2)}) async-start(bf16[32,17,16,128]{3,2,1,0:T(8,128)(2,1)} %shard_map.65), calls=%async_computation | async-start | bytes 4456448 | tf_op jit(solution)/shard_map/all_to_all | solution.py:376

commit v7 on v6

--- a/solution.py
+++ b/solution.py
@@ -11,6 +11,7 @@
 SIDE = 4
 CHUNKS = 2
 LANES = 128
+TILES = 17
 PIECES = 12
 VMEM_LIMIT = 12 * 1024 * 1024
 VMEM_MOST = 20 * 1024 * 1024
@@ -50,7 +51,7 @@
     return pltpu.with_memory_space_constraint(value, pltpu.VMEM)
 
 
-def call(kernel, out_shape, grid, in_specs, out_specs, scratch=(), cost=1, after=(), grant=VMEM_MOST):
+def call(kernel, out_shape, grid, in_specs, out_specs, scratch=(), cost=1, after=(), grant=VMEM_MOST, aliases=()):
     inputs = len(in_specs)
     in_specs = list(in_specs) + [pl.BlockSpec(memory_space=pl.ANY)] * len(after)
 
@@ -63,6 +64,7 @@
         grid_spec=pltpu.PrefetchScalarGridSpec(
             num_scalar_prefetch=1, grid=grid, in_specs=in_specs, out_specs=out_specs, scratch_shapes=list(scratch)
         ),
+        input_output_aliases=dict(aliases),
         compiler_params=pltpu.CompilerParams(vmem_limit_bytes=grant),
         cost_estimate=pl.CostEstimate(flops=cost, bytes_accessed=4 * cost, transcendentals=0),
     )
@@ -203,41 +205,41 @@
     )(ids, *sums, moment, *earlier)
 
 
-def choose(picks, held, after):
+def choose(picks, held, filled, start, after):
     slots = picks.shape[0] // 2
-    count = len(held[0])
-    total, rows, _ = held[0][0].shape
-    tiles = total // PIECES
+    total, rows, _ = held[0].shape
+    tiles, extra = divmod(total, PIECES)
 
     def kernel(picks, *refs):
-        first, second, out, staged, sem = refs[:count], refs[count : 2 * count], *refs[2 * count :]
-
-        @pl.loop(0, slots)
+        sources, (out, staged, sem) = refs[: len(held)], refs[-3:]
+
+        @pl.loop(0, slots, unroll=4)
         def _(slot):
             piece = pl.ds(picks[2 * slot + 1] * tiles, tiles)
-            for number in range(count):
+            for number, source in enumerate(sources):
 
                 @pl.when(picks[2 * slot] == number)
-                def _(number=number):
-                    staged[slot, :tiles] = first[number][piece]
-                    staged[slot, tiles : 2 * tiles] = second[number][piece]
-                    staged[slot, 2 * tiles] = second[number][total]
-
-            pltpu.make_async_copy(staged.at[slot], out.at[slot], sem).start()
-
-        pltpu.make_async_copy(staged, out, sem).wait()
-
-    shape = (slots, 2 * tiles + 1, rows, LANES)
-    return call(
-        kernel,
-        jax.ShapeDtypeStruct(shape, BF16),
+                def _(source=source):
+                    staged[slot, :tiles] = source[piece]
+                    if extra:
+                        staged[slot, tiles] = source[total - 1]
+
+            pltpu.make_async_copy(staged.at[slot], out.at[slot, pl.ds(start, tiles + extra)], sem).start()
+
+        pltpu.make_async_copy(staged, out.at[:, pl.ds(start, tiles + extra)], sem).wait()
+
+    anywhere = pl.BlockSpec(memory_space=pl.ANY)
+    return call(
+        kernel,
+        jax.ShapeDtypeStruct((slots, TILES, rows, LANES), BF16),
         (1,),
-        [pl.BlockSpec(memory_space=pltpu.VMEM)] * (2 * count),
-        pl.BlockSpec(memory_space=pl.ANY),
-        [pltpu.VMEM(shape, BF16), pltpu.SemaphoreType.DMA],
+        [pl.BlockSpec(memory_space=pltpu.VMEM)] * len(held) + [anywhere] * len(filled),
+        anywhere,
+        [pltpu.VMEM((slots, tiles + extra, rows, LANES), BF16), pltpu.SemaphoreType.DMA],
         after=after,
         grant=VMEM_LIMIT,
-    )(picks, *(in_vmem(value) for value in (*held[0], *held[1])))
+        aliases=[(1 + len(held), 0)] if filled else (),
+    )(picks, *(in_vmem(value) for value in held), *filled)
 
 
 def finish(ids, received, left_root, right_root, block):
@@ -372,7 +374,8 @@
         pieces, *power = second_sum(ids, sums[chunk], known, chunk, block, power, last)
         last = (pieces,)
         held.append([pieces] + [send(pieces, lambda core, k=k: (0, 0, -k, 0)) for k in (1, 2, 3)])
-    outgoing = choose(picks, held, last)
+    outgoing = choose(picks, held[0], (), 0, last)
+    outgoing = choose(picks, held[1], (outgoing,), TILES // 2, ())
     received = lax.all_to_all(outgoing, ("dp", "core"), 0, 0, tiled=True)
     received = received.reshape((dp_count, 2) + received.shape[1:])
     left, right = (pltpu.with_memory_space_constraint(value, pltpu.HBM) for value in (left_roots, right_roots))

time: 158 us -> 158 us (level)
  waiting for transfers between devices: 79.9 us -> 77.6 us
  Pallas kernels: 28.9 us -> 31.1 us
    ppermute x20, waiting for transfers between devices: 54.9 us -> 52.6 us  [send(): return lax.ppermute(value, ('dp', 'z', 'core'), routes(move))]
    pallas_call x12 -> x13, Pallas kernels: 28.9 us -> 31.1 us  [call(): return lambda *operands: made(*operands, *after)]
  transfers between devices with their start and end apart: 21 -> 21, of which waited for: 14 -> 14; matrix products, arithmetic and copies ran while one was open for 2% -> 2% of each run, Pallas kernels for 10% -> 11%
where the time goes in v7:
time: 158 us; the launch traced here: 157 us
  waiting for transfers between devices  77.6 us (49%)
  starting transfers between devices  42.9 us (27%)
  Pallas kernels  31.1 us (20%)
  between operations  2.97 us (2%)
  local copies, waits for them, and re-layouts  1.71 us (1%)
    ppermute x20, waiting for transfers between devices, send(): return lax.ppermute(value, ('dp', 'z', 'core'), routes(move))  52.6 us
    pallas_call x13, Pallas kernels, call(): return lambda *operands: made(*operands, *after)  31.1 us
    ppermute x20, starting transfers between devices, send(): return lax.ppermute(value, ('dp', 'z', 'core'), routes(move))  29.1 us
    all_to_all x1, waiting for transfers between devices, shards(): received = lax.all_to_all(outgoing, ('dp', 'core'), 0, 0, tiled=True)  25.1 us
    all_to_all x1, starting transfers between devices, shards(): received = lax.all_to_all(outgoing, ('dp', 'core'), 0, 0, tiled=True)  13.9 us
  transfers between devices with their start and end apart: 21, of which 14 were waited for; matrix products, arithmetic and copies ran while one was open for 2% of the time, Pallas kernels for 11%

profile of v7, /device:TPU:1, one launch (start us, length us, event | category | flops | bytes accessed | tf_op | source)
XLA Modules:
  0.0 157.3 jit_solution(1159155379767634765)
XLA Ops:
  0.1 2.6 %shard_map.55 = (bf16[2,3,4,16,2048]{4,3,2,1,0:T(8,128)(2,1)S(1)}, bf16[2,3,4,16,2048]{4,3,2,1,0:T(8,128)(2,1)S(1)}) custom-call(s32[3]{0:T(128)S(1)} %pad_add_fusion.2.ids, bf16[3,16,2,16,4096]{4,3,2,1,0:T(8,128)(2,1)} %bitcast.11), custom_call_target="tpu_custom_call" | custom-call | flops 1 | bytes 4 | tf_op jit(solution)/shard_map/pallas_call | solution.py:71
  2.7 3.6 %collective-permute-start.3 = (bf16[2,3,4,16,2048]{4,3,2,1,0:T(8,128)(2,1)S(1)}, bf16[2,3,4,16,2048]{4,3,2,1,0:T(8,128)(2,1)S(1)}, u32[]{:S(2)}, u32[]{:S(2)}) collective-permute-start(bf16[2,3,4,16,2048]{4,3,2,1,0:T(8,128)(2,1)S(1)} %get-tuple-element.34), channel_id=1, source_target_pairs={{0,96},{1,25},{2,98},{3,27},{4,100},{5,29},{6,102},{7,31},{8,104},... | collective-permute-start | bytes 4718600 | tf_op jit(solution)/shard_map/ppermute | solution.py:39
  6.4 2.6 %shard_map.56 = (bf16[2,3,4,16,2048]{4,3,2,1,0:T(8,128)(2,1)S(1)}, bf16[2,3,4,16,2048]{4,3,2,1,0:T(8,128)(2,1)S(1)}) custom-call(s32[3]{0:T(128)S(1)} %pad_add_fusion.2.ids, bf16[3,16,2,16,4096]{4,3,2,1,0:T(8,128)(2,1)} %bitcast.12, bf16[2,3,4,16,2048]{4,3,2,1,0:T(8,128)(2,1)S(1)} %get-tuple-element.27.refs_1_), custom_call_target="tpu_custom_call" | custom-call | flops 1 | bytes 4 | tf_op jit(solution)/shard_map/pallas_call | solution.py:71
  9.0 2.7 %collective-permute-start.1 = (bf16[2,3,4,16,2048]{4,3,2,1,0:T(8,128)(2,1)S(1)}, bf16[2,3,4,16,2048]{4,3,2,1,0:T(8,128)(2,1)S(1)}, u32[]{:S(2)}, u32[]{:S(2)}) collective-permute-start(bf16[2,3,4,16,2048]{4,3,2,1,0:T(8,128)(2,1)S(1)} %get-tuple-element.32), channel_id=1, source_target_pairs={{0,96},{1,25},{2,98},{3,27},{4,100},{5,29},{6,102},{7,31},{8,104},... | collective-permute-start | bytes 4718600 | tf_op jit(solution)/shard_map/ppermute | solution.py:39
  11.8 2.6 %shard_map.57 = (bf16[2,3,4,16,2048]{4,3,2,1,0:T(8,128)(2,1)S(1)}, bf16[2,3,4,16,2048]{4,3,2,1,0:T(8,128)(2,1)S(1)}) custom-call(s32[3]{0:T(128)S(1)} %pad_add_fusion.2.ids, bf16[3,16,2,16,4096]{4,3,2,1,0:T(8,128)(2,1)} %bitcast.13, bf16[2,3,4,16,2048]{4,3,2,1,0:T(8,128)(2,1)S(1)} %get-tuple-element.28.refs_1_), custom_call_target="tpu_custom_call" | custom-call | flops 1 | bytes 4 | tf_op jit(solution)/shard_map/pallas_call | solution.py:71
  14.4 2.6 %shard_map.58 = (bf16[2,3,4,16,2048]{4,3,2,1,0:T(8,128)(2,1)S(1)}, bf16[2,3,4,16,2048]{4,3,2,1,0:T(8,128)(2,1)S(1)}) custom-call(s32[3]{0:T(128)S(1)} %pad_add_fusion.2.ids, bf16[3,16,2,16,4096]{4,3,2,1,0:T(8,128)(2,1)} %bitcast.14, bf16[2,3,4,16,2048]{4,3,2,1,0:T(8,128)(2,1)S(1)} %get-tuple-element.29.refs_1_.refs_0_), custom_call_target="tpu_custom_call" | custom-call | flops 1 | bytes 4 | tf_op jit(solution)/shard_map/pallas_call | solution.py:71
  17.1 6.7 %collective-permute-done.3.refs_3_ = bf16[2,3,4,16,2048]{4,3,2,1,0:T(8,128)(2,1)S(1)} collective-permute-done((bf16[2,3,4,16,2048]{4,3,2,1,0:T(8,128)(2,1)S(1)}, bf16[2,3,4,16,2048]{4,3,2,1,0:T(8,128)(2,1)S(1)}, u32[]{:S(2)}, u32[]{:S(2)}) %collective-permute-start.3) | collective-permute-done | bytes 1572896 | tf_op jit(solution)/shard_map/ppermute | solution.py:39
  23.7 3.4 %collective-permute-done.2.refs_2_ = bf16[2,3,4,16,2048]{4,3,2,1,0:T(8,128)(2,1)S(1)} collective-permute-done((bf16[2,3,4,16,2048]{4,3,2,1,0:T(8,128)(2,1)S(1)}, bf16[2,3,4,16,2048]{4,3,2,1,0:T(8,128)(2,1)S(1)}, u32[]{:S(2)}, u32[]{:S(2)}) %collective-permute-start.2) | collective-permute-done | bytes 1572896 | tf_op jit(solution)/shard_map/ppermute | solution.py:39
  28.2 1.5 collective-permute-start.7
  29.6 10.9 %collective-permute-done.1.refs_3_ = bf16[2,3,4,16,2048]{4,3,2,1,0:T(8,128)(2,1)S(1)} collective-permute-done((bf16[2,3,4,16,2048]{4,3,2,1,0:T(8,128)(2,1)S(1)}, bf16[2,3,4,16,2048]{4,3,2,1,0:T(8,128)(2,1)S(1)}, u32[]{:S(2)}, u32[]{:S(2)}) %collective-permute-start.1) | collective-permute-done | bytes 1572896 | tf_op jit(solution)/shard_map/ppermute | solution.py:39
  40.6 3.4 %collective-permute-done.refs_2_ = bf16[2,3,4,16,2048]{4,3,2,1,0:T(8,128)(2,1)S(1)} collective-permute-done((bf16[2,3,4,16,2048]{4,3,2,1,0:T(8,128)(2,1)S(1)}, bf16[2,3,4,16,2048]{4,3,2,1,0:T(8,128)(2,1)S(1)}, u32[]{:S(2)}, u32[]{:S(2)}) %collective-permute-start) | collective-permute-done | bytes 1572896 | tf_op jit(solution)/shard_map/ppermute | solution.py:39
  45.0 1.5 collective-permute-start.5
  46.5 2.5 %collective-permute-done.6.refs_4_ = bf16[3,4,16,2048]{3,2,1,0:T(8,128)(2,1)S(1)} collective-permute-done((bf16[3,4,16,2048]{3,2,1,0:T(8,128)(2,1)S(1)}, bf16[3,4,16,2048]{3,2,1,0:T(8,128)(2,1)S(1)}, u32[]{:S(2)}, u32[]{:S(2)}) %collective-permute-start.6) | collective-permute-done | bytes 786464 | tf_op jit(solution)/shard_map/ppermute | solution.py:39
  49.0 3.4 %collective-permute-done.7.refs_5_ = bf16[3,4,16,2048]{3,2,1,0:T(8,128)(2,1)S(1)} collective-permute-done((bf16[3,4,16,2048]{3,2,1,0:T(8,128)(2,1)S(1)}, bf16[3,4,16,2048]{3,2,1,0:T(8,128)(2,1)S(1)}, u32[]{:S(2)}, u32[]{:S(2)}) %collective-permute-start.7) | collective-permute-done | bytes 786464 | tf_op jit(solution)/shard_map/ppermute | solution.py:39
  52.4 1.6 %shard_map.61 = (bf16[3,16,4096]{2,1,0:T(8,128)(2,1)S(1)}, bf16[3,16,4096]{2,1,0:T(8,128)(2,1)S(1)}, bf16[3,16,4096]{2,1,0:T(8,128)(2,1)S(1)}, bf16[3,16,4096]{2,1,0:T(8,128)(2,1)S(1)}) custom-call(s32[3]{0:T(128)S(1)} %pad_add_fusion.2.ids, bf16[2,3,4,16,2048]{4,3,2,1,0:T(8,128)(2,1)S(1)} %get-tuple-element.29.refs_1_.refs_0_, ...), custom_call_target="tpu_custom_call" | custom-call | flops 1 | bytes 4 | tf_op jit(solution)/shard_map/pallas_call | solution.py:71
  54.0 2.5 %collective-permute-start.11 = (bf16[3,16,4096]{2,1,0:T(8,128)(2,1)S(1)}, bf16[3,16,4096]{2,1,0:T(8,128)(2,1)S(1)}, u32[]{:S(2)}, u32[]{:S(2)}) collective-permute-start(bf16[3,16,4096]{2,1,0:T(8,128)(2,1)S(1)} %get-tuple-element.44), channel_id=1, source_target_pairs={{0,24},{1,97},{2,26},{3,99},{4,28},{5,101},{6,30},{7,103},{8,0},{9... | collective-permute-start | bytes 1179656 | tf_op jit(solution)/shard_map/ppermute | solution.py:39
  56.6 1.4 collective-permute-start.13
  58.0 2.8 %collective-permute-done.5.refs_5_ = bf16[3,4,16,2048]{3,2,1,0:T(8,128)(2,1)S(1)} collective-permute-done((bf16[3,4,16,2048]{3,2,1,0:T(8,128)(2,1)S(1)}, bf16[3,4,16,2048]{3,2,1,0:T(8,128)(2,1)S(1)}, u32[]{:S(2)}, u32[]{:S(2)}) %collective-permute-start.5) | collective-permute-done | bytes 786464 | tf_op jit(solution)/shard_map/ppermute | solution.py:39
  60.8 1.6 %shard_map.62 = (bf16[3,16,4096]{2,1,0:T(8,128)(2,1)S(1)}, bf16[3,16,4096]{2,1,0:T(8,128)(2,1)S(1)}, bf16[3,16,4096]{2,1,0:T(8,128)(2,1)S(1)}, bf16[3,16,4096]{2,1,0:T(8,128)(2,1)S(1)}) custom-call(s32[3]{0:T(128)S(1)} %pad_add_fusion.2.ids, bf16[2,3,4,16,2048]{4,3,2,1,0:T(8,128)(2,1)S(1)} %get-tuple-element.30.refs_4_.refs_0_, ...), custom_call_target="tpu_custom_call" | custom-call | flops 1 | bytes 4 | tf_op jit(solution)/shard_map/pallas_call | solution.py:71
  62.5 3.0 %collective-permute-start.8 = (bf16[3,16,4096]{2,1,0:T(8,128)(2,1)S(1)}, bf16[3,16,4096]{2,1,0:T(8,128)(2,1)S(1)}, u32[]{:S(2)}, u32[]{:S(2)}) collective-permute-start(bf16[3,16,4096]{2,1,0:T(8,128)(2,1)S(1)} %get-tuple-element.41), channel_id=1, source_target_pairs={{0,24},{1,97},{2,26},{3,99},{4,28},{5,101},{6,30},{7,103},{8,0},{9... | collective-permute-start | bytes 1179656 | tf_op jit(solution)/shard_map/ppermute | solution.py:39
  67.9 2.5 %collective-permute-done.12.refs_2_ = bf16[3,16,4096]{2,1,0:T(8,128)(2,1)S(1)} collective-permute-done((bf16[3,16,4096]{2,1,0:T(8,128)(2,1)S(1)}, bf16[3,16,4096]{2,1,0:T(8,128)(2,1)S(1)}, u32[]{:S(2)}, u32[]{:S(2)}) %collective-permute-start.12) | collective-permute-done | bytes 393248 | tf_op jit(solution)/shard_map/ppermute | solution.py:39
  71.7 1.7 %collective-permute-start.19 = (bf16[96,16,128]{2,1,0:T(8,128)(2,1)S(1)}, bf16[96,16,128]{2,1,0:T(8,128)(2,1)S(1)}, u32[]{:S(2)}, u32[]{:S(2)}) collective-permute-start(bf16[96,16,128]{2,1,0:T(8,128)(2,1)S(1)} %get-tuple-element.48.refs_6_.refs_0_), channel_id=1, source_target_pairs={{0,2},{1,3},{2,4},{3,5},{4,6},{5,7},{6,0},{7,1},{8,10},{9,11},{10,... | collective-permute-start | bytes 1179656 | tf_op jit(solution)/shard_map/ppermute | solution.py:39
  73.4 3.3 %collective-permute-start.18 = (bf16[96,16,128]{2,1,0:T(8,128)(2,1)S(1)}, bf16[96,16,128]{2,1,0:T(8,128)(2,1)S(1)}, u32[]{:S(2)}, u32[]{:S(2)}) collective-permute-start(bf16[96,16,128]{2,1,0:T(8,128)(2,1)S(1)} %get-tuple-element.48.refs_6_.refs_0_), channel_id=1, source_target_pairs={{0,4},{1,5},{2,6},{3,7},{4,0},{5,1},{6,2},{7,3},{8,12},{9,13},{10,... | collective-permute-start | bytes 1179656 | tf_op jit(solution)/shard_map/ppermute | solution.py:39
  79.8 1.7 %collective-permute-start.16 = (bf16[97,16,128]{2,1,0:T(8,128)(2,1)S(1)}, bf16[97,16,128]{2,1,0:T(8,128)(2,1)S(1)}, u32[]{:S(2)}, u32[]{:S(2)}) collective-permute-start(bf16[97,16,128]{2,1,0:T(8,128)(2,1)S(1)} %shard_map.64.refs_4_.refs_0_), channel_id=1, source_target_pairs={{0,2},{1,3},{2,4},{3,5},{4,6},{5,7},{6,0},{7,1},{8,10},{9,11},{10,... | collective-permute-start | bytes 1191944 | tf_op jit(solution)/shard_map/ppermute | solution.py:39
  81.5 3.3 %collective-permute-start.15 = (bf16[97,16,128]{2,1,0:T(8,128)(2,1)S(1)}, bf16[97,16,128]{2,1,0:T(8,128)(2,1)S(1)}, u32[]{:S(2)}, u32[]{:S(2)}) collective-permute-start(bf16[97,16,128]{2,1,0:T(8,128)(2,1)S(1)} %shard_map.64.refs_4_.refs_0_), channel_id=1, source_target_pairs={{0,4},{1,5},{2,6},{3,7},{4,0},{5,1},{6,2},{7,3},{8,12},{9,13},{10,... | collective-permute-start | bytes 1191944 | tf_op jit(solution)/shard_map/ppermute | solution.py:39
  86.3 2.3 %shard_map.65.refs_4_ = bf16[32,17,16,128]{3,2,1,0:T(8,128)(2,1)} custom-call(s32[64]{0:T(128)S(1)} %reshape.234.ids, bf16[96,16,128]{2,1,0:T(8,128)(2,1)S(1)} %get-tuple-element.48.refs_6_.refs_0_, bf16[96,16,128]{2,1,0:T(8,128)(2,1)S(1)} %collective-permute-done.17.refs_1_, bf16[96,16,128]{2,1,0:T(8,128)(2,1)S(1)} %collective-permute-done.18.refs_2_, ...), custom_call_target="tpu_custom_call" | custom-call | flops 1 | bytes 4 | tf_op jit(solution)/shard_map/pallas_call | solution.py:71
  88.6 6.5 %collective-permute-done.16.refs_3_ = bf16[97,16,128]{2,1,0:T(8,128)(2,1)S(1)} collective-permute-done((bf16[97,16,128]{2,1,0:T(8,128)(2,1)S(1)}, bf16[97,16,128]{2,1,0:T(8,128)(2,1)S(1)}, u32[]{:S(2)}, u32[]{:S(2)}) %collective-permute-start.16) | collective-permute-done | bytes 397344 | tf_op jit(solution)/shard_map/ppermute | solution.py:39
  95.1 7.8 %collective-permute-done.15.refs_2_ = bf16[97,16,128]{2,1,0:T(8,128)(2,1)S(1)} collective-permute-done((bf16[97,16,128]{2,1,0:T(8,128)(2,1)S(1)}, bf16[97,16,128]{2,1,0:T(8,128)(2,1)S(1)}, u32[]{:S(2)}, u32[]{:S(2)}) %collective-permute-start.15) | collective-permute-done | bytes 397344 | tf_op jit(solution)/shard_map/ppermute | solution.py:39
  103.0 2.3 %shard_map.66 = bf16[32,17,16,128]{3,2,1,0:T(8,128)(2,1)} custom-call(s32[64]{0:T(128)S(1)} %reshape.234.ids, bf16[97,16,128]{2,1,0:T(8,128)(2,1)S(1)} %shard_map.64.refs_4_.refs_0_, bf16[97,16,128]{2,1,0:T(8,128)(2,1)S(1)} %collective-permute-done.14.refs_1_, ...), custom_call_target="tpu_custom_call", output_to_operand_aliasing={{}: (5, {})} | custom-call | flops 1 | bytes 4 | tf_op jit(solution)/shard_map/pallas_call | solution.py:71
  105.3 13.9 %all-to-all-start = ((bf16[32,17,16,128]{3,2,1,0:T(8,128)(2,1)}), bf16[32,17,16,128]{3,2,1,0:T(8,128)(2,1)S(1)}, u32[]{:S(2)}, u32[]{:S(2)}) async-start(bf16[32,17,16,128]{3,2,1,0:T(8,128)(2,1)} %shard_map.66), calls=%async_computation | async-start | bytes 4456448 | tf_op jit(solution)/shard_map/all_to_all | solution.py:379
  123.8 25.1 %all-to-all-done = bf16[32,17,16,128]{3,2,1,0:T(8,128)(2,1)S(1)} async-done(((bf16[32,17,16,128]{3,2,1,0:T(8,128)(2,1)}), bf16[32,17,16,128]{3,2,1,0:T(8,128)(2,1)S(1)}, u32[]{:S(2)}, u32[]{:S(2)}) %all-to-all-start) | async-done | bytes 2228256 | tf_op jit(solution)/shard_map/all_to_all | solution.py:379
  148.8 8.2 %shard_map.67 = bf16[1,1024,1024]{2,1,0:T(8,128)(2,1)} custom-call(s32[2]{0:T(128)S(1)} %pad_add_fusion.1.ids, bf16[16,2,17,16,128]{4,3,2,1,0:T(8,128)(2,1)S(1)} %bitcast.8, bf16[1,1024,1024]{2,1,0:T(8,128)(2,1)} %refs_1_.1, bf16[1,1024,1024]{2,1,0:T(8,128)(2,1)} %refs_2_.1), custom_call_target="tpu_custom_call" | custom-call | flops 1048576 | bytes 4194304 | tf_op jit(solution)/shard_map/pallas_call | solution.py:71
  (39 shorter events, 12.4 us)
Async XLA Ops:
  2.7 21.0 %collective-permute-start.3 = (bf16[2,3,4,16,2048]{4,3,2,1,0:T(8,128)(2,1)S(1)}, bf16[2,3,4,16,2048]{4,3,2,1,0:T(8,128)(2,1)S(1)}, u32[]{:S(2)}, u32[]{:S(2)}) collective-permute-start(bf16[2,3,4,16,2048]{4,3,2,1,0:T(8,128)(2,1)S(1)} %get-tuple-element.34), channel_id=1, source_target_pairs={{0,96},{1,25},{2,98},{3,27},{4,100},{5,29},{6,102},{7,31},{8,104},... | collective-permute-start | bytes 4718600 | tf_op jit(solution)/shard_map/ppermute | solution.py:39
  6.4 20.8 %collective-permute-start.2 = (bf16[2,3,4,16,2048]{4,3,2,1,0:T(8,128)(2,1)S(1)}, bf16[2,3,4,16,2048]{4,3,2,1,0:T(8,128)(2,1)S(1)}, u32[]{:S(2)}, u32[]{:S(2)}) collective-permute-start(bf16[2,3,4,16,2048]{4,3,2,1,0:T(8,128)(2,1)S(1)} %get-tuple-element.27.refs_1_), channel_id=1, source_target_pairs={{0,32},{1,9},{2,34},{3,11},{4,36},{5,13},{6,38},{7,15},{8,40},{9,1... | collective-permute-start | bytes 4718600 | tf_op jit(solution)/shard_map/ppermute | solution.py:39
  9.0 31.6 %collective-permute-start.1 = (bf16[2,3,4,16,2048]{4,3,2,1,0:T(8,128)(2,1)S(1)}, bf16[2,3,4,16,2048]{4,3,2,1,0:T(8,128)(2,1)S(1)}, u32[]{:S(2)}, u32[]{:S(2)}) collective-permute-start(bf16[2,3,4,16,2048]{4,3,2,1,0:T(8,128)(2,1)S(1)} %get-tuple-element.32), channel_id=1, source_target_pairs={{0,96},{1,25},{2,98},{3,27},{4,100},{5,29},{6,102},{7,31},{8,104},... | collective-permute-start | bytes 4718600 | tf_op jit(solution)/shard_map/ppermute | solution.py:39
  11.8 32.2 %collective-permute-start = (bf16[2,3,4,16,2048]{4,3,2,1,0:T(8,128)(2,1)S(1)}, bf16[2,3,4,16,2048]{4,3,2,1,0:T(8,128)(2,1)S(1)}, u32[]{:S(2)}, u32[]{:S(2)}) collective-permute-start(bf16[2,3,4,16,2048]{4,3,2,1,0:T(8,128)(2,1)S(1)} %get-tuple-element.28.refs_1_), channel_id=1, source_target_pairs={{0,32},{1,9},{2,34},{3,11},{4,36},{5,13},{6,38},{7,15},{8,40},{9,1... | collective-permute-start | bytes 4718600 | tf_op jit(solution)/shard_map/ppermute | solution.py:39
  28.1 20.9 %collective-permute-start.6 = (bf16[3,4,16,2048]{3,2,1,0:T(8,128)(2,1)S(1)}, bf16[3,4,16,2048]{3,2,1,0:T(8,128)(2,1)S(1)}, u32[]{:S(2)}, u32[]{:S(2)}) collective-permute-start(bf16[3,4,16,2048]{3,2,1,0:T(8,128)(2,1)S(1)} %get-tuple-element.38), channel_id=1, source_target_pairs={{0,96},{1,25},{2,98},{3,27},{4,100},{5,29},{6,102},{7,31},{8,104},... | collective-permute-start | bytes 2359304 | tf_op jit(solution)/shard_map/ppermute | solution.py:39
  28.2 24.2 %collective-permute-start.7 = (bf16[3,4,16,2048]{3,2,1,0:T(8,128)(2,1)S(1)}, bf16[3,4,16,2048]{3,2,1,0:T(8,128)(2,1)S(1)}, u32[]{:S(2)}, u32[]{:S(2)}) collective-permute-start(bf16[3,4,16,2048]{3,2,1,0:T(8,128)(2,1)S(1)} %get-tuple-element.35.refs_4_), channel_id=1, source_target_pairs={{0,32},{1,9},{2,34},{3,11},{4,36},{5,13},{6,38},{7,15},{8,40},{9,1... | collective-permute-start | bytes 2359304 | tf_op jit(solution)/shard_map/ppermute | solution.py:39
  45.0 13.1 %collective-permute-start.4 = (bf16[3,4,16,2048]{3,2,1,0:T(8,128)(2,1)S(1)}, bf16[3,4,16,2048]{3,2,1,0:T(8,128)(2,1)S(1)}, u32[]{:S(2)}, u32[]{:S(2)}) collective-permute-start(bf16[3,4,16,2048]{3,2,1,0:T(8,128)(2,1)S(1)} %get-tuple-element.36), channel_id=1, source_target_pairs={{0,96},{1,25},{2,98},{3,27},{4,100},{5,29},{6,102},{7,31},{8,104},... | collective-permute-start | bytes 2359304 | tf_op jit(solution)/shard_map/ppermute | solution.py:39
  45.0 15.8 %collective-permute-start.5 = (bf16[3,4,16,2048]{3,2,1,0:T(8,128)(2,1)S(1)}, bf16[3,4,16,2048]{3,2,1,0:T(8,128)(2,1)S(1)}, u32[]{:S(2)}, u32[]{:S(2)}) collective-permute-start(bf16[3,4,16,2048]{3,2,1,0:T(8,128)(2,1)S(1)} %get-tuple-element.37.refs_6_), channel_id=1, source_target_pairs={{0,32},{1,9},{2,34},{3,11},{4,36},{5,13},{6,38},{7,15},{8,40},{9,1... | collective-permute-start | bytes 2359304 | tf_op jit(solution)/shard_map/ppermute | solution.py:39
  54.0 12.7 %collective-permute-start.11 = (bf16[3,16,4096]{2,1,0:T(8,128)(2,1)S(1)}, bf16[3,16,4096]{2,1,0:T(8,128)(2,1)S(1)}, u32[]{:S(2)}, u32[]{:S(2)}) collective-permute-start(bf16[3,16,4096]{2,1,0:T(8,128)(2,1)S(1)} %get-tuple-element.44), channel_id=1, source_target_pairs={{0,24},{1,97},{2,26},{3,99},{4,28},{5,101},{6,30},{7,103},{8,0},{9... | collective-permute-start | bytes 1179656 | tf_op jit(solution)/shard_map/ppermute | solution.py:39
  56.6 13.8 %collective-permute-start.12 = (bf16[3,16,4096]{2,1,0:T(8,128)(2,1)S(1)}, bf16[3,16,4096]{2,1,0:T(8,128)(2,1)S(1)}, u32[]{:S(2)}, u32[]{:S(2)}) collective-permute-start(bf16[3,16,4096]{2,1,0:T(8,128)(2,1)S(1)} %get-tuple-element.45), channel_id=1, source_target_pairs={{0,8},{1,33},{2,10},{3,35},{4,12},{5,37},{6,14},{7,39},{8,16},{9,4... | collective-permute-start | bytes 1179656 | tf_op jit(solution)/shard_map/ppermute | solution.py:39
  56.6 13.8 %collective-permute-start.13 = (bf16[3,16,4096]{2,1,0:T(8,128)(2,1)S(1)}, bf16[3,16,4096]{2,1,0:T(8,128)(2,1)S(1)}, u32[]{:S(2)}, u32[]{:S(2)}) collective-permute-start(bf16[3,16,4096]{2,1,0:T(8,128)(2,1)S(1)} %get-tuple-element.46), channel_id=1, source_target_pairs={{0,16},{1,65},{2,18},{3,67},{4,20},{5,69},{6,22},{7,71},{8,24},{9,... | collective-permute-start | bytes 1179656 | tf_op jit(solution)/shard_map/ppermute | solution.py:39
  60.8 9.6 %copy-start = (f32[3,32,4096]{2,1,0:T(8,128)S(1)}, f32[3,32,4096]{2,1,0:T(8,128)}, u32[]{:S(2)}) copy-start(f32[3,32,4096]{2,1,0:T(8,128)} %param.6) | copy-start | bytes 4718596
  62.5 14.2 %collective-permute-start.8 = (bf16[3,16,4096]{2,1,0:T(8,128)(2,1)S(1)}, bf16[3,16,4096]{2,1,0:T(8,128)(2,1)S(1)}, u32[]{:S(2)}, u32[]{:S(2)}) collective-permute-start(bf16[3,16,4096]{2,1,0:T(8,128)(2,1)S(1)} %get-tuple-element.41), channel_id=1, source_target_pairs={{0,24},{1,97},{2,26},{3,99},{4,28},{5,101},{6,30},{7,103},{8,0},{9... | collective-permute-start | bytes 1179656 | tf_op jit(solution)/shard_map/ppermute | solution.py:39
  65.5 13.1 %collective-permute-start.9 = (bf16[3,16,4096]{2,1,0:T(8,128)(2,1)S(1)}, bf16[3,16,4096]{2,1,0:T(8,128)(2,1)S(1)}, u32[]{:S(2)}, u32[]{:S(2)}) collective-permute-start(bf16[3,16,4096]{2,1,0:T(8,128)(2,1)S(1)} %get-tuple-element.42), channel_id=1, source_target_pairs={{0,8},{1,33},{2,10},{3,35},{4,12},{5,37},{6,14},{7,39},{8,16},{9,4... | collective-permute-start | bytes 1179656 | tf_op jit(solution)/shard_map/ppermute | solution.py:39
  66.7 11.8 %collective-permute-start.10 = (bf16[3,16,4096]{2,1,0:T(8,128)(2,1)S(1)}, bf16[3,16,4096]{2,1,0:T(8,128)(2,1)S(1)}, u32[]{:S(2)}, u32[]{:S(2)}) collective-permute-start(bf16[3,16,4096]{2,1,0:T(8,128)(2,1)S(1)} %get-tuple-element.43), channel_id=1, source_target_pairs={{0,16},{1,65},{2,18},{3,67},{4,20},{5,69},{6,22},{7,71},{8,24},{9,... | collective-permute-start | bytes 1179656 | tf_op jit(solution)/shard_map/ppermute | solution.py:39
  71.7 13.2 %collective-permute-start.19 = (bf16[96,16,128]{2,1,0:T(8,128)(2,1)S(1)}, bf16[96,16,128]{2,1,0:T(8,128)(2,1)S(1)}, u32[]{:S(2)}, u32[]{:S(2)}) collective-permute-start(bf16[96,16,128]{2,1,0:T(8,128)(2,1)S(1)} %get-tuple-element.48.refs_6_.refs_0_), channel_id=1, source_target_pairs={{0,2},{1,3},{2,4},{3,5},{4,6},{5,7},{6,0},{7,1},{8,10},{9,11},{10,... | collective-permute-start | bytes 1179656 | tf_op jit(solution)/shard_map/ppermute | solution.py:39
  73.4 13.0 %collective-permute-start.18 = (bf16[96,16,128]{2,1,0:T(8,128)(2,1)S(1)}, bf16[96,16,128]{2,1,0:T(8,128)(2,1)S(1)}, u32[]{:S(2)}, u32[]{:S(2)}) collective-permute-start(bf16[96,16,128]{2,1,0:T(8,128)(2,1)S(1)} %get-tuple-element.48.refs_6_.refs_0_), channel_id=1, source_target_pairs={{0,4},{1,5},{2,6},{3,7},{4,0},{5,1},{6,2},{7,3},{8,12},{9,13},{10,... | collective-permute-start | bytes 1179656 | tf_op jit(solution)/shard_map/ppermute | solution.py:39
  76.7 9.7 %collective-permute-start.17 = (bf16[96,16,128]{2,1,0:T(8,128)(2,1)S(1)}, bf16[96,16,128]{2,1,0:T(8,128)(2,1)S(1)}, u32[]{:S(2)}, u32[]{:S(2)}) collective-permute-start(bf16[96,16,128]{2,1,0:T(8,128)(2,1)S(1)} %get-tuple-element.48.refs_6_.refs_0_), channel_id=1, source_target_pairs={{0,6},{1,7},{2,0},{3,1},{4,2},{5,3},{6,4},{7,5},{8,14},{9,15},{10,... | collective-permute-start | bytes 1179656 | tf_op jit(solution)/shard_map/ppermute | solution.py:39
  78.6 7.0 %copy-start.1 = (s32[48]{0:T(128)S(1)}, s32[48]{0:T(128)}, u32[]{:S(2)}) copy-start(s32[48]{0:T(128)} %param.9) | copy-start | bytes 580
  79.8 15.3 %collective-permute-start.16 = (bf16[97,16,128]{2,1,0:T(8,128)(2,1)S(1)}, bf16[97,16,128]{2,1,0:T(8,128)(2,1)S(1)}, u32[]{:S(2)}, u32[]{:S(2)}) collective-permute-start(bf16[97,16,128]{2,1,0:T(8,128)(2,1)S(1)} %shard_map.64.refs_4_.refs_0_), channel_id=1, source_target_pairs={{0,2},{1,3},{2,4},{3,5},{4,6},{5,7},{6,0},{7,1},{8,10},{9,11},{10,... | collective-permute-start | bytes 1191944 | tf_op jit(solution)/shard_map/ppermute | solution.py:39
  81.5 21.4 %collective-permute-start.15 = (bf16[97,16,128]{2,1,0:T(8,128)(2,1)S(1)}, bf16[97,16,128]{2,1,0:T(8,128)(2,1)S(1)}, u32[]{:S(2)}, u32[]{:S(2)}) collective-permute-start(bf16[97,16,128]{2,1,0:T(8,128)(2,1)S(1)} %shard_map.64.refs_4_.refs_0_), channel_id=1, source_target_pairs={{0,4},{1,5},{2,6},{3,7},{4,0},{5,1},{6,2},{7,3},{8,12},{9,13},{10,... | collective-permute-start | bytes 1191944 | tf_op jit(solution)/shard_map/ppermute | solution.py:39
  84.9 18.1 %collective-permute-start.14 = (bf16[97,16,128]{2,1,0:T(8,128)(2,1)S(1)}, bf16[97,16,128]{2,1,0:T(8,128)(2,1)S(1)}, u32[]{:S(2)}, u32[]{:S(2)}) collective-permute-start(bf16[97,16,128]{2,1,0:T(8,128)(2,1)S(1)} %shard_map.64.refs_4_.refs_0_), channel_id=1, source_target_pairs={{0,6},{1,7},{2,0},{3,1},{4,2},{5,3},{6,4},{7,5},{8,14},{9,15},{10,... | collective-permute-start | bytes 1191944 | tf_op jit(solution)/shard_map/ppermute | solution.py:39
  105.3 43.6 %all-to-all-start = ((bf16[32,17,16,128]{3,2,1,0:T(8,128)(2,1)}), bf16[32,17,16,128]{3,2,1,0:T(8,128)(2,1)S(1)}, u32[]{:S(2)}, u32[]{:S(2)}) async-start(bf16[32,17,16,128]{3,2,1,0:T(8,128)(2,1)} %shard_map.66), calls=%async_computation | async-start | bytes 4456448 | tf_op jit(solution)/shard_map/all_to_all | solution.py:379
